TPU v7x, 32 devices: a whole 2x2x4 slice. The times are simulated.
32 devices in a mesh: replica: 2 (over y), tensor: 4 (over z), dp: 4 (over x, core).
Axes of the slice: x: 2, y: 2, z: 4, core: 2. Of those that a mesh axis runs over, the one named last changes fastest.
Arguments:
- residual: bfloat16 [2, 128, 8192], P(None, 'replica', 'dp'), parts along dimension 1
- queries: bfloat16 [2, 128, 8192], P(None, ('replica', 'dp'), 'tensor'), parts along dimension 1, may hold values from -6 to 6
- new_keys: bfloat16 [2, 128, 8, 128], P(None, ('replica', 'dp'), 'tensor'), parts along dimension 1, as said below
- new_values: bfloat16 [2, 128, 8, 128], P(None, ('replica', 'dp'), 'tensor'), parts along dimension 1, as said below
- key_cache: bfloat16 [128, 8, 1024, 128], P(('replica', 'dp'), 'tensor'), parts along dimension 0, as said below
- value_cache: bfloat16 [128, 8, 1024, 128], P(('replica', 'dp'), 'tensor'), parts along dimension 0, as said below
- lengths: int32 [128], P(('replica', 'dp')), parts along dimension 0, may hold values from 1 to 1022, as said below
- out_weight: bfloat16 [8192, 8192], P('tensor', 'dp'), may hold values from -0.5 to 0.5
- norm_gain: bfloat16 [8192], P('dp'), may hold values from 0.099609375 to 1.8984375
- gate_weight: bfloat16 [8192, 14336], P('dp', 'tensor'), may hold values from -0.0625 to 0.0625
- up_weight: bfloat16 [8192, 14336], P('dp', 'tensor'), may hold values from -0.0625 to 0.0625
- down_weight: bfloat16 [14336, 8192], P('tensor', 'dp'), may hold values from -0.125 to 0.125
Outputs:
- output: bfloat16 [2, 128, 8192], P(None, 'replica', 'dp'), parts along dimension 1
There are 2 independent parts, one for each index of `replica`. A program takes and returns all parts, laid end to end along the dimension named above; an argument that names none is the same for every part. Nothing has to cross between parts.
Inputs may be any that keep to these rules, and one draw needn't show every extreme that they name: `lengths`: cached tokens of each sequence before the first step; some sequence has exactly 1022 in every draw. `key_cache`: head copies c and c2 with c // 1 == c2 // 1 hold equal entries. `value_cache`: head copies c and c2 with c // 1 == c2 // 1 hold equal entries. `new_keys`: head copies c and c2 with c // 1 == c2 // 1 hold equal entries. `new_values`: head copies c and c2 with c // 1 == c2 // 1 hold equal entries.
All inputs are finite; a program needn't handle non-finite values.
Results may differ from a plain program's by a relative error of at most 0.018.
Values may be sent and summed in bfloat16 or wider, within the bound.
No kernel may reach another device: no remote copies, remote signals or barrier semaphores. Data moves between devices by JAX's collectives and lax.ppermute only.
A program may use at most 192 MiB of HBM per device.

v0:
```python
import jax
import jax.numpy as jnp
from jax import lax
from jax.sharding import PartitionSpec as P


def body(
    residual,
    queries,
    new_keys,
    new_values,
    key_cache,
    value_cache,
    lengths,
    out_weight,
    norm_gain,
    gate_weight,
    up_weight,
    down_weight,
):
    steps_count, all_seqs, width_local = residual.shape
    local_seqs = queries.shape[1]
    local_copies = key_cache.shape[1]
    ctx_slots = key_cache.shape[2]
    head_size = key_cache.shape[3]
    local_heads = queries.shape[2] // head_size
    group_size = local_heads // local_copies
    scaling = head_size ** (-0.5)
    grouped = queries.reshape(steps_count, local_seqs, local_copies, group_size, head_size)
    cached = (
        jnp.einsum("sbgjd,bgtd->sbgjt", grouped, key_cache, preferred_element_type=jnp.float32)
        * scaling
    )
    alive_mask = jnp.arange(ctx_slots)[None, :] < lengths[:, None]
    cached = jnp.where(alive_mask[None, :, None, None, :], cached, -jnp.inf)
    recent = (
        jnp.einsum("sbgjd,rbgd->sbgjr", grouped, new_keys, preferred_element_type=jnp.float32)
        * scaling
    )
    causal = jnp.arange(steps_count)[None, :] <= jnp.arange(steps_count)[:, None]
    recent = jnp.where(causal[:, None, None, None, :], recent, -jnp.inf)
    row_max = jnp.maximum(jnp.max(cached, axis=-1), jnp.max(recent, axis=-1))
    w_cached = jnp.exp(cached - row_max[..., None])
    w_recent = jnp.exp(recent - row_max[..., None])
    totals = jnp.sum(w_cached, axis=-1) + jnp.sum(w_recent, axis=-1)
    blended = jnp.einsum(
        "sbgjt,bgtd->sbgjd",
        w_cached.astype(jnp.bfloat16),
        value_cache,
        preferred_element_type=jnp.float32,
    )
    blended = blended + jnp.einsum(
        "sbgjr,rbgd->sbgjd",
        w_recent.astype(jnp.bfloat16),
        new_values,
        preferred_element_type=jnp.float32,
    )
    heads_out = (
        (blended / totals[..., None])
        .astype(jnp.bfloat16)
        .reshape(steps_count, local_seqs, local_heads * head_size)
    )
    piece = lax.all_gather(heads_out, "dp", axis=1, tiled=True)
    flat_piece = piece.reshape(piece.shape[0] * piece.shape[1], piece.shape[2])
    product = jnp.dot(flat_piece, out_weight, preferred_element_type=jnp.float32)
    partials = product.reshape(piece.shape[0], piece.shape[1], out_weight.shape[1])
    attn = lax.psum(partials.astype(jnp.bfloat16), "tensor")
    mid = (residual.astype(jnp.float32) + attn.astype(jnp.float32)).astype(jnp.bfloat16)
    mid_wide = mid.astype(jnp.float32)
    row_count = steps_count * all_seqs
    squares = lax.psum(jnp.sum(mid_wide * mid_wide, axis=2), "dp")
    full_width = width_local * lax.axis_size("dp")
    inv_norm = lax.rsqrt(squares / full_width + 1e-05).reshape(1, row_count)
    normed = (
        (mid_wide * norm_gain.astype(jnp.float32)[None, None, :])
        .astype(jnp.bfloat16)
        .reshape(row_count, width_local)
    )
    contract_first = (((0,), (1,)), ((), ()))
    gate_term = lax.dot_general(
        gate_weight, normed, contract_first, preferred_element_type=jnp.float32
    )
    up_term = lax.dot_general(up_weight, normed, contract_first, preferred_element_type=jnp.float32)
    both_terms = lax.psum_scatter(
        jnp.concatenate((gate_term, up_term), axis=1).astype(jnp.bfloat16),
        "dp",
        scatter_dimension=0,
        tiled=True,
    ).astype(jnp.float32)
    gate = both_terms[:, :row_count] * inv_norm
    up_proj = both_terms[:, row_count:] * inv_norm
    hidden = (jax.nn.silu(gate) * up_proj).astype(jnp.bfloat16)
    down_term = lax.dot_general(
        lax.all_gather(hidden, "dp", axis=0, tiled=True),
        down_weight,
        (((0,), (0,)), ((), ())),
        preferred_element_type=jnp.float32,
    )
    ffn = lax.psum(down_term.astype(jnp.bfloat16), "tensor").astype(jnp.float32)
    return (mid_wide + ffn.reshape(steps_count, all_seqs, width_local)).astype(jnp.bfloat16)


def solution(mesh):
    in_specs = (
        P(None, "replica", "dp"),
        P(None, ("replica", "dp"), "tensor"),
        P(None, ("replica", "dp"), "tensor", None),
        P(None, ("replica", "dp"), "tensor", None),
        P(("replica", "dp"), "tensor", None, None),
        P(("replica", "dp"), "tensor", None, None),
        P(("replica", "dp")),
        P("tensor", "dp"),
        P("dp"),
        P("dp", "tensor"),
        P("dp", "tensor"),
        P("tensor", "dp"),
    )
    out_specs = P(None, "replica", "dp")
    return jax.shard_map(body, mesh=mesh, in_specs=in_specs, out_specs=out_specs, check_vma=False)
```

profile of v0, /device:TPU:0, one launch (start us, length us, event | category | flops | bytes accessed | tf_op | source)
XLA Modules:
  0.0 186.5 jit_solution(6171208281686468155)
XLA Ops:
  6.5 0.0 copy-start
  6.5 0.0 all-reduce.3.cloned.1.call-start
  6.5 0.7 iota_compare_fusion
  7.3 0.9 copy.37
  8.2 1.4 fusion.39
  9.7 0.0 copy-start.2
  9.7 5.9 %bitcast_reduce_fusion = (f32[2,16,2,8]{3,0,2,1:T(2,128)S(1)}, f32[16,2,1024,2,8]{2,4,3,1,0:T(8,128)S(1)}) fusion(pred[16,1024]{1,0:T(8,128)(4,1)S(1)} %iota_compare_fusion, bf16[2,16,2,8,128]{4,3,2,1,0:T(8,128)(2,1)S(1)} %bitcast.64, bf16[16,2,1024,128]{3,2,1,0:T(8,128)(2,1)} %param.16), kind=kOutput, calls=%fused_computation.13 | convolution fusion | flops 135790080 | bytes 10635264 | tf_op jit(solution)/shard_map/sbgjd,bgtd->sbgjt/dot_general | solution.py:31
  15.6 0.1 fusion.31
  15.8 0.7 fusion.12
  16.4 0.0 copy-done.2
  16.4 1.4 fusion
  17.9 0.0 copy-done
  17.9 0.3 fusion.16
  18.2 0.1 reshape.62
  18.3 8.6 %all_gather.6 = bf16[2,64,2048]{2,1,0:T(8,128)(2,1)S(1)} all-gather(bf16[2,16,2048]{2,1,0:T(8,128)(2,1)S(1)} %reshape.62), channel_id=1, replica_groups=mesh['replica'=2,'tensor'=4,'dp'=4] {'dp'}, dimensions={1}, use_global_device_ids=true | all-gather | bytes 655360 | tf_op jit(solution)/shard_map/all_gather | solution.py:63
  26.9 0.0 copy-start.5
  26.9 0.0 copy-start.3
  26.9 5.5 %fusion.8 = bf16[2,64,2048]{2,1,0:T(8,128)(2,1)} fusion(bf16[2,64,2048]{2,1,0:T(8,128)(2,1)S(1)} %all_gather.6, bf16[2048,2048]{1,0:T(8,128)(2,1)} %param.19), kind=kOutput, calls=%fused_computation.10 | convolution fusion | flops 1074003968 | bytes 9437184 | tf_op jit(solution)/shard_map/dot_general | solution.py:65
  32.4 0.0 all-reduce.3.cloned.1.call-update
  32.4 0.0 reduce-scatter.4.cloned.1.call-start
  32.5 0.0 copy-done.5
  32.5 39.2 %all-reduce.3.cloned.1.call-done = bf16[2,64,2048]{2,1,0:T(8,128)(2,1)} async-done(((bf16[2,64,2048]{2,1,0:T(8,128)(2,1)}), bf16[2,64,2048]{2,1,0:T(8,128)(2,1)}) %all-reduce.3.cloned.1.call-update) | async-done | bytes 524304 | tf_op jit(solution)/shard_map/psum | solution.py:67
  71.8 0.0 copy-done.3
  71.8 1.3 fusion.20
  73.1 7.3 %fusion.7 = bf16[3584,128]{0,1:T(8,128)(2,1)S(1)} fusion(bf16[128,2048]{1,0:T(8,128)(2,1)S(1)} %bitcast.60, bf16[2048,3584]{1,0:T(8,128)(2,1)} %param.22), kind=kOutput, calls=%fused_computation.9 | convolution fusion | flops 1879506944 | bytes 16121856 | tf_op jit(solution)/shard_map/dot_general | solution.py:83
  80.3 7.3 %fusion.6 = bf16[3584,128]{0,1:T(8,128)(2,1)S(1)} fusion(bf16[128,2048]{1,0:T(8,128)(2,1)S(1)} %bitcast.61, bf16[2048,3584]{1,0:T(8,128)(2,1)} %param.21), kind=kOutput, calls=%fused_computation.8 | convolution fusion | flops 1879506944 | bytes 16121856 | tf_op jit(solution)/shard_map/dot_general | solution.py:80
  87.6 0.1 pad_maximum_fusion
  87.7 2.3 %copy.35 = bf16[3584,256]{1,0:T(8,128)(2,1)} copy(bf16[3584,256]{0,1:T(8,128)(2,1)S(1)} %pad_maximum_fusion) | data formatting | bytes 3670016
  90.0 0.0 reduce-scatter.4.cloned.1.call-update
  90.1 0.0 all-reduce.5.cloned.1.call-start
  90.1 5.9 %psum.22 = f32[2,64]{1,0:T(2,128)S(1)} all-reduce(f32[2,64]{1,0:T(2,128)S(1)} %get-tuple-element.5), channel_id=1, replica_groups=mesh['replica'=2,'tensor'=4,'dp'=4] {'dp'}, use_global_device_ids=true, to_apply=%region_7.8 | all-reduce | flops 128 | bytes 1024 | tf_op jit(solution)/shard_map/psum | solution.py:71
  96.0 0.1 mul.58
  96.1 23.9 %reduce-scatter.4.cloned.1.call-done = bf16[896,256]{1,0:T(8,128)(2,1)} async-done(((bf16[3584,256]{1,0:T(8,128)(2,1)}), bf16[896,256]{1,0:T(8,128)(2,1)}) %reduce-scatter.4.cloned.1.call-update) | async-done | bytes 458768
  120.0 1.3 copy.36
  121.3 0.1 convert_element_type.54
  121.4 0.2 fusion.28
  121.6 9.1 %all_gather.7 = bf16[3584,128]{0,1:T(8,128)(2,1)S(1)} all-gather(bf16[896,128]{0,1:T(8,128)(2,1)S(1)} %fusion.28), channel_id=1, replica_groups=mesh['replica'=2,'tensor'=4,'dp'=4] {'dp'}, dimensions={0}, use_global_device_ids=true | all-gather | bytes 1146880 | tf_op jit(solution)/shard_map/all_gather | solution.py:94
  130.7 0.0 copy-start.4
  130.7 0.0 copy-start.1
  130.7 8.4 %convolution_convert_fusion.2 = bf16[128,2048]{1,0:T(8,128)(2,1)} fusion(bf16[3584,128]{0,1:T(8,128)(2,1)S(1)} %all_gather.7, bf16[3584,2048]{1,0:T(8,128)(2,1)} %param.23), kind=kOutput, calls=%fused_computation.11 | convolution fusion | flops 1879310336 | bytes 16121856 | tf_op jit(solution)/shard_map/dot_general | solution.py:93
  139.1 0.0 all-reduce.5.cloned.1.call-update
  139.1 38.8 %all-reduce.5.cloned.1.call-done = bf16[2,64,2048]{2,1,0:T(8,128)(2,1)} async-done(((bf16[2,64,2048]{2,1,0:T(8,128)(2,1)}), bf16[2,64,2048]{2,1,0:T(8,128)(2,1)}) %all-reduce.5.cloned.1.call-update) | async-done | bytes 524304 | tf_op jit(solution)/shard_map/psum | solution.py:99
  177.9 0.0 copy-done.4
  177.9 2.1 %fusion.21 = bf16[2,64,2048]{2,1,0:T(8,128)(2,1)} fusion(bf16[2,64,2048]{2,1,0:T(8,128)(2,1)} %all-reduce.5.cloned.1.call-done, bf16[2,64,2048]{2,1,0:T(8,128)(2,1)S(1)} %copy-done.4, bf16[2,64,2048]{2,1,0:T(8,128)(2,1)S(1)} %copy-done.3), kind=kLoop, calls=%fused_computation.31 | loop fusion | flops 2097152 | bytes 2097152 | tf_op jit(solution)/shard_map/convert_element_type | solution.py:100
  180.0 0.0 copy-done.1
  (6 shorter events, 0.1 us)
Async XLA Ops:
  6.5 11.4 %copy-start = (bf16[2,16,2,128]{3,2,1,0:T(2,128)(2,1)S(1)}, bf16[2,16,2,128]{3,2,1,0:T(2,128)(2,1)}, u32[]{:S(2)}) copy-start(bf16[2,16,2,128]{3,2,1,0:T(2,128)(2,1)} %param.15) | copy-start | bytes 49156
  6.5 65.2 %all-reduce.3.cloned.1.call-start = ((), (), s32[]{:S(2)}) async-start(), calls=%async_computation.1 | async-start | bytes 1048576 | tf_op jit(solution)/shard_map/psum | solution.py:67
  9.7 6.8 %copy-start.2 = (bf16[16,2,1024,128]{3,2,1,0:T(8,128)(2,1)S(1)}, bf16[16,2,1024,128]{3,2,1,0:T(8,128)(2,1)}, u32[]{:S(2)}) copy-start(bf16[16,2,1024,128]{3,2,1,0:T(8,128)(2,1)} %param.17) | copy-start | bytes 25165828
  26.9 5.6 %copy-start.5 = (bf16[2048]{0:T(1024)(128)(2,1)S(1)}, bf16[2048]{0:T(1024)(128)(2,1)}, u32[]{:S(2)}) copy-start(bf16[2048]{0:T(1024)(128)(2,1)} %param.20) | copy-start | bytes 12292
  26.9 44.9 %copy-start.3 = (bf16[2,64,2048]{2,1,0:T(8,128)(2,1)S(1)}, bf16[2,64,2048]{2,1,0:T(8,128)(2,1)}, u32[]{:S(2)}) copy-start(bf16[2,64,2048]{2,1,0:T(8,128)(2,1)} %param.12) | copy-start | bytes 1572868
  32.4 87.6 %reduce-scatter.4.cloned.1.call-start = ((), (), s32[]{:S(2)}) async-start(), calls=%async_computation.3 | async-start | bytes 2293760
  90.1 87.8 %all-reduce.5.cloned.1.call-start = ((), (), s32[]{:S(2)}) async-start(), calls=%async_computation.2 | async-start | bytes 1048576 | tf_op jit(solution)/shard_map/psum | solution.py:99
  130.7 47.2 %copy-start.4 = (bf16[2,64,2048]{2,1,0:T(8,128)(2,1)S(1)}, bf16[2,64,2048]{2,1,0:T(8,128)(2,1)}, u32[]{:S(2)}) copy-start(bf16[2,64,2048]{2,1,0:T(8,128)(2,1)} %all-reduce.3.cloned.1.call-done) | copy-start | bytes 1572868
  130.7 49.3 %copy-start.1 = (bf16[2,16,2,128]{3,2,1,0:T(2,128)(2,1)S(1)}, bf16[2,16,2,128]{3,2,1,0:T(2,128)(2,1)}, u32[]{:S(2)}) copy-start(bf16[2,16,2,128]{3,2,1,0:T(2,128)(2,1)} %param.15) | copy-start | bytes 49156
Sparse Core Ops, SparseCore 0:
  32.6 39.1 all-reduce.2
  90.2 29.7 reduce-scatter.3
  139.2 38.6 all-reduce.4
where the time goes:
time: 187 us
  waiting for transfers between devices  102 us (55%)
  matrix products  37.5 us (20%)
  blocking collectives  23.6 us (13%)
  between operations  13.3 us (7%)
  other arithmetic  5.37 us (3%)
  local copies, waits for them, and re-layouts  4.68 us (3%)
    psum x1, waiting for transfers between devices, body(): attn = lax.psum(partials.astype(jnp.bfloat16), 'tensor')  39.2 us
    psum x1, waiting for transfers between devices, body(): ffn = lax.psum(down_term.astype(jnp.bfloat16), 'tensor').astype(jnp.float32)  38.8 us
    unnamed x4, waiting for transfers between devices  24 us
    all_gather x1, blocking collectives, body(): lax.all_gather(hidden, 'dp', axis=0, tiled=True)  9.1 us
    all_gather x1, blocking collectives, body(): piece = lax.all_gather(heads_out, 'dp', axis=1, tiled=True)  8.62 us
    dot_general x1, matrix products, body(): lax.dot_general(lax.all_gather(hidden, 'dp', axis=0, tiled=True), down_we...  8.38 us
    dot_general x1, matrix products, body(): lax.dot_general(up_weight, normed, contract_first, preferred_element_type...  7.27 us
    dot_general x1, matrix products, body(): lax.dot_general(gate_weight, normed, contract_first, preferred_element_ty...  7.27 us
  transfers between devices with their start and end apart: 3, of which 3 were waited for; matrix products, arithmetic and copies ran while one was open for 0% of the time, Pallas kernels for 0%

commit v1 on v0

--- a/solution.py
+++ b/solution.py
@@ -2,6 +2,66 @@
 import jax.numpy as jnp
 from jax import lax
 from jax.sharding import PartitionSpec as P
+
+BF16 = jnp.bfloat16
+F32 = jnp.float32
+
+
+def add(a, b):
+    return (a.astype(F32) + b.astype(F32)).astype(BF16)
+
+
+def pick(halves, index):
+    return lax.dynamic_index_in_dim(halves, index, 0, keepdims=False)
+
+
+def in_order(mine, other, bit):
+    first = jnp.where(bit == 0, mine, other)
+    second = jnp.where(bit == 0, other, mine)
+    return jnp.concatenate((first, second), axis=0)
+
+
+def pairs(size, step):
+    return [(i, i ^ step) for i in range(size)]
+
+
+def sum_tensor(part, size):
+    if size != 4:
+        return lax.psum(part, "tensor")
+    bit = lax.axis_index("tensor") % 2
+    halves = part.reshape(2, part.shape[0] // 2, part.shape[1])
+    got = lax.ppermute(pick(halves, 1 - bit), "tensor", pairs(4, 1))
+    held = add(pick(halves, bit), got)
+    held = add(held, lax.ppermute(held, "tensor", pairs(4, 2)))
+    return in_order(held, lax.ppermute(held, "tensor", pairs(4, 1)), bit)
+
+
+def levels(size):
+    return [1 << k for k in range(size.bit_length() - 1)]
+
+
+def sum_scatter_dp(part, size):
+    me = lax.axis_index("dp")
+    for step in levels(size):
+        bit = (me // step) % 2
+        halves = part.reshape(2, part.shape[0] // 2, part.shape[1])
+        got = lax.ppermute(pick(halves, 1 - bit), "dp", pairs(size, step))
+        part = add(pick(halves, bit), got)
+    return part
+
+
+def gather_dp(block, size):
+    me = lax.axis_index("dp")
+    for step in reversed(levels(size)):
+        bit = (me // step) % 2
+        block = in_order(block, lax.ppermute(block, "dp", pairs(size, step)), bit)
+    return block
+
+
+def sum_dp(value, size):
+    for step in levels(size):
+        value = value + lax.ppermute(value, "dp", pairs(size, step))
+    return value
 
 
 def body(
@@ -18,6 +78,8 @@
     up_weight,
     down_weight,
 ):
+    dp = lax.axis_size("dp")
+    tensor = lax.axis_size("tensor")
     steps_count, all_seqs, width_local = residual.shape
     local_seqs = queries.shape[1]
     local_copies = key_cache.shape[1]
@@ -60,44 +122,52 @@
         .astype(jnp.bfloat16)
         .reshape(steps_count, local_seqs, local_heads * head_size)
     )
-    piece = lax.all_gather(heads_out, "dp", axis=1, tiled=True)
-    flat_piece = piece.reshape(piece.shape[0] * piece.shape[1], piece.shape[2])
-    product = jnp.dot(flat_piece, out_weight, preferred_element_type=jnp.float32)
-    partials = product.reshape(piece.shape[0], piece.shape[1], out_weight.shape[1])
-    attn = lax.psum(partials.astype(jnp.bfloat16), "tensor")
-    mid = (residual.astype(jnp.float32) + attn.astype(jnp.float32)).astype(jnp.bfloat16)
-    mid_wide = mid.astype(jnp.float32)
+    rows = gather_dp(heads_out.reshape(steps_count * local_seqs, -1), dp)
     row_count = steps_count * all_seqs
-    squares = lax.psum(jnp.sum(mid_wide * mid_wide, axis=2), "dp")
-    full_width = width_local * lax.axis_size("dp")
-    inv_norm = lax.rsqrt(squares / full_width + 1e-05).reshape(1, row_count)
-    normed = (
-        (mid_wide * norm_gain.astype(jnp.float32)[None, None, :])
-        .astype(jnp.bfloat16)
-        .reshape(row_count, width_local)
-    )
-    contract_first = (((0,), (1,)), ((), ()))
-    gate_term = lax.dot_general(
-        gate_weight, normed, contract_first, preferred_element_type=jnp.float32
-    )
-    up_term = lax.dot_general(up_weight, normed, contract_first, preferred_element_type=jnp.float32)
-    both_terms = lax.psum_scatter(
-        jnp.concatenate((gate_term, up_term), axis=1).astype(jnp.bfloat16),
-        "dp",
-        scatter_dimension=0,
-        tiled=True,
-    ).astype(jnp.float32)
-    gate = both_terms[:, :row_count] * inv_norm
-    up_proj = both_terms[:, row_count:] * inv_norm
-    hidden = (jax.nn.silu(gate) * up_proj).astype(jnp.bfloat16)
-    down_term = lax.dot_general(
-        lax.all_gather(hidden, "dp", axis=0, tiled=True),
-        down_weight,
-        (((0,), (0,)), ((), ())),
-        preferred_element_type=jnp.float32,
-    )
-    ffn = lax.psum(down_term.astype(jnp.bfloat16), "tensor").astype(jnp.float32)
-    return (mid_wide + ffn.reshape(steps_count, all_seqs, width_local)).astype(jnp.bfloat16)
+    order = [0] * dp
+    for d in range(dp):
+        place = 0
+        for k, step in enumerate(levels(dp)):
+            place = place * 2 + (d // step) % 2
+        order[d] = place
+
+    def to_rows(block):
+        block = block.reshape(dp, steps_count, local_seqs, block.shape[-1])
+        block = jnp.stack([block[order[d]] for d in range(dp)], axis=1)
+        return block.reshape(row_count, block.shape[-1])
+
+    rows = to_rows(rows)
+    chunks = 2
+    wide = width_local // chunks
+    mids = []
+    resid = residual.reshape(row_count, width_local)
+    for c in range(chunks):
+        cols = slice(c * wide, (c + 1) * wide)
+        part = jnp.dot(rows, out_weight[:, cols], preferred_element_type=F32).astype(BF16)
+        mids.append(add(resid[:, cols], sum_tensor(part, tensor)))
+    mid = jnp.concatenate(mids, axis=1)
+    mid_wide = mid.astype(F32)
+    squares = sum_dp(jnp.sum(mid_wide * mid_wide, axis=1)[None, :], dp)
+    full_width = width_local * dp
+    inv_norm = lax.rsqrt(squares / full_width + 1e-05)
+    normed = (mid_wide * norm_gain.astype(F32)[None, :]).astype(BF16)
+    contract = (((0,), (1,)), ((), ()))
+    gate_term = lax.dot_general(gate_weight, normed, contract, preferred_element_type=F32)
+    up_term = lax.dot_general(up_weight, normed, contract, preferred_element_type=F32)
+    both = jnp.concatenate((gate_term, up_term), axis=1).astype(BF16)
+    both = sum_scatter_dp(both, dp).astype(F32)
+    gate = both[:, :row_count] * inv_norm
+    up_proj = both[:, row_count:] * inv_norm
+    hidden = (jax.nn.silu(gate) * up_proj).astype(BF16)
+    hidden = gather_dp(hidden, dp)
+    outs = []
+    for c in range(chunks):
+        cols = slice(c * wide, (c + 1) * wide)
+        part = lax.dot_general(
+            hidden, down_weight[:, cols], (((0,), (0,)), ((), ())), preferred_element_type=F32
+        ).astype(BF16)
+        outs.append(add(mids[c], sum_tensor(part, tensor)))
+    return jnp.concatenate(outs, axis=1).reshape(residual.shape)
 
 
 def solution(mesh):

time: 187 us -> 123 us (0.66)
  waiting for transfers between devices: 102 us -> 51.7 us
  starting transfers between devices: 0.09 us -> 24.8 us
  blocking collectives: 23.6 us -> 0 us
  between operations: 13.3 us -> 0.52 us
  local copies, waits for them, and re-layouts: 4.68 us -> 2.61 us
    psum x2 -> x0, waiting for transfers between devices: 78.1 us -> none  [the longest x1 39.2 us: body(): attn = lax.psum(partials.astype(jnp.bfloat16), 'tensor')]
    ppermute x0 -> x20, waiting for transfers between devices: none -> 51.7 us  [the longest x4 12 us: gather_dp(): block = in_order(block, lax.ppermute(block, 'dp', pairs(size, step)), bit)]
    ppermute x0 -> x20, starting transfers between devices: none -> 24.8 us  [the longest x4 7.66 us: sum_tensor(): held = add(held, lax.ppermute(held, 'tensor', pairs(4, 2)))]
    unnamed x4 -> x0, waiting for transfers between devices: 24 us -> none
    all_gather x2 -> x0, blocking collectives: 17.7 us -> none  [the longest x1 9.1 us: body(): lax.all_gather(hidden, 'dp', axis=0, tiled=True)]
    psum x1 -> x0, blocking collectives: 5.87 us -> none  [body(): squares = lax.psum(jnp.sum(mid_wide * mid_wide, axis=2), 'dp')]
    unnamed x15 -> x13, local copies, waits for them, and re-layouts: 4.52 us -> 0.96 us
    dot_general x4 -> x6, matrix products: 28.4 us -> 28.8 us  [the longest x2 8.45 us: body(): lax.dot_general(hidden, down_weight[:, cols], (((0,), (0,)), ((), ())), p...]
  transfers between devices with their start and end apart: 3 -> 20, of which waited for: 3 -> 16; matrix products, arithmetic and copies ran while one was open for 0% -> 6% of each run, Pallas kernels for 0% -> 0%
where the time goes in v1:
time: 123 us
  waiting for transfers between devices  51.7 us (42%)
  matrix products  37.1 us (30%)
  starting transfers between devices  24.8 us (20%)
  other arithmetic  5.7 us (5%)
  local copies, waits for them, and re-layouts  2.61 us (2%)
    ppermute x4, waiting for transfers between devices, gather_dp(): block = in_order(block, lax.ppermute(block, 'dp', pairs(size, step)), bit)  12 us
    ppermute x2, waiting for transfers between devices, sum_dp(): value = value + lax.ppermute(value, 'dp', pairs(size, step))  10.3 us
    ppermute x4, waiting for transfers between devices, sum_tensor(): return in_order(held, lax.ppermute(held, 'tensor', pairs(4, 1)), bit)  10.3 us
    ppermute x4, waiting for transfers between devices, sum_tensor(): got = lax.ppermute(pick(halves, 1 - bit), 'tensor', pairs(4, 1))  9.05 us
    dot_general x2, matrix products, body(): lax.dot_general(hidden, down_weight[:, cols], (((0,), (0,)), ((), ())), p...  8.45 us
    ppermute x4, starting transfers between devices, sum_tensor(): held = add(held, lax.ppermute(held, 'tensor', pairs(4, 2)))  7.66 us
    ppermute x4, waiting for transfers between devices, sum_tensor(): held = add(held, lax.ppermute(held, 'tensor', pairs(4, 2)))  7.43 us
    dot_general x1, matrix products, body(): lax.dot_general(gate_weight, normed, contract, preferred_element_type=F32)  7.26 us
  transfers between devices with their start and end apart: 20, of which 16 were waited for; matrix products, arithmetic and copies ran while one was open for 6% of the time, Pallas kernels for 0%

profile of v1, /device:TPU:0, one launch (start us, length us, event | category | flops | bytes accessed | tf_op | source)
XLA Modules:
  0.0 122.5 jit_solution(12946415278818103442)
XLA Ops:
  0.0 0.7 iota_compare_fusion
  0.8 0.9 copy.38
  1.7 5.9 %bitcast_reduce_fusion = (f32[2,16,2,8]{3,0,2,1:T(2,128)S(1)}, f32[16,2,1024,2,8]{2,4,3,1,0:T(8,128)S(1)}) fusion(pred[16,1024]{1,0:T(8,128)(4,1)S(1)} %iota_compare_fusion, bf16[2,16,2,8,128]{4,3,2,1,0:T(8,128)(2,1)S(1)} %bitcast.120, bf16[16,2,1024,128]{3,2,1,0:T(8,128)(2,1)} %param.16), kind=kOutput, calls=%fused_computation.17 | convolution fusion | flops 135790080 | bytes 10635264 | tf_op jit(solution)/shard_map/sbgjd,bgtd->sbgjt/dot_general | solution.py:93
  7.6 0.7 fusion.72
  8.4 0.7 fusion.16
  9.1 1.4 %fusion = f32[16,2,2,8,128]{4,3,2,1,0:T(8,128)S(1)} fusion(bf16[16,2,1024,128]{3,2,1,0:T(8,128)(2,1)S(1)} %copy-done.2, f32[16,2,1024,2,8]{2,4,3,1,0:T(8,128)S(1)} %get-tuple-element.28, f32[2,16,2,8]{3,0,2,1:T(2,128)S(1)} %max.7, pred[16,1024]{1,0:T(8,128)(4,1)S(1)} %iota_compare_fusion), kind=kOutput, calls=%fused_computation | convolution fusion | flops 136314880 | bytes 10766336 | tf_op jit(solution)/shard_map/sbgjt,bgtd->sbgjd/dot_general | solution.py:108
  10.5 0.1 fusion.58
  10.7 0.3 fusion.32
  11.0 3.0 %collective-permute-start = (bf16[32,2048]{1,0:T(8,128)(2,1)S(1)}, bf16[32,2048]{1,0:T(8,128)(2,1)S(1)}, u32[]{:S(2)}, u32[]{:S(2)}) collective-permute-start(bf16[32,2048]{1,0:T(8,128)(2,1)S(1)} %reshape_reshape.3), channel_id=1, source_target_pairs={{0,2},{1,3},{2,0},{3,1},{4,6},{5,7},{6,4},{7,5},{8,10},{9,11},{10,... | collective-permute-start | bytes 393224 | tf_op jit(solution)/shard_map/ppermute | solution.py:57
  14.0 3.5 %collective-permute-done = bf16[32,2048]{1,0:T(8,128)(2,1)S(1)} collective-permute-done((bf16[32,2048]{1,0:T(8,128)(2,1)S(1)}, bf16[32,2048]{1,0:T(8,128)(2,1)S(1)}, u32[]{:S(2)}, u32[]{:S(2)}) %collective-permute-start) | collective-permute-done | bytes 131104 | tf_op jit(solution)/shard_map/ppermute | solution.py:57
  17.6 0.1 collective-permute-start.1
  17.7 1.4 %collective-permute-done.1 = bf16[64,2048]{1,0:T(8,128)(2,1)S(1)} collective-permute-done((bf16[64,2048]{1,0:T(8,128)(2,1)S(1)}, bf16[64,2048]{1,0:T(8,128)(2,1)S(1)}, u32[]{:S(2)}, u32[]{:S(2)}) %collective-permute-start.1) | collective-permute-done | bytes 262176 | tf_op jit(solution)/shard_map/ppermute | solution.py:57
  19.2 0.1 broadcast_select_fusion.3
  19.3 0.1 pad_maximum_fusion.3
  19.4 2.9 %fusion.18 = bf16[128,1024]{1,0:T(8,128)(2,1)S(1)} fusion(bf16[128,2048]{1,0:T(8,128)(2,1)S(1)} %bitcast.114, bf16[2048,2048]{1,0:T(8,128)(2,1)} %param.19), kind=kOutput, calls=%fused_computation.30 | convolution fusion | flops 537001984 | bytes 4980736 | tf_op jit(solution)/shard_map/dot_general | solution.py:146
  22.4 1.9 %collective-permute-start.2 = (bf16[64,1024]{1,0:T(8,128)(2,1)S(1)}, bf16[64,1024]{1,0:T(8,128)(2,1)S(1)}, u32[]{:S(2)}, u32[]{:S(2)}) collective-permute-start(bf16[64,1024]{1,0:T(8,128)(2,1)S(1)} %dynamic-slice_bitcast_fusion.4), channel_id=1, source_target_pairs={{0,4},{4,0},{8,12},{12,8},{1,5},{5,1},{9,13},{13,9},{2,6},{6,2},{1... | collective-permute-start | bytes 393224 | tf_op jit(solution)/shard_map/ppermute | solution.py:33
  24.3 2.9 %fusion.21 = bf16[128,1024]{1,0:T(8,128)(2,1)S(1)} fusion(bf16[128,2048]{1,0:T(8,128)(2,1)S(1)} %bitcast.115, bf16[2048,2048]{1,0:T(8,128)(2,1)} %param.19), kind=kOutput, calls=%fused_computation.31 | convolution fusion | flops 537001984 | bytes 4980736 | tf_op jit(solution)/shard_map/dot_general | solution.py:146
  27.3 0.3 collective-permute-start.5
  27.5 0.6 collective-permute-done.2
  28.1 2.8 %collective-permute-start.3 = (bf16[64,1024]{1,0:T(8,128)(2,1)S(1)}, bf16[64,1024]{1,0:T(8,128)(2,1)S(1)}, u32[]{:S(2)}, u32[]{:S(2)}) collective-permute-start(bf16[64,1024]{1,0:T(8,128)(2,1)S(1)} %fusion.55), channel_id=1, source_target_pairs={{0,8},{4,12},{8,0},{12,4},{1,9},{5,13},{9,1},{13,5},{2,10},{6,14},... | collective-permute-start | bytes 393224 | tf_op jit(solution)/shard_map/ppermute | solution.py:35
  30.9 4.5 %collective-permute-done.5 = bf16[64,1024]{1,0:T(8,128)(2,1)S(1)} collective-permute-done((bf16[64,1024]{1,0:T(8,128)(2,1)S(1)}, bf16[64,1024]{1,0:T(8,128)(2,1)S(1)}, u32[]{:S(2)}, u32[]{:S(2)}) %collective-permute-start.5) | collective-permute-done | bytes 131104 | tf_op jit(solution)/shard_map/ppermute | solution.py:33
  35.4 1.0 collective-permute-start.6
  36.4 2.9 %collective-permute-start.4 = (bf16[64,1024]{1,0:T(8,128)(2,1)S(1)}, bf16[64,1024]{1,0:T(8,128)(2,1)S(1)}, u32[]{:S(2)}, u32[]{:S(2)}) collective-permute-start(bf16[64,1024]{1,0:T(8,128)(2,1)S(1)} %add_convert_fusion.7), channel_id=1, source_target_pairs={{0,4},{4,0},{8,12},{12,8},{1,5},{5,1},{9,13},{13,9},{2,6},{6,2},{1... | collective-permute-start | bytes 393224 | tf_op jit(solution)/shard_map/ppermute | solution.py:36
  39.3 3.8 %collective-permute-done.6 = bf16[64,1024]{1,0:T(8,128)(2,1)S(1)} collective-permute-done((bf16[64,1024]{1,0:T(8,128)(2,1)S(1)}, bf16[64,1024]{1,0:T(8,128)(2,1)S(1)}, u32[]{:S(2)}, u32[]{:S(2)}) %collective-permute-start.6) | collective-permute-done | bytes 131104 | tf_op jit(solution)/shard_map/ppermute | solution.py:35
  43.2 0.1 collective-permute-start.7
  43.3 2.0 %collective-permute-done.4 = bf16[64,1024]{1,0:T(8,128)(2,1)S(1)} collective-permute-done((bf16[64,1024]{1,0:T(8,128)(2,1)S(1)}, bf16[64,1024]{1,0:T(8,128)(2,1)S(1)}, u32[]{:S(2)}, u32[]{:S(2)}) %collective-permute-start.4) | collective-permute-done | bytes 131104 | tf_op jit(solution)/shard_map/ppermute | solution.py:36
  45.3 3.3 %collective-permute-done.7 = bf16[64,1024]{1,0:T(8,128)(2,1)S(1)} collective-permute-done((bf16[64,1024]{1,0:T(8,128)(2,1)S(1)}, bf16[64,1024]{1,0:T(8,128)(2,1)S(1)}, u32[]{:S(2)}, u32[]{:S(2)}) %collective-permute-start.7) | collective-permute-done | bytes 131104 | tf_op jit(solution)/shard_map/ppermute | solution.py:36
  48.6 0.2 add_convert_fusion.3
  48.8 7.3 %fusion.8 = bf16[3584,128]{0,1:T(8,128)(2,1)S(1)} fusion(bf16[2048,3584]{1,0:T(8,128)(2,1)} %param.21, f32[2048]{0:T(1024)S(1)} %convert_element_type.209, bf16[128,1024]{1,0:T(8,128)(2,1)S(1)} %get-tuple-element.8, bf16[128,1024]{1,0:T(8,128)(2,1)S(1)} %get-tuple-element.7), kind=kOutput, calls=%fused_computation.10 | convolution fusion | flops 1881079808 | bytes 16130048 | tf_op jit(solution)/shard_map/dot_general | solution.py:155
  56.1 0.8 copy.36
  56.9 7.3 %fusion.9 = bf16[3584,128]{0,1:T(8,128)(2,1)S(1)} fusion(bf16[2048,3584]{1,0:T(8,128)(2,1)} %param.22, f32[2048]{0:T(1024)S(1)} %convert_element_type.209, bf16[128,1024]{1,0:T(8,128)(2,1)S(1)} %get-tuple-element.8, bf16[128,1024]{1,0:T(8,128)(2,1)S(1)} %get-tuple-element.7), kind=kOutput, calls=%fused_computation.11 | convolution fusion | flops 1881079808 | bytes 16130048 | tf_op jit(solution)/shard_map/dot_general | solution.py:156
  64.1 0.6 copy.37
  64.8 0.1 fusion.43
  64.9 0.1 collective-permute-start.8
  65.0 2.6 %collective-permute-done.8 = bf16[1792,256]{1,0:T(8,128)(2,1)} collective-permute-done((bf16[1792,256]{1,0:T(8,128)(2,1)S(1)}, bf16[1792,256]{1,0:T(8,128)(2,1)}, u32[]{:S(2)}, u32[]{:S(2)}) %collective-permute-start.8) | collective-permute-done | bytes 917536 | tf_op jit(solution)/shard_map/ppermute | solution.py:48
  67.5 1.4 %fusion.15 = bf16[1792,256]{1,0:T(8,128)(2,1)S(1)} fusion(bf16[1792,256]{1,0:T(8,128)(2,1)} %collective-permute-done.8, s32[]{:T(128)S(6)} %select_n.182, bf16[2,1792,128]{2,1,0:T(8,128)(2,1)S(1)} %bitcast.108, bf16[2,1792,128]{2,1,0:T(8,128)(2,1)S(1)} %bitcast.110), kind=kLoop, calls=%fused_computation.25 | loop fusion | flops 3670016 | bytes 3670020 | tf_op jit(solution)/shard_map/convert_element_type | solution.py:11
  69.0 1.5 %collective-permute-start.9 = (bf16[896,256]{1,0:T(8,128)(2,1)S(1)}, bf16[896,256]{1,0:T(8,128)(2,1)S(1)}, u32[]{:S(2)}, u32[]{:S(2)}) collective-permute-start(bf16[896,256]{1,0:T(8,128)(2,1)S(1)} %dynamic-slice_bitcast_fusion), channel_id=1, source_target_pairs={{0,2},{1,3},{2,0},{3,1},{4,6},{5,7},{6,4},{7,5},{8,10},{9,11},{10,... | collective-permute-start | bytes 1376264 | tf_op jit(solution)/shard_map/ppermute | solution.py:48
  70.6 0.2 fusion.36
  70.8 1.1 collective-permute-done.10
  71.9 0.6 collective-permute-start.11
  72.5 9.2 %collective-permute-done.11 = f32[1,128]{1,0:T(1,128)S(1)} collective-permute-done((f32[1,128]{1,0:T(1,128)S(1)}, f32[1,128]{1,0:T(1,128)S(1)}, u32[]{:S(2)}, u32[]{:S(2)}) %collective-permute-start.11) | collective-permute-done | bytes 544 | tf_op jit(solution)/shard_map/ppermute | solution.py:63
  81.7 0.1 fusion.47
  81.8 0.1 fusion.49
  82.0 1.5 %collective-permute-start.12 = (bf16[896,128]{1,0:T(8,128)(2,1)S(1)}, bf16[896,128]{1,0:T(8,128)(2,1)S(1)}, u32[]{:S(2)}, u32[]{:S(2)}) collective-permute-start(bf16[896,128]{1,0:T(8,128)(2,1)S(1)} %fusion.49), channel_id=1, source_target_pairs={{0,2},{1,3},{2,0},{3,1},{4,6},{5,7},{6,4},{7,5},{8,10},{9,11},{10,... | collective-permute-start | bytes 688136 | tf_op jit(solution)/shard_map/ppermute | solution.py:57
  83.5 5.3 %collective-permute-done.12 = bf16[896,128]{1,0:T(8,128)(2,1)S(1)} collective-permute-done((bf16[896,128]{1,0:T(8,128)(2,1)S(1)}, bf16[896,128]{1,0:T(8,128)(2,1)S(1)}, u32[]{:S(2)}, u32[]{:S(2)}) %collective-permute-start.12) | collective-permute-done | bytes 229408 | tf_op jit(solution)/shard_map/ppermute | solution.py:57
  88.8 0.2 broadcast_select_fusion.5
  89.0 0.1 collective-permute-start.13
  89.1 1.8 %collective-permute-done.13 = bf16[1792,128]{1,0:T(8,128)(2,1)S(1)} collective-permute-done((bf16[1792,128]{1,0:T(8,128)(2,1)S(1)}, bf16[1792,128]{1,0:T(8,128)(2,1)S(1)}, u32[]{:S(2)}, u32[]{:S(2)}) %collective-permute-start.13) | collective-permute-done | bytes 458784 | tf_op jit(solution)/shard_map/ppermute | solution.py:57
  90.9 0.2 broadcast_select_fusion.1
  91.1 4.2 %fusion.27 = bf16[128,1024]{1,0:T(8,128)(2,1)S(1)} fusion(bf16[3584,2048]{1,0:T(8,128)(2,1)} %param.23, bf16[1792,128]{1,0:T(8,128)(2,1)S(1)} %get-tuple-element.6, bf16[1792,128]{1,0:T(8,128)(2,1)S(1)} %get-tuple-element.5), kind=kOutput, calls=%fused_computation.33 | convolution fusion | flops 941490176 | bytes 8519680 | tf_op jit(solution)/shard_map/dot_general | solution.py:166
  95.4 0.4 collective-permute-start.17
  95.7 4.2 %fusion.24 = bf16[128,1024]{1,0:T(8,128)(2,1)S(1)} fusion(bf16[3584,2048]{1,0:T(8,128)(2,1)} %param.23, bf16[1792,128]{1,0:T(8,128)(2,1)S(1)} %get-tuple-element.6, bf16[1792,128]{1,0:T(8,128)(2,1)S(1)} %get-tuple-element.5), kind=kOutput, calls=%fused_computation.32 | convolution fusion | flops 941490176 | bytes 8519680 | tf_op jit(solution)/shard_map/dot_general | solution.py:166
  100.0 1.8 %collective-permute-start.14 = (bf16[64,1024]{1,0:T(8,128)(2,1)S(1)}, bf16[64,1024]{1,0:T(8,128)(2,1)S(1)}, u32[]{:S(2)}, u32[]{:S(2)}) collective-permute-start(bf16[64,1024]{1,0:T(8,128)(2,1)S(1)} %dynamic-slice_bitcast_fusion.2), channel_id=1, source_target_pairs={{0,4},{4,0},{8,12},{12,8},{1,5},{5,1},{9,13},{13,9},{2,6},{6,2},{1... | collective-permute-start | bytes 393224 | tf_op jit(solution)/shard_map/ppermute | solution.py:33
  101.8 1.6 %collective-permute-start.18 = (bf16[64,1024]{1,0:T(8,128)(2,1)S(1)}, bf16[64,1024]{1,0:T(8,128)(2,1)S(1)}, u32[]{:S(2)}, u32[]{:S(2)}) collective-permute-start(bf16[64,1024]{1,0:T(8,128)(2,1)S(1)} %fusion.52), channel_id=1, source_target_pairs={{0,8},{4,12},{8,0},{12,4},{1,9},{5,13},{9,1},{13,5},{2,10},{6,14},... | collective-permute-start | bytes 393224 | tf_op jit(solution)/shard_map/ppermute | solution.py:35
  103.5 4.0 %collective-permute-done.14 = bf16[64,1024]{1,0:T(8,128)(2,1)S(1)} collective-permute-done((bf16[64,1024]{1,0:T(8,128)(2,1)S(1)}, bf16[64,1024]{1,0:T(8,128)(2,1)S(1)}, u32[]{:S(2)}, u32[]{:S(2)}) %collective-permute-start.14) | collective-permute-done | bytes 131104 | tf_op jit(solution)/shard_map/ppermute | solution.py:33
  107.5 2.2 %collective-permute-start.15 = (bf16[64,1024]{1,0:T(8,128)(2,1)S(1)}, bf16[64,1024]{1,0:T(8,128)(2,1)S(1)}, u32[]{:S(2)}, u32[]{:S(2)}) collective-permute-start(bf16[64,1024]{1,0:T(8,128)(2,1)S(1)} %fusion.53), channel_id=1, source_target_pairs={{0,8},{4,12},{8,0},{12,4},{1,9},{5,13},{9,1},{13,5},{2,10},{6,14},... | collective-permute-start | bytes 393224 | tf_op jit(solution)/shard_map/ppermute | solution.py:35
  109.8 2.9 %collective-permute-start.19 = (bf16[64,1024]{1,0:T(8,128)(2,1)S(1)}, bf16[64,1024]{1,0:T(8,128)(2,1)S(1)}, u32[]{:S(2)}, u32[]{:S(2)}) collective-permute-start(bf16[64,1024]{1,0:T(8,128)(2,1)S(1)} %add_convert_fusion.4), channel_id=1, source_target_pairs={{0,4},{4,0},{8,12},{12,8},{1,5},{5,1},{9,13},{13,9},{2,6},{6,2},{1... | collective-permute-start | bytes 393224 | tf_op jit(solution)/shard_map/ppermute | solution.py:36
  112.7 3.6 %collective-permute-done.15 = bf16[64,1024]{1,0:T(8,128)(2,1)S(1)} collective-permute-done((bf16[64,1024]{1,0:T(8,128)(2,1)S(1)}, bf16[64,1024]{1,0:T(8,128)(2,1)S(1)}, u32[]{:S(2)}, u32[]{:S(2)}) %collective-permute-start.15) | collective-permute-done | bytes 131104 | tf_op jit(solution)/shard_map/ppermute | solution.py:35
  116.4 0.1 collective-permute-start.16
  116.5 1.2 collective-permute-done.19
  117.7 0.1 add_convert_fusion
  117.7 3.9 %collective-permute-done.16 = bf16[64,1024]{1,0:T(8,128)(2,1)S(1)} collective-permute-done((bf16[64,1024]{1,0:T(8,128)(2,1)S(1)}, bf16[64,1024]{1,0:T(8,128)(2,1)S(1)}, u32[]{:S(2)}, u32[]{:S(2)}) %collective-permute-start.16) | collective-permute-done | bytes 131104 | tf_op jit(solution)/shard_map/ppermute | solution.py:36
  121.6 0.1 add_convert_fusion.1
  121.7 0.8 pad_maximum_fusion.5
  (46 shorter events, 0.8 us)
Async XLA Ops:
  0.0 10.7 %copy-start = (bf16[2,16,2,128]{3,2,1,0:T(2,128)(2,1)S(1)}, bf16[2,16,2,128]{3,2,1,0:T(2,128)(2,1)}, u32[]{:S(2)}) copy-start(bf16[2,16,2,128]{3,2,1,0:T(2,128)(2,1)} %param.15) | copy-start | bytes 49156
  1.7 6.0 %copy-start.5 = (bf16[2,16,2,128]{3,2,1,0:T(2,128)(2,1)S(1)}, bf16[2,16,2,128]{3,2,1,0:T(2,128)(2,1)}, u32[]{:S(2)}) copy-start(bf16[2,16,2,128]{3,2,1,0:T(2,128)(2,1)} %param.14) | copy-start | bytes 49156
  1.7 7.4 %copy-start.2 = (bf16[16,2,1024,128]{3,2,1,0:T(8,128)(2,1)S(1)}, bf16[16,2,1024,128]{3,2,1,0:T(8,128)(2,1)}, u32[]{:S(2)}) copy-start(bf16[16,2,1024,128]{3,2,1,0:T(8,128)(2,1)} %param.17) | copy-start | bytes 25165828
  10.5 7.2 %copy-start.4 = (bf16[2048]{0:T(1024)(128)(2,1)S(1)}, bf16[2048]{0:T(1024)(128)(2,1)}, u32[]{:S(2)}) copy-start(bf16[2048]{0:T(1024)(128)(2,1)} %param.20) | copy-start | bytes 12292
  11.0 6.5 %collective-permute-start = (bf16[32,2048]{1,0:T(8,128)(2,1)S(1)}, bf16[32,2048]{1,0:T(8,128)(2,1)S(1)}, u32[]{:S(2)}, u32[]{:S(2)}) collective-permute-start(bf16[32,2048]{1,0:T(8,128)(2,1)S(1)} %reshape_reshape.3), channel_id=1, source_target_pairs={{0,2},{1,3},{2,0},{3,1},{4,6},{5,7},{6,4},{7,5},{8,10},{9,11},{10,... | collective-permute-start | bytes 393224 | tf_op jit(solution)/shard_map/ppermute | solution.py:57
  17.6 1.6 %collective-permute-start.1 = (bf16[64,2048]{1,0:T(8,128)(2,1)S(1)}, bf16[64,2048]{1,0:T(8,128)(2,1)S(1)}, u32[]{:S(2)}, u32[]{:S(2)}) collective-permute-start(bf16[64,2048]{1,0:T(8,128)(2,1)S(1)} %pad_maximum_fusion.7), channel_id=1, source_target_pairs={{0,1},{1,0},{2,3},{3,2},{4,5},{5,4},{6,7},{7,6},{8,9},{9,8},{10,11... | collective-permute-start | bytes 786440 | tf_op jit(solution)/shard_map/ppermute | solution.py:57
  22.4 5.7 %collective-permute-start.2 = (bf16[64,1024]{1,0:T(8,128)(2,1)S(1)}, bf16[64,1024]{1,0:T(8,128)(2,1)S(1)}, u32[]{:S(2)}, u32[]{:S(2)}) collective-permute-start(bf16[64,1024]{1,0:T(8,128)(2,1)S(1)} %dynamic-slice_bitcast_fusion.4), channel_id=1, source_target_pairs={{0,4},{4,0},{8,12},{12,8},{1,5},{5,1},{9,13},{13,9},{2,6},{6,2},{1... | collective-permute-start | bytes 393224 | tf_op jit(solution)/shard_map/ppermute | solution.py:33
  27.2 21.4 %copy-start.3 = (bf16[2,64,2048]{2,1,0:T(8,128)(2,1)S(1)}, bf16[2,64,2048]{2,1,0:T(8,128)(2,1)}, u32[]{:S(2)}) copy-start(bf16[2,64,2048]{2,1,0:T(8,128)(2,1)} %param.12) | copy-start | bytes 1572868
  27.3 8.1 %collective-permute-start.5 = (bf16[64,1024]{1,0:T(8,128)(2,1)S(1)}, bf16[64,1024]{1,0:T(8,128)(2,1)S(1)}, u32[]{:S(2)}, u32[]{:S(2)}) collective-permute-start(bf16[64,1024]{1,0:T(8,128)(2,1)S(1)} %dynamic-slice_bitcast_fusion.3), channel_id=1, source_target_pairs={{0,4},{4,0},{8,12},{12,8},{1,5},{5,1},{9,13},{13,9},{2,6},{6,2},{1... | collective-permute-start | bytes 393224 | tf_op jit(solution)/shard_map/ppermute | solution.py:33
  28.1 8.3 %collective-permute-start.3 = (bf16[64,1024]{1,0:T(8,128)(2,1)S(1)}, bf16[64,1024]{1,0:T(8,128)(2,1)S(1)}, u32[]{:S(2)}, u32[]{:S(2)}) collective-permute-start(bf16[64,1024]{1,0:T(8,128)(2,1)S(1)} %fusion.55), channel_id=1, source_target_pairs={{0,8},{4,12},{8,0},{12,4},{1,9},{5,13},{9,1},{13,5},{2,10},{6,14},... | collective-permute-start | bytes 393224 | tf_op jit(solution)/shard_map/ppermute | solution.py:35
  35.4 7.7 %collective-permute-start.6 = (bf16[64,1024]{1,0:T(8,128)(2,1)S(1)}, bf16[64,1024]{1,0:T(8,128)(2,1)S(1)}, u32[]{:S(2)}, u32[]{:S(2)}) collective-permute-start(bf16[64,1024]{1,0:T(8,128)(2,1)S(1)} %fusion.54), channel_id=1, source_target_pairs={{0,8},{4,12},{8,0},{12,4},{1,9},{5,13},{9,1},{13,5},{2,10},{6,14},... | collective-permute-start | bytes 393224 | tf_op jit(solution)/shard_map/ppermute | solution.py:35
  36.4 8.8 %collective-permute-start.4 = (bf16[64,1024]{1,0:T(8,128)(2,1)S(1)}, bf16[64,1024]{1,0:T(8,128)(2,1)S(1)}, u32[]{:S(2)}, u32[]{:S(2)}) collective-permute-start(bf16[64,1024]{1,0:T(8,128)(2,1)S(1)} %add_convert_fusion.7), channel_id=1, source_target_pairs={{0,4},{4,0},{8,12},{12,8},{1,5},{5,1},{9,13},{13,9},{2,6},{6,2},{1... | collective-permute-start | bytes 393224 | tf_op jit(solution)/shard_map/ppermute | solution.py:36
  43.2 5.4 %collective-permute-start.7 = (bf16[64,1024]{1,0:T(8,128)(2,1)S(1)}, bf16[64,1024]{1,0:T(8,128)(2,1)S(1)}, u32[]{:S(2)}, u32[]{:S(2)}) collective-permute-start(bf16[64,1024]{1,0:T(8,128)(2,1)S(1)} %add_convert_fusion.6), channel_id=1, source_target_pairs={{0,4},{4,0},{8,12},{12,8},{1,5},{5,1},{9,13},{13,9},{2,6},{6,2},{1... | collective-permute-start | bytes 393224 | tf_op jit(solution)/shard_map/ppermute | solution.py:36
  64.9 2.7 %collective-permute-start.8 = (bf16[1792,256]{1,0:T(8,128)(2,1)S(1)}, bf16[1792,256]{1,0:T(8,128)(2,1)}, u32[]{:S(2)}, u32[]{:S(2)}) collective-permute-start(bf16[1792,256]{1,0:T(8,128)(2,1)S(1)} %fusion.43), channel_id=1, source_target_pairs={{0,1},{1,0},{2,3},{3,2},{4,5},{5,4},{6,7},{7,6},{8,9},{9,8},{10,11... | collective-permute-start | bytes 2752520 | tf_op jit(solution)/shard_map/ppermute | solution.py:48
  69.0 12.7 %collective-permute-start.9 = (bf16[896,256]{1,0:T(8,128)(2,1)S(1)}, bf16[896,256]{1,0:T(8,128)(2,1)S(1)}, u32[]{:S(2)}, u32[]{:S(2)}) collective-permute-start(bf16[896,256]{1,0:T(8,128)(2,1)S(1)} %dynamic-slice_bitcast_fusion), channel_id=1, source_target_pairs={{0,2},{1,3},{2,0},{3,1},{4,6},{5,7},{6,4},{7,5},{8,10},{9,11},{10,... | collective-permute-start | bytes 1376264 | tf_op jit(solution)/shard_map/ppermute | solution.py:48
  70.7 1.2 collective-permute-start.10
  71.9 9.8 %collective-permute-start.11 = (f32[1,128]{1,0:T(1,128)S(1)}, f32[1,128]{1,0:T(1,128)S(1)}, u32[]{:S(2)}, u32[]{:S(2)}) collective-permute-start(f32[1,128]{1,0:T(1,128)S(1)} %bitcast_add_fusion), channel_id=1, source_target_pairs={{0,2},{1,3},{2,0},{3,1},{4,6},{5,7},{6,4},{7,5},{8,10},{9,11},{10,... | collective-permute-start | bytes 1544 | tf_op jit(solution)/shard_map/ppermute | solution.py:63
  82.0 6.8 %collective-permute-start.12 = (bf16[896,128]{1,0:T(8,128)(2,1)S(1)}, bf16[896,128]{1,0:T(8,128)(2,1)S(1)}, u32[]{:S(2)}, u32[]{:S(2)}) collective-permute-start(bf16[896,128]{1,0:T(8,128)(2,1)S(1)} %fusion.49), channel_id=1, source_target_pairs={{0,2},{1,3},{2,0},{3,1},{4,6},{5,7},{6,4},{7,5},{8,10},{9,11},{10,... | collective-permute-start | bytes 688136 | tf_op jit(solution)/shard_map/ppermute | solution.py:57
  89.0 1.9 %collective-permute-start.13 = (bf16[1792,128]{1,0:T(8,128)(2,1)S(1)}, bf16[1792,128]{1,0:T(8,128)(2,1)S(1)}, u32[]{:S(2)}, u32[]{:S(2)}) collective-permute-start(bf16[1792,128]{1,0:T(8,128)(2,1)S(1)} %pad_maximum_fusion.6), channel_id=1, source_target_pairs={{0,1},{1,0},{2,3},{3,2},{4,5},{5,4},{6,7},{7,6},{8,9},{9,8},{10,11... | collective-permute-start | bytes 1376264 | tf_op jit(solution)/shard_map/ppermute | solution.py:57
  95.4 6.4 %collective-permute-start.17 = (bf16[64,1024]{1,0:T(8,128)(2,1)S(1)}, bf16[64,1024]{1,0:T(8,128)(2,1)S(1)}, u32[]{:S(2)}, u32[]{:S(2)}) collective-permute-start(bf16[64,1024]{1,0:T(8,128)(2,1)S(1)} %dynamic-slice_bitcast_fusion.1), channel_id=1, source_target_pairs={{0,4},{4,0},{8,12},{12,8},{1,5},{5,1},{9,13},{13,9},{2,6},{6,2},{1... | collective-permute-start | bytes 393224 | tf_op jit(solution)/shard_map/ppermute | solution.py:33
  100.0 7.5 %collective-permute-start.14 = (bf16[64,1024]{1,0:T(8,128)(2,1)S(1)}, bf16[64,1024]{1,0:T(8,128)(2,1)S(1)}, u32[]{:S(2)}, u32[]{:S(2)}) collective-permute-start(bf16[64,1024]{1,0:T(8,128)(2,1)S(1)} %dynamic-slice_bitcast_fusion.2), channel_id=1, source_target_pairs={{0,4},{4,0},{8,12},{12,8},{1,5},{5,1},{9,13},{13,9},{2,6},{6,2},{1... | collective-permute-start | bytes 393224 | tf_op jit(solution)/shard_map/ppermute | solution.py:33
  101.8 8.0 %collective-permute-start.18 = (bf16[64,1024]{1,0:T(8,128)(2,1)S(1)}, bf16[64,1024]{1,0:T(8,128)(2,1)S(1)}, u32[]{:S(2)}, u32[]{:S(2)}) collective-permute-start(bf16[64,1024]{1,0:T(8,128)(2,1)S(1)} %fusion.52), channel_id=1, source_target_pairs={{0,8},{4,12},{8,0},{12,4},{1,9},{5,13},{9,1},{13,5},{2,10},{6,14},... | collective-permute-start | bytes 393224 | tf_op jit(solution)/shard_map/ppermute | solution.py:35
  107.5 8.8 %collective-permute-start.15 = (bf16[64,1024]{1,0:T(8,128)(2,1)S(1)}, bf16[64,1024]{1,0:T(8,128)(2,1)S(1)}, u32[]{:S(2)}, u32[]{:S(2)}) collective-permute-start(bf16[64,1024]{1,0:T(8,128)(2,1)S(1)} %fusion.53), channel_id=1, source_target_pairs={{0,8},{4,12},{8,0},{12,4},{1,9},{5,13},{9,1},{13,5},{2,10},{6,14},... | collective-permute-start | bytes 393224 | tf_op jit(solution)/shard_map/ppermute | solution.py:35
  109.8 12.8 %copy-start.1 = (bf16[2,16,2,128]{3,2,1,0:T(2,128)(2,1)S(1)}, bf16[2,16,2,128]{3,2,1,0:T(2,128)(2,1)}, u32[]{:S(2)}) copy-start(bf16[2,16,2,128]{3,2,1,0:T(2,128)(2,1)} %param.15) | copy-start | bytes 49156
  109.8 7.8 %collective-permute-start.19 = (bf16[64,1024]{1,0:T(8,128)(2,1)S(1)}, bf16[64,1024]{1,0:T(8,128)(2,1)S(1)}, u32[]{:S(2)}, u32[]{:S(2)}) collective-permute-start(bf16[64,1024]{1,0:T(8,128)(2,1)S(1)} %add_convert_fusion.4), channel_id=1, source_target_pairs={{0,4},{4,0},{8,12},{12,8},{1,5},{5,1},{9,13},{13,9},{2,6},{6,2},{1... | collective-permute-start | bytes 393224 | tf_op jit(solution)/shard_map/ppermute | solution.py:36
  116.4 5.2 %collective-permute-start.16 = (bf16[64,1024]{1,0:T(8,128)(2,1)S(1)}, bf16[64,1024]{1,0:T(8,128)(2,1)S(1)}, u32[]{:S(2)}, u32[]{:S(2)}) collective-permute-start(bf16[64,1024]{1,0:T(8,128)(2,1)S(1)} %add_convert_fusion.5), channel_id=1, source_target_pairs={{0,4},{4,0},{8,12},{12,8},{1,5},{5,1},{9,13},{13,9},{2,6},{6,2},{1... | collective-permute-start | bytes 393224 | tf_op jit(solution)/shard_map/ppermute | solution.py:36

commit v2 on v0

v2 whole, which is shorter than its diff:
```python
import functools

import jax
import jax.numpy as jnp
from jax import lax
from jax.experimental import pallas as pl
from jax.experimental.pallas import tpu as pltpu
from jax.sharding import PartitionSpec as P

BF16 = jnp.bfloat16
F32 = jnp.float32
MIB = 1 << 20


def add(a, b):
    return (a.astype(F32) + b.astype(F32)).astype(BF16)


def sum_kernel(dtype, *refs):
    total = functools.reduce(jnp.add, [ref[...].astype(F32) for ref in refs[:-1]])
    refs[-1][...] = total.astype(dtype)


def total_of(*terms, dtype=BF16):
    vmem = pl.BlockSpec(memory_space=pltpu.VMEM)
    return pl.pallas_call(
        functools.partial(sum_kernel, dtype),
        in_specs=[vmem] * len(terms),
        out_specs=vmem,
        out_shape=jax.ShapeDtypeStruct(terms[0].shape, dtype),
        cost_estimate=cost(terms[0].size, 4 * terms[0].size),
        compiler_params=pltpu.CompilerParams(vmem_limit_bytes=2 * MIB),
    )(*terms)


def cost(flops, read):
    return pl.CostEstimate(flops=flops, bytes_accessed=read, transcendentals=0)


def attention_kernel(first, count, len_ref, q_hbm, k_hbm, v_hbm, nk_hbm, nv_hbm, w_hbm, *refs):
    o_ref, w_ref, q_ref, nk_ref, nv_ref, k_buf, v_buf, out_buf, sem, small_sem, w_sem = refs
    small = [
        pltpu.make_async_copy(src, dst, small_sem.at[k])
        for k, (src, dst) in enumerate(((q_hbm, q_ref), (nk_hbm, nk_ref), (nv_hbm, nv_ref)))
    ]
    for move in small:
        move.start()
    steps = q_ref.shape[0]
    _, copies, slots, head = k_hbm.shape
    group = q_ref.shape[2] // (copies * head)
    rows = steps * group
    part = 256
    parts = slots // part
    batch = 4
    scaling = head ** (-0.5)

    def moves(b, c):
        here = pl.ds(c * part, part)
        return (
            pltpu.make_async_copy(k_hbm.at[first + b, :, here], k_buf.at[b, :, here], sem.at[0, b]),
            pltpu.make_async_copy(v_hbm.at[first + b, :, here], v_buf.at[b, :, here], sem.at[1, b]),
        )

    def start(b, c):
        for move in moves(b, c):
            move.start()

    def clear(b, c):
        v_buf[b, :, c * part : (c + 1) * part] = jnp.zeros((copies, part, head), BF16)

    def wait(b, c):
        for move in moves(b, c):
            move.wait()

    for b in range(count):
        start(b, 0)
        for c in range(1, parts):
            live = len_ref[first + b] > c * part
            pl.when(live)(functools.partial(start, b, c))
            pl.when(jnp.logical_not(live))(functools.partial(clear, b, c))

    weight = pltpu.make_async_copy(w_hbm, w_ref, w_sem)
    weight.start()
    for move in small:
        move.wait()
    slot = lax.broadcasted_iota(jnp.int32, (rows, slots), 1)
    step = lax.broadcasted_iota(jnp.int32, (rows, 1), 0) // group
    for b0 in range(0, count, batch):
        work = [(b, g) for b in range(b0, min(b0 + batch, count)) for g in range(copies)]
        asked, recent = [], []
        for b, g in work:
            pick = [
                q_ref[s, first + b : first + b + 1, (g * group + j) * head : (g * group + j + 1) * head]
                for s in range(steps)
                for j in range(group)
            ]
            wide = jnp.concatenate([p.astype(F32) for p in pick], axis=0)
            asked.append(wide.astype(BF16))
            found = []
            for r in range(steps):
                key = nk_ref[r, first + b, g : g + 1, :].astype(F32)
                score = jnp.sum(wide * key, axis=1, keepdims=True) * scaling
                found.append(jnp.where(step >= r, score, -jnp.inf))
            recent.append(found)
        for b in range(b0, min(b0 + batch, count)):
            wait(b, 0)
            for c in range(1, parts):
                pl.when(len_ref[first + b] > c * part)(functools.partial(wait, b, c))
        scores = [
            lax.dot_general(q, k_buf[b, g], (((1,), (1,)), ((), ())), preferred_element_type=F32)
            for q, (b, g) in zip(asked, work)
        ]
        scores = [
            jnp.where(slot < len_ref[first + b], s * scaling, -jnp.inf)
            for s, (b, g) in zip(scores, work)
        ]
        tops = [
            functools.reduce(jnp.maximum, [jnp.max(s, axis=1, keepdims=True)] + found)
            for s, found in zip(scores, recent)
        ]
        weights = [jnp.exp(s - top) for s, top in zip(scores, tops)]
        fresh = [[jnp.exp(x - top) for x in found] for found, top in zip(recent, tops)]
        totals = [jnp.sum(w, axis=1, keepdims=True) + sum(f) for w, f in zip(weights, fresh)]
        blends = [
            jnp.dot(w.astype(BF16), v_buf[b, g], preferred_element_type=F32)
            for w, (b, g) in zip(weights, work)
        ]
        for (b, g), blend, f, total in zip(work, blends, fresh, totals):
            for r in range(steps):
                value = nv_ref[r, first + b, g : g + 1, :].astype(F32)
                blend = blend + f[r].astype(BF16).astype(F32) * value
            out = blend / total
            for s in range(steps):
                for j in range(group):
                    cols = slice((g * group + j) * head, (g * group + j + 1) * head)
                    at = s * count + b
                    out_buf[at : at + 1, cols] = out[s * group + j : s * group + j + 1, :]
    o_ref[...] = out_buf[...].astype(BF16)
    weight.wait()


def attention(queries, new_keys, new_values, key_cache, value_cache, lengths, weight):
    first, count = 0, queries.shape[1]
    steps, _, deep = queries.shape
    _, copies, slots, head = key_cache.shape
    vmem = pl.BlockSpec(memory_space=pltpu.VMEM)
    hbm = pl.BlockSpec(memory_space=pl.ANY)
    buffer = pltpu.VMEM((count, copies, slots, head), BF16)
    moved = [queries, key_cache, value_cache, new_keys, new_values, weight]
    moved = [pltpu.with_memory_space_constraint(x, pltpu.HBM) for x in moved]
    return pl.pallas_call(
        functools.partial(attention_kernel, first, count),
        in_specs=[pl.BlockSpec(memory_space=pltpu.SMEM)] + [hbm] * 6,
        out_specs=[vmem, vmem],
        out_shape=[
            jax.ShapeDtypeStruct((steps * count, deep), BF16),
            pltpu.VMEM(weight.shape, weight.dtype),
        ],
        scratch_shapes=[
            pltpu.VMEM(queries.shape, BF16),
            pltpu.VMEM(new_keys.shape, BF16),
            pltpu.VMEM(new_values.shape, BF16),
            buffer,
            buffer,
            pltpu.VMEM((steps * count, deep), F32),
            pltpu.SemaphoreType.DMA((2, count)),
            pltpu.SemaphoreType.DMA((3,)),
            pltpu.SemaphoreType.DMA(()),
        ],
        cost_estimate=cost(4 * steps * count * slots * deep, 4 * count * copies * slots * head),
        compiler_params=pltpu.CompilerParams(vmem_limit_bytes=40 * MIB),
    )(lengths, *moved)


def fetch_kernel(after, pieces, src_ref, *refs):
    o_ref, sem = refs[after], refs[-1]
    step = src_ref.shape[0] // pieces
    moves = [
        pltpu.make_async_copy(
            src_ref.at[pl.ds(k * step, step)], o_ref.at[pl.ds(k * step, step)], sem.at[k]
        )
        for k in range(pieces)
    ]
    for move in moves:
        move.start()
    for move in moves:
        move.wait()


def fetch(weight, after):
    src = pltpu.with_memory_space_constraint(weight, pltpu.HBM)
    hbm = pl.BlockSpec(memory_space=pl.ANY)
    pieces = 8
    return pl.pallas_call(
        functools.partial(fetch_kernel, len(after), pieces),
        in_specs=[hbm] * (1 + len(after)),
        out_specs=pl.BlockSpec(memory_space=pltpu.VMEM),
        out_shape=pltpu.VMEM(weight.shape, weight.dtype),
        scratch_shapes=[pltpu.SemaphoreType.DMA((pieces,))],
        cost_estimate=cost(0, 2 * weight.size),
        compiler_params=pltpu.CompilerParams(vmem_limit_bytes=1 * MIB),
    )(src, *after)


def half_of(where_ref, flip, length):
    return pl.ds(pl.multiple_of((where_ref[1] ^ flip) * length, 128), length)


def product_kernel(flip, where_ref, *refs):
    block_refs, (w_ref, o_ref, x_buf) = refs[:-3], refs[-3:]
    count = block_refs[0].shape[0]
    for k, block_ref in enumerate(block_refs):
        at = pl.multiple_of((where_ref[0] ^ k) * count, count)
        x_buf[pl.ds(at, count), :] = block_ref[...]
    cols = half_of(where_ref, flip, o_ref.shape[1])
    o_ref[...] = jnp.dot(x_buf[...], w_ref[:, cols], preferred_element_type=F32).astype(BF16)


def product(where, blocks, w, flip):
    wide = w.shape[1] // 2
    count, deep = blocks[0].shape
    rows = count * len(blocks)
    vmem = pl.BlockSpec(memory_space=pltpu.VMEM)
    return pl.pallas_call(
        functools.partial(product_kernel, flip),
        in_specs=[pl.BlockSpec(memory_space=pltpu.SMEM)] + [vmem] * (len(blocks) + 1),
        out_specs=vmem,
        out_shape=jax.ShapeDtypeStruct((rows, wide), BF16),
        scratch_shapes=[pltpu.VMEM((rows, deep), BF16)],
        cost_estimate=cost(2 * rows * deep * wide, 2 * deep * wide),
        compiler_params=pltpu.CompilerParams(vmem_limit_bytes=4 * MIB),
    )(where, *blocks, w)


def middle_kernel(flip, where_ref, attn_ref, res_ref, gain_ref, *o_refs):
    mid_ref, normed_ref, sq_ref = o_refs
    steps, seqs, _ = res_ref.shape
    rows, wide = mid_ref.shape
    count = rows // (steps * 4)
    cols = half_of(where_ref, flip, wide)
    parts = []
    for d in range(4):
        for s in range(steps):
            parts.append(res_ref[s, d * count : (d + 1) * count, cols].astype(F32))
    mid = (jnp.concatenate(parts, axis=0) + attn_ref[...].astype(F32)).astype(BF16)
    whole = mid.astype(F32)
    mid_ref[...] = mid
    normed_ref[...] = (whole * gain_ref[:1, cols].astype(F32)).astype(BF16)
    sq_ref[...] = jnp.broadcast_to(jnp.sum(whole * whole, axis=1, keepdims=True), sq_ref.shape)


def middle_part(where, flip, attn, residual, gain):
    rows, wide = attn.shape
    vmem = pl.BlockSpec(memory_space=pltpu.VMEM)
    return pl.pallas_call(
        functools.partial(middle_kernel, flip),
        in_specs=[pl.BlockSpec(memory_space=pltpu.SMEM)] + [vmem] * 3,
        out_specs=[vmem] * 3,
        out_shape=[
            jax.ShapeDtypeStruct((rows, wide), BF16),
            jax.ShapeDtypeStruct((rows, wide), BF16),
            jax.ShapeDtypeStruct((rows, 128), F32),
        ],
        cost_estimate=cost(8 * rows * wide, 8 * rows * wide),
        compiler_params=pltpu.CompilerParams(vmem_limit_bytes=6 * MIB),
    )(where, attn, residual, gain)


def first_kernel(wide, where_ref, x_ref, g_ref, u_ref, o_ref):
    deep = half_of(where_ref, 0, x_ref.shape[1])
    length = g_ref.shape[1]
    for k, w_ref in enumerate((g_ref, u_ref)):
        for at in range(0, length, wide):
            here = slice(at, at + wide)
            out = jnp.dot(x_ref[...], w_ref[deep, here], preferred_element_type=F32)
            o_ref[:, k * length + at : k * length + at + wide] = out


def gate_up_first(where, x, weights):
    rows, deep = x.shape
    length = weights[0].shape[1]
    vmem = pl.BlockSpec(memory_space=pltpu.VMEM)
    return pl.pallas_call(
        functools.partial(first_kernel, length // 7),
        in_specs=[pl.BlockSpec(memory_space=pltpu.SMEM)] + [vmem] * 3,
        out_specs=vmem,
        out_shape=jax.ShapeDtypeStruct((rows, 2 * length), F32),
        cost_estimate=cost(4 * rows * deep * length, 4 * deep * length),
        compiler_params=pltpu.CompilerParams(vmem_limit_bytes=4 * MIB),
    )(where, x, *weights)


def second_kernel(chip, groups, where_ref, x_ref, f_ref, g_ref, u_ref, *refs):
    give_refs, (keep_ref, buf) = refs[:groups], refs[groups:]
    me = where_ref[0]
    deep = half_of(where_ref, 1, x_ref.shape[1])
    length = g_ref.shape[1]
    own = length // 4
    rows = give_refs[0].shape[0]
    start = pl.multiple_of(((me // 2) ^ chip) * (2 * own), 128)
    for k, w_ref in enumerate((g_ref, u_ref)):
        out = jnp.dot(x_ref[...], w_ref[deep, pl.ds(start, 2 * own)], preferred_element_type=F32)
        buf[...] = out + f_ref[:, pl.ds(pl.multiple_of(k * length + start, 128), 2 * own)]
        mine = pl.ds(pl.multiple_of((me % 2) * own, 128), own)
        other = pl.ds(pl.multiple_of((1 - me % 2) * own, 128), own)
        here = slice(k * own, (k + 1) * own)
        keep_ref[:, here] = buf[:, mine]
        for n, give_ref in enumerate(give_refs):
            give_ref[:, here] = buf[n * rows : (n + 1) * rows, other].astype(BF16)


def gate_up_second(where, x, first, weights, chip, groups):
    rows, deep = x.shape
    length = weights[0].shape[1]
    own = length // 4
    vmem = pl.BlockSpec(memory_space=pltpu.VMEM)
    *give, keep = pl.pallas_call(
        functools.partial(second_kernel, chip, groups),
        in_specs=[pl.BlockSpec(memory_space=pltpu.SMEM)] + [vmem] * 4,
        out_specs=[vmem] * (groups + 1),
        out_shape=[jax.ShapeDtypeStruct((rows // groups, 2 * own), BF16)] * groups
        + [jax.ShapeDtypeStruct((rows, 2 * own), F32)],
        scratch_shapes=[pltpu.VMEM((rows, 2 * own), F32)],
        cost_estimate=cost(4 * rows * deep * 2 * own, 8 * deep * own),
        compiler_params=pltpu.CompilerParams(vmem_limit_bytes=6 * MIB),
    )(where, x, first, *weights)
    return give, keep


def relay_kernel(n, keep_ref, got_ref, o_ref):
    rows = got_ref.shape[0]
    here = slice(n * rows, (n + 1) * rows)
    o_ref[...] = (keep_ref[here, :] + got_ref[...].astype(F32)).astype(BF16)


def relay(n, keep, got):
    vmem = pl.BlockSpec(memory_space=pltpu.VMEM)
    return pl.pallas_call(
        functools.partial(relay_kernel, n),
        in_specs=[vmem] * 2,
        out_specs=vmem,
        out_shape=jax.ShapeDtypeStruct(got.shape, BF16),
        cost_estimate=cost(got.size, 4 * got.size),
        compiler_params=pltpu.CompilerParams(vmem_limit_bytes=2 * MIB),
    )(keep, got)


def act_kernel(n, full, near_ref, got_ref, far_ref, *refs):
    sq_refs, o_ref = refs[:-1], refs[-1]
    rows, cols = o_ref.shape
    total = functools.reduce(jnp.add, [sq[n * rows : (n + 1) * rows, :1] for sq in sq_refs])
    inv_norm = lax.rsqrt(total / full + 1e-05)
    here = slice(n * rows, (n + 1) * rows)
    both = near_ref[here, :] + got_ref[...].astype(F32) + far_ref[...].astype(F32)
    gate = both[:, :cols] * inv_norm
    up = both[:, cols:] * inv_norm
    o_ref[...] = (gate / (1.0 + jnp.exp(-gate)) * up).astype(BF16)


def act(n, near, got, far, squares, full):
    rows, both = far.shape
    vmem = pl.BlockSpec(memory_space=pltpu.VMEM)
    return pl.pallas_call(
        functools.partial(act_kernel, n, full),
        in_specs=[vmem] * (3 + len(squares)),
        out_specs=vmem,
        out_shape=jax.ShapeDtypeStruct((rows, both // 2), BF16),
        cost_estimate=cost(8 * rows * both, 8 * rows * both),
        compiler_params=pltpu.CompilerParams(vmem_limit_bytes=4 * MIB),
    )(near, got, far, *squares)


def final_kernel(groups, where_ref, *refs):
    mid_refs, ffn_refs, o_ref = refs[:2], refs[2:-1], refs[-1]
    steps = o_ref.shape[0]
    wide = mid_refs[0].shape[1]
    rows = ffn_refs[0].shape[0]
    count = rows * groups // (steps * 4)
    for flip in range(2):
        cols = half_of(where_ref, flip, wide)
        for n in range(groups):
            here = slice(n * rows, (n + 1) * rows)
            ffn = ffn_refs[2 * n + flip][...].astype(F32)
            out = (mid_refs[flip][here, :].astype(F32) + ffn).astype(BF16)
            for k in range(rows // count):
                d, s = divmod(n * (rows // count) + k, steps)
                o_ref[s, d * count : (d + 1) * count, cols] = out[k * count : (k + 1) * count]


def final(where, mids, groups, shape):
    vmem = pl.BlockSpec(memory_space=pltpu.VMEM)
    flat = [*mids, *(x for group in groups for x in group)]
    return pl.pallas_call(
        functools.partial(final_kernel, len(groups)),
        in_specs=[pl.BlockSpec(memory_space=pltpu.SMEM)] + [vmem] * len(flat),
        out_specs=vmem,
        out_shape=jax.ShapeDtypeStruct(shape, BF16),
        cost_estimate=cost(2 * shape[1] * shape[2], 8 * shape[1] * shape[2]),
        compiler_params=pltpu.CompilerParams(vmem_limit_bytes=12 * MIB),
    )(where, *flat)


def down_kernel(chip, flip, has_sum, where_ref, mine_ref, other_ref, w_ref, *refs):
    o_ref, buf = refs[-2:]
    own = mine_ref.shape[1]
    me = where_ref[0]
    buf[:, pl.ds(pl.multiple_of((me % 2) * own, 128), own)] = mine_ref[...]
    buf[:, pl.ds(pl.multiple_of((1 - me % 2) * own, 128), own)] = other_ref[...]
    at = pl.ds(pl.multiple_of(((me // 2) ^ chip) * (2 * own), 128), 2 * own)
    cols = slice(None) if flip is None else half_of(where_ref, flip, o_ref.shape[1])
    total = jnp.dot(buf[...], w_ref[at, cols], preferred_element_type=F32)
    if has_sum:
        total = total + refs[0][:, cols]
    o_ref[...] = total.astype(o_ref.dtype)


def down(where, mine, other, chip, weight, flip=None, total=None, dtype=F32):
    rows, own = mine.shape
    wide = weight.shape[1] // (1 if flip is None else 2)
    vmem = pl.BlockSpec(memory_space=pltpu.VMEM)
    args = [where, mine, other, weight] + ([] if total is None else [total])
    return pl.pallas_call(
        functools.partial(down_kernel, chip, flip, total is not None),
        in_specs=[pl.BlockSpec(memory_space=pltpu.SMEM)] + [vmem] * (len(args) - 1),
        out_specs=vmem,
        out_shape=jax.ShapeDtypeStruct((rows, wide), dtype),
        scratch_shapes=[pltpu.VMEM((rows, 2 * own), BF16)],
        cost_estimate=cost(4 * rows * own * wide, 4 * own * wide),
        compiler_params=pltpu.CompilerParams(vmem_limit_bytes=4 * MIB),
    )(*args)


def pairs(size, step):
    return [(i, i ^ step) for i in range(size)]


def in_order(mine, other, bit, axis=0):
    first = jnp.where(bit == 0, mine, other)
    second = jnp.where(bit == 0, other, mine)
    return jnp.concatenate((first, second), axis=axis)


def levels(size):
    return [1 << k for k in range(size.bit_length() - 1)]


def sum_tensor(send, keep, during=None):
    held = total_of(keep, lax.ppermute(send, "tensor", pairs(4, 1)))
    got = lax.ppermute(held, "tensor", pairs(4, 2))
    beside = None if during is None else during(held)
    if beside is not None:
        got, beside = lax.optimization_barrier((got, beside))
    return total_of(held, got), beside


def gather_rows(block, size):
    me = lax.axis_index("dp")
    count, deep = block.shape
    for step in reversed(levels(size)):
        bit = (me // step) % 2
        block = in_order(block, lax.ppermute(block, "dp", pairs(size, step)), bit)
    block = block.reshape(size, count, deep)
    order = []
    for d in range(size):
        place = 0
        for step in levels(size):
            place = place * 2 + (d // step) % 2
        order.append(block[place])
    return jnp.concatenate(order, axis=0)


def sum_dp(value, size):
    for step in levels(size):
        value = value + lax.ppermute(value, "dp", pairs(size, step))
    return value


def activate(both, inv_norm):
    cols = both.shape[1] // 2
    gate = both[:, :cols] * inv_norm
    up = both[:, cols:] * inv_norm
    return (jax.nn.silu(gate) * up).astype(BF16)


def middle(resid, attn, norm_gain, dp):
    mid = add(resid, attn)
    wide = mid.astype(F32)
    squares = sum_dp(jnp.sum(wide * wide, axis=1)[None, :], dp)
    inv_norm = lax.rsqrt(squares / (mid.shape[1] * dp) + 1e-05).reshape(mid.shape[0], 1)
    normed = (wide * norm_gain.astype(F32)[None, :]).astype(BF16)
    return mid, inv_norm, normed


def plain(rows, resid, out_weight, norm_gain, gate_weight, up_weight, down_weight, dp):
    part = jnp.dot(rows, out_weight, preferred_element_type=F32).astype(BF16)
    mid, inv_norm, normed = middle(resid, lax.psum(part, "tensor"), norm_gain, dp)
    both = []
    for weight in (gate_weight, up_weight):
        term = jnp.dot(normed, weight, preferred_element_type=F32).astype(BF16)
        both.append(lax.psum_scatter(term, "dp", scatter_dimension=1, tiled=True).astype(F32))
    hidden = activate(jnp.concatenate(both, axis=1), inv_norm)
    hidden = lax.all_gather(hidden, "dp", axis=1, tiled=True)
    part = jnp.dot(hidden, down_weight, preferred_element_type=F32).astype(BF16)
    return add(mid, lax.psum(part, "tensor"))


def body(
    residual,
    queries,
    new_keys,
    new_values,
    key_cache,
    value_cache,
    lengths,
    out_weight,
    norm_gain,
    gate_weight,
    up_weight,
    down_weight,
):
    dp = lax.axis_size("dp")
    tensor = lax.axis_size("tensor")
    steps, all_seqs, width = residual.shape
    local_seqs = queries.shape[1]
    where = jnp.stack([lax.axis_index("dp"), lax.axis_index("tensor") % 2])
    where, lengths = lax.optimization_barrier((where, lengths))
    heads, out_w = attention(
        queries, new_keys, new_values, key_cache, value_cache, lengths, out_weight
    )
    if dp == 4 and tensor == 4:
        weights = gate_weight, up_weight, down_weight
        gain, heads = lax.optimization_barrier((norm_gain, heads))
        return fast(where, heads, residual, gain, out_w, *weights)
    row_count = steps * all_seqs
    resid = residual.reshape(steps, dp, local_seqs, width).swapaxes(0, 1)
    weights = out_w, norm_gain, gate_weight, up_weight, down_weight
    out = plain(gather_rows(heads, dp), resid.reshape(row_count, width), *weights, dp)
    return out.reshape(dp, steps, local_seqs, width).swapaxes(0, 1).reshape(residual.shape)


def fast(where, heads, residual, gain, out_w, gate_weight, up_weight, down_weight):
    width = out_w.shape[1]
    groups = 2
    core = lambda value: lax.ppermute(value, "dp", pairs(4, 1))
    across = lambda value: lax.ppermute(value, "dp", pairs(4, 2))
    swap = lambda value: lax.ppermute(value, "tensor", pairs(4, 1))
    gain = jnp.broadcast_to(gain[None, :], (16, width))
    far = across(heads)
    blocks = [heads, core(heads), far, core(far)]
    blocks, gain = lax.optimization_barrier((blocks, gain))
    send = product(where, blocks, out_w, 1)
    keep = product(where, blocks, out_w, 0)
    gate_w = fetch(gate_weight, [keep])
    got = swap(send)
    got, gate_w = lax.optimization_barrier((got, gate_w))
    held = total_of(keep, got)
    got = lax.ppermute(held, "tensor", pairs(4, 2))
    up_w = fetch(up_weight, [held])
    got, up_w = lax.optimization_barrier((got, up_w))
    held = total_of(held, got)
    other = swap(held)
    weights = gate_w, up_w
    mid, normed, sq = middle_part(where, 0, held, residual, gain)
    first = gate_up_first(where, normed, weights)
    other, first = lax.optimization_barrier((other, first))
    mid_other, normed, sq_other = middle_part(where, 1, other, residual, gain)
    sq = total_of(sq, sq_other, dtype=F32)
    sq_far = across(sq)
    normed, sq_core = lax.optimization_barrier((normed, core(sq)))
    give, keep = gate_up_second(where, normed, first, weights, 1, groups)
    far = [core(x) for x in give]
    far, sq_far = lax.optimization_barrier((far, sq_far))
    squares = [sq, sq_core, sq_far, core(sq_far)]
    relayed = [relay(n, keep, x) for n, x in enumerate(far)]
    far = [across(x) for x in relayed]
    normed, relayed = lax.optimization_barrier((normed, relayed))
    give, near = gate_up_second(where, normed, first, weights, 0, groups)
    got = [core(x) for x in give]
    down_w = fetch(down_weight, [near])
    far[0], down_w = lax.optimization_barrier((far[0], down_w))
    mine, mine_far, other, totals, outs = [], [], [], [], []
    for n in range(groups):
        if n:
            far[n], totals[0] = lax.optimization_barrier((far[n], totals[0]))
        mine.append(act(n, near, got[n], far[n], squares, width * 4))
        mine_far.append(across(mine[n]))
        other.append(core(mine[n]))
        totals.append(down(where, mine[n], other[n], 0, down_w))
    for n in range(groups):
        last = lambda flip: down(
            where, mine_far[n], other_far, 1, down_w, flip, totals[n], BF16
        )
        if n:
            mine_far[n], send = lax.optimization_barrier((mine_far[n], send))
        other_far = core(mine_far[n])
        send = last(1)
        keep = last(0)
        held, _ = sum_tensor(send, keep)
        outs.append((held, swap(held)))
    return final(where, [mid, mid_other], outs, residual.shape)


def solution(mesh):
    in_specs = (
        P(None, "replica", "dp"),
        P(None, ("replica", "dp"), "tensor"),
        P(None, ("replica", "dp"), "tensor", None),
        P(None, ("replica", "dp"), "tensor", None),
        P(("replica", "dp"), "tensor", None, None),
        P(("replica", "dp"), "tensor", None, None),
        P(("replica", "dp")),
        P("tensor", "dp"),
        P("dp"),
        P("dp", "tensor"),
        P("dp", "tensor"),
        P("tensor", "dp"),
    )
    out_specs = P(None, "replica", "dp")
    return jax.shard_map(body, mesh=mesh, in_specs=in_specs, out_specs=out_specs, check_vma=False)
```

time: 187 us -> 112 us (0.60)
  waiting for transfers between devices: 102 us -> 40.8 us
  Pallas kernels: 0 us -> 46.1 us
  matrix products: 37.5 us -> 0 us
  starting transfers between devices: 0.09 us -> 23.8 us
  blocking collectives: 23.6 us -> 0 us
  between operations: 13.3 us -> 0.29 us
  other arithmetic: 5.37 us -> 0.07 us
  local copies, waits for them, and re-layouts: 4.68 us -> 0.67 us
    psum x2 -> x0, waiting for transfers between devices: 78.1 us -> none  [the longest x1 39.2 us: body(): attn = lax.psum(partials.astype(jnp.bfloat16), 'tensor')]
    pallas_call x0 -> x29, Pallas kernels: none -> 46.1 us  [the longest x3 15.9 us: fetch(): pl.pallas_call(functools.partial(fetch_kernel, len(after), pieces), in_sp...]
    ppermute x0 -> x27, waiting for transfers between devices: none -> 40.8 us  [the longest x6 12.4 us: fast(): across = lambda value: lax.ppermute(value, 'dp', pairs(4, 2))]
    dot_general x8 -> x0, matrix products: 37.5 us -> none  [the longest x1 8.38 us: body(): lax.dot_general(lax.all_gather(hidden, 'dp', axis=0, tiled=True), down_we...]
    unnamed x4 -> x0, waiting for transfers between devices: 24 us -> none
    ppermute x0 -> x27, starting transfers between devices: none -> 23.8 us  [the longest x6 10.1 us: fast(): across = lambda value: lax.ppermute(value, 'dp', pairs(4, 2))]
    all_gather x2 -> x0, blocking collectives: 17.7 us -> none  [the longest x1 9.1 us: body(): lax.all_gather(hidden, 'dp', axis=0, tiled=True)]
    psum x1 -> x0, blocking collectives: 5.87 us -> none  [body(): squares = lax.psum(jnp.sum(mid_wide * mid_wide, axis=2), 'dp')]
  transfers between devices with their start and end apart: 3 -> 27, of which waited for: 3 -> 13; matrix products, arithmetic and copies ran while one was open for 0% -> 0% of each run, Pallas kernels for 0% -> 29%
where the time goes in v2:
time: 112 us
  Pallas kernels  46.1 us (41%)
  waiting for transfers between devices  40.8 us (36%)
  starting transfers between devices  23.8 us (21%)
    pallas_call x3, Pallas kernels, fetch(): pl.pallas_call(functools.partial(fetch_kernel, len(after), pieces), in_sp...  15.9 us
    ppermute x6, waiting for transfers between devices, fast(): across = lambda value: lax.ppermute(value, 'dp', pairs(4, 2))  12.4 us
    ppermute x6, starting transfers between devices, fast(): across = lambda value: lax.ppermute(value, 'dp', pairs(4, 2))  10.1 us
    ppermute x2, waiting for transfers between devices, sum_tensor(): got = lax.ppermute(held, 'tensor', pairs(4, 2))  9.7 us
    ppermute x4, waiting for transfers between devices, fast(): swap = lambda value: lax.ppermute(value, 'tensor', pairs(4, 1))  9.54 us
    pallas_call x6, Pallas kernels, down(): pl.pallas_call(functools.partial(down_kernel, chip, flip, total is not No...  9.14 us
    pallas_call x1, Pallas kernels, attention(): pl.pallas_call(functools.partial(attention_kernel, first, count), in_spec...  7.87 us
    ppermute x1, waiting for transfers between devices, fast(): got = lax.ppermute(held, 'tensor', pairs(4, 2))  6.56 us
  transfers between devices with their start and end apart: 27, of which 13 were waited for; matrix products, arithmetic and copies ran while one was open for 0% of the time, Pallas kernels for 29%

profile of v2, /device:TPU:0, one launch (start us, length us, event | category | flops | bytes accessed | tf_op | source)
XLA Modules:
  0.0 111.7 jit_solution(14768738147877165919)
XLA Ops:
  0.0 0.1 pad_add_fusion.where_ref
  0.1 0.7 copy-done.1
  0.7 7.9 %shard_map.118 = (bf16[32,2048]{1,0:T(8,128)(2,1)S(1)}, bf16[2048,2048]{1,0:T(8,128)(2,1)S(1)}) custom-call(s32[16]{0:T(128)S(1)} %copy-done.1, bf16[2,16,2048]{2,1,0:T(8,128)(2,1)} %q_hbm.1, bf16[16,2,1024,128]{3,2,1,0:T(8,128)(2,1)} %k_hbm.1, bf16[16,2,1024,128]{3,2,1,0:T(8,128)(2,1)} %v_hbm.1, bf16[2,16,2,128]{3,2,1,0:T(2,128)(2,1)} %nk_hbm.1, ...), custom_call_target="tpu_custom_call" | custom-call | flops 268435456 | bytes 16777216 | tf_op jit(solution)/shard_map/pallas_call | solution.py:151
  8.6 2.8 %collective-permute-start.1 = (bf16[32,2048]{1,0:T(8,128)(2,1)S(1)}, bf16[32,2048]{1,0:T(8,128)(2,1)S(1)}, u32[]{:S(2)}, u32[]{:S(2)}) collective-permute-start(bf16[32,2048]{1,0:T(8,128)(2,1)S(1)} %get-tuple-element.50.refs_0_), channel_id=1, source_target_pairs={{0,2},{1,3},{2,0},{3,1},{4,6},{5,7},{6,4},{7,5},{8,10},{9,11},{10,... | collective-permute-start | bytes 393224 | tf_op jit(solution)/shard_map/ppermute | solution.py:545
  11.4 0.0 collective-permute-start
  11.4 3.9 %collective-permute-done.1.refs_2_ = bf16[32,2048]{1,0:T(8,128)(2,1)S(1)} collective-permute-done((bf16[32,2048]{1,0:T(8,128)(2,1)S(1)}, bf16[32,2048]{1,0:T(8,128)(2,1)S(1)}, u32[]{:S(2)}, u32[]{:S(2)}) %collective-permute-start.1) | collective-permute-done | bytes 131104 | tf_op jit(solution)/shard_map/ppermute | solution.py:545
  15.3 0.0 collective-permute-start.2
  15.3 0.0 collective-permute-done.refs_1_
  15.3 1.3 %collective-permute-done.2.refs_3_ = bf16[32,2048]{1,0:T(8,128)(2,1)S(1)} collective-permute-done((bf16[32,2048]{1,0:T(8,128)(2,1)S(1)}, bf16[32,2048]{1,0:T(8,128)(2,1)S(1)}, u32[]{:S(2)}, u32[]{:S(2)}) %collective-permute-start.2) | collective-permute-done | bytes 131104 | tf_op jit(solution)/shard_map/ppermute | solution.py:544
  16.7 1.3 %shard_map.120 = bf16[128,1024]{1,0:T(8,128)(2,1)S(1)} custom-call(s32[2]{0:T(128)S(1)} %pad_add_fusion.where_ref, bf16[32,2048]{1,0:T(8,128)(2,1)S(1)} %get-tuple-element.50.refs_0_, bf16[32,2048]{1,0:T(8,128)(2,1)S(1)} %collective-permute-done.refs_1_, bf16[32,2048]{1,0:T(8,128)(2,1)S(1)} %collective-permute-done.1.refs_2_, ...), custom_call_target="tpu_custom_call" | custom-call | flops 536870912 | bytes 4194304 | tf_op jit(solution)/shard_map/pallas_call | solution.py:224
  18.0 1.6 %collective-permute-start.3 = (bf16[128,1024]{1,0:T(8,128)(2,1)S(1)}, bf16[128,1024]{1,0:T(8,128)(2,1)S(1)}, u32[]{:S(2)}, u32[]{:S(2)}) collective-permute-start(bf16[128,1024]{1,0:T(8,128)(2,1)S(1)} %shard_map.120), channel_id=1, source_target_pairs={{0,4},{4,0},{8,12},{12,8},{1,5},{5,1},{9,13},{13,9},{2,6},{6,2},{1... | collective-permute-start | bytes 786440 | tf_op jit(solution)/shard_map/ppermute | solution.py:546
  19.6 1.3 %shard_map.119.refs_0_ = bf16[128,1024]{1,0:T(8,128)(2,1)S(1)} custom-call(s32[2]{0:T(128)S(1)} %pad_add_fusion.where_ref, bf16[32,2048]{1,0:T(8,128)(2,1)S(1)} %get-tuple-element.50.refs_0_, bf16[32,2048]{1,0:T(8,128)(2,1)S(1)} %collective-permute-done.refs_1_, bf16[32,2048]{1,0:T(8,128)(2,1)S(1)} %collective-permute-done.1.refs_2_, ...), custom_call_target="tpu_custom_call" | custom-call | flops 536870912 | bytes 4194304 | tf_op jit(solution)/shard_map/pallas_call | solution.py:224
  21.0 5.3 %shard_map.121.g_ref = bf16[2048,3584]{1,0:T(8,128)(2,1)S(1)} custom-call(bf16[2048,3584]{1,0:T(8,128)(2,1)} %src_ref.3, bf16[128,1024]{1,0:T(8,128)(2,1)S(1)} %shard_map.119.refs_0_), custom_call_target="tpu_custom_call" | custom-call | bytes 14680064 | tf_op jit(solution)/shard_map/pallas_call | solution.py:194
  26.3 0.1 collective-permute-done.3.refs_1_
  26.4 0.1 shard_map.122.refs_0_
  26.5 0.0 copy-start
  26.5 2.7 %collective-permute-start.4 = (bf16[128,1024]{1,0:T(8,128)(2,1)S(1)}, bf16[128,1024]{1,0:T(8,128)(2,1)S(1)}, u32[]{:S(2)}, u32[]{:S(2)}) collective-permute-start(bf16[128,1024]{1,0:T(8,128)(2,1)S(1)} %shard_map.122.refs_0_), channel_id=1, source_target_pairs={{0,8},{4,12},{8,0},{12,4},{1,9},{5,13},{9,1},{13,5},{2,10},{6,14},... | collective-permute-start | bytes 786440 | tf_op jit(solution)/shard_map/ppermute | solution.py:557
  29.2 5.3 %shard_map.123.u_ref = bf16[2048,3584]{1,0:T(8,128)(2,1)S(1)} custom-call(bf16[2048,3584]{1,0:T(8,128)(2,1)} %src_ref.4, bf16[128,1024]{1,0:T(8,128)(2,1)S(1)} %shard_map.122.refs_0_), custom_call_target="tpu_custom_call" | custom-call | bytes 14680064 | tf_op jit(solution)/shard_map/pallas_call | solution.py:194
  34.5 6.6 %collective-permute-done.4.refs_1_ = bf16[128,1024]{1,0:T(8,128)(2,1)S(1)} collective-permute-done((bf16[128,1024]{1,0:T(8,128)(2,1)S(1)}, bf16[128,1024]{1,0:T(8,128)(2,1)S(1)}, u32[]{:S(2)}, u32[]{:S(2)}) %collective-permute-start.4) | collective-permute-done | bytes 262176 | tf_op jit(solution)/shard_map/ppermute | solution.py:557
  41.0 0.1 shard_map.124.attn_ref
  41.1 0.4 collective-permute-start.5
  41.5 0.7 shard_map.125
  42.3 2.6 %shard_map.126.f_ref = f32[128,7168]{1,0:T(8,128)S(1)} custom-call(s32[2]{0:T(128)S(1)} %pad_add_fusion.where_ref, bf16[128,1024]{1,0:T(8,128)(2,1)S(1)} %get-tuple-element.59.x_ref, bf16[2048,3584]{1,0:T(8,128)(2,1)S(1)} %shard_map.121.g_ref, bf16[2048,3584]{1,0:T(8,128)(2,1)S(1)} %shard_map.123.u_ref), custom_call_target="tpu_custom_call" | custom-call | flops 1879048192 | bytes 14680064 | tf_op jit(solution)/shard_map/pallas_call | solution.py:283
  44.9 3.8 %collective-permute-done.5.attn_ref = bf16[128,1024]{1,0:T(8,128)(2,1)S(1)} collective-permute-done((bf16[128,1024]{1,0:T(8,128)(2,1)S(1)}, bf16[128,1024]{1,0:T(8,128)(2,1)S(1)}, u32[]{:S(2)}, u32[]{:S(2)}) %collective-permute-start.5) | collective-permute-done | bytes 262176 | tf_op jit(solution)/shard_map/ppermute | solution.py:546
  48.8 0.8 shard_map.127
  49.5 0.1 collective-permute-start.6
  49.6 1.2 %collective-permute-done.6.refs_1_ = f32[128,128]{1,0:T(8,128)S(1)} collective-permute-done((f32[128,128]{1,0:T(8,128)S(1)}, f32[128,128]{1,0:T(8,128)S(1)}, u32[]{:S(2)}, u32[]{:S(2)}) %collective-permute-start.6) | collective-permute-done | bytes 65568 | tf_op jit(solution)/shard_map/ppermute | solution.py:544
  50.8 2.1 %shard_map.129 = (bf16[64,1792]{1,0:T(8,128)(2,1)S(1)}, bf16[64,1792]{1,0:T(8,128)(2,1)S(1)}, f32[128,1792]{1,0:T(8,128)S(1)}) custom-call(s32[2]{0:T(128)S(1)} %pad_add_fusion.where_ref, bf16[128,1024]{1,0:T(8,128)(2,1)S(1)} %get-tuple-element.74.x_ref, f32[128,7168]{1,0:T(8,128)S(1)} %shard_map.126.f_ref, bf16[2048,3584]{1,0:T(8,128)(2,1)S(1)} %shard_map.121.g_ref, ...), custom_call_target="tpu_custom_call" | custom-call | flops 939524096 | bytes 7340032 | tf_op jit(solution)/shard_map/pallas_call | solution.py:317
  52.9 0.2 collective-permute-start.7
  53.1 0.4 collective-permute-start.8
  53.5 1.7 %collective-permute-start.9 = (f32[128,128]{1,0:T(8,128)S(1)}, f32[128,128]{1,0:T(8,128)S(1)}, u32[]{:S(2)}, u32[]{:S(2)}) collective-permute-start(f32[128,128]{1,0:T(8,128)S(1)} %shard_map.128.refs_0_), channel_id=1, source_target_pairs={{0,2},{1,3},{2,0},{3,1},{4,6},{5,7},{6,4},{7,5},{8,10},{9,11},{10,... | collective-permute-start | bytes 196616 | tf_op jit(solution)/shard_map/ppermute | solution.py:545
  55.2 2.6 %collective-permute-done.9.refs_2_ = f32[128,128]{1,0:T(8,128)S(1)} collective-permute-done((f32[128,128]{1,0:T(8,128)S(1)}, f32[128,128]{1,0:T(8,128)S(1)}, u32[]{:S(2)}, u32[]{:S(2)}) %collective-permute-start.9) | collective-permute-done | bytes 65568 | tf_op jit(solution)/shard_map/ppermute | solution.py:545
  57.7 0.0 collective-permute-done.7.got_ref
  57.8 1.8 %collective-permute-start.11 = (bf16[64,1792]{1,0:T(8,128)(2,1)S(1)}, bf16[64,1792]{1,0:T(8,128)(2,1)S(1)}, u32[]{:S(2)}, u32[]{:S(2)}) collective-permute-start(bf16[64,1792]{1,0:T(8,128)(2,1)S(1)} %shard_map.130), channel_id=1, source_target_pairs={{0,2},{1,3},{2,0},{3,1},{4,6},{5,7},{6,4},{7,5},{8,10},{9,11},{10,... | collective-permute-start | bytes 688136 | tf_op jit(solution)/shard_map/ppermute | solution.py:545
  59.6 2.0 %shard_map.132 = (bf16[64,1792]{1,0:T(8,128)(2,1)S(1)}, bf16[64,1792]{1,0:T(8,128)(2,1)S(1)}, f32[128,1792]{1,0:T(8,128)S(1)}) custom-call(s32[2]{0:T(128)S(1)} %pad_add_fusion.where_ref, bf16[128,1024]{1,0:T(8,128)(2,1)S(1)} %get-tuple-element.74.x_ref, f32[128,7168]{1,0:T(8,128)S(1)} %shard_map.126.f_ref, bf16[2048,3584]{1,0:T(8,128)(2,1)S(1)} %shard_map.121.g_ref, ...), custom_call_target="tpu_custom_call" | custom-call | flops 939524096 | bytes 7340032 | tf_op jit(solution)/shard_map/pallas_call | solution.py:317
  61.6 0.1 collective-permute-start.10
  61.7 0.4 collective-permute-start.15
  62.1 0.2 collective-permute-start.20
  62.3 0.3 collective-permute-start.12
  62.6 5.3 %shard_map.133.w_ref = bf16[3584,2048]{1,0:T(8,128)(2,1)S(1)} custom-call(bf16[3584,2048]{1,0:T(8,128)(2,1)} %src_ref.5, f32[128,1792]{1,0:T(8,128)S(1)} %get-tuple-element.75.refs_0_.near_ref), custom_call_target="tpu_custom_call" | custom-call | bytes 14680064 | tf_op jit(solution)/shard_map/pallas_call | solution.py:194
  68.0 0.2 shard_map.134.mine_ref
  68.2 1.7 %collective-permute-start.13 = (bf16[64,896]{1,0:T(8,128)(2,1)S(1)}, bf16[64,896]{1,0:T(8,128)(2,1)S(1)}, u32[]{:S(2)}, u32[]{:S(2)}) collective-permute-start(bf16[64,896]{1,0:T(8,128)(2,1)S(1)} %shard_map.134.mine_ref), channel_id=1, source_target_pairs={{0,2},{1,3},{2,0},{3,1},{4,6},{5,7},{6,4},{7,5},{8,10},{9,11},{10,... | collective-permute-start | bytes 344072 | tf_op jit(solution)/shard_map/ppermute | solution.py:545
  69.9 3.6 %collective-permute-done.13.mine_ref = bf16[64,896]{1,0:T(8,128)(2,1)S(1)} collective-permute-done((bf16[64,896]{1,0:T(8,128)(2,1)S(1)}, bf16[64,896]{1,0:T(8,128)(2,1)S(1)}, u32[]{:S(2)}, u32[]{:S(2)}) %collective-permute-start.13) | collective-permute-done | bytes 114720 | tf_op jit(solution)/shard_map/ppermute | solution.py:545
  73.5 1.9 %shard_map.135.refs_0_ = f32[64,2048]{1,0:T(8,128)S(1)} custom-call(s32[2]{0:T(128)S(1)} %pad_add_fusion.where_ref, bf16[64,896]{1,0:T(8,128)(2,1)S(1)} %shard_map.134.mine_ref, bf16[64,896]{1,0:T(8,128)(2,1)S(1)} %collective-permute-done.16.other_ref, bf16[3584,2048]{1,0:T(8,128)(2,1)S(1)} %shard_map.133.w_ref), custom_call_target="tpu_custom_call" | custom-call | flops 469762048 | bytes 7340032 | tf_op jit(solution)/shard_map/pallas_call | solution.py:422
  75.4 0.4 shard_map.140.mine_ref
  75.8 1.7 %collective-permute-start.21 = (bf16[64,896]{1,0:T(8,128)(2,1)S(1)}, bf16[64,896]{1,0:T(8,128)(2,1)S(1)}, u32[]{:S(2)}, u32[]{:S(2)}) collective-permute-start(bf16[64,896]{1,0:T(8,128)(2,1)S(1)} %shard_map.140.mine_ref), channel_id=1, source_target_pairs={{0,2},{1,3},{2,0},{3,1},{4,6},{5,7},{6,4},{7,5},{8,10},{9,11},{10,... | collective-permute-start | bytes 344072 | tf_op jit(solution)/shard_map/ppermute | solution.py:545
  77.5 0.2 collective-permute-start.23
  77.8 1.3 %shard_map.137 = bf16[64,1024]{1,0:T(8,128)(2,1)S(1)} custom-call(s32[2]{0:T(128)S(1)} %pad_add_fusion.where_ref, bf16[64,896]{1,0:T(8,128)(2,1)S(1)} %collective-permute-done.13.mine_ref, bf16[64,896]{1,0:T(8,128)(2,1)S(1)} %collective-permute-done.14.other_ref, bf16[3584,2048]{1,0:T(8,128)(2,1)S(1)} %shard_map.133.w_ref, f32[64,2048]{1,0:T(8,128)S(1)} %shard_map.135.refs_0_), custom_call_target="tpu_custom_call" | custom-call | flops 234881024 | bytes 3670016 | tf_op jit(solution)/shard_map/pallas_call | solution.py:422
  79.1 2.4 %collective-permute-done.21.mine_ref = bf16[64,896]{1,0:T(8,128)(2,1)S(1)} collective-permute-done((bf16[64,896]{1,0:T(8,128)(2,1)S(1)}, bf16[64,896]{1,0:T(8,128)(2,1)S(1)}, u32[]{:S(2)}, u32[]{:S(2)}) %collective-permute-start.21) | collective-permute-done | bytes 114720 | tf_op jit(solution)/shard_map/ppermute | solution.py:545
  81.4 0.6 collective-permute-start.17
  82.1 1.9 %shard_map.141.refs_0_ = f32[64,2048]{1,0:T(8,128)S(1)} custom-call(s32[2]{0:T(128)S(1)} %pad_add_fusion.where_ref, bf16[64,896]{1,0:T(8,128)(2,1)S(1)} %shard_map.140.mine_ref, bf16[64,896]{1,0:T(8,128)(2,1)S(1)} %collective-permute-done.23.other_ref, bf16[3584,2048]{1,0:T(8,128)(2,1)S(1)} %shard_map.133.w_ref), custom_call_target="tpu_custom_call" | custom-call | flops 469762048 | bytes 7340032 | tf_op jit(solution)/shard_map/pallas_call | solution.py:422
  84.0 1.3 %shard_map.143 = bf16[64,1024]{1,0:T(8,128)(2,1)S(1)} custom-call(s32[2]{0:T(128)S(1)} %pad_add_fusion.where_ref, bf16[64,896]{1,0:T(8,128)(2,1)S(1)} %collective-permute-done.21.mine_ref, bf16[64,896]{1,0:T(8,128)(2,1)S(1)} %collective-permute-done.22.other_ref, bf16[3584,2048]{1,0:T(8,128)(2,1)S(1)} %shard_map.133.w_ref, f32[64,2048]{1,0:T(8,128)S(1)} %shard_map.141.refs_0_), custom_call_target="tpu_custom_call" | custom-call | flops 234881024 | bytes 3670016 | tf_op jit(solution)/shard_map/pallas_call | solution.py:422
  85.4 1.5 %collective-permute-start.24 = (bf16[64,1024]{1,0:T(8,128)(2,1)S(1)}, bf16[64,1024]{1,0:T(8,128)(2,1)S(1)}, u32[]{:S(2)}, u32[]{:S(2)}) collective-permute-start(bf16[64,1024]{1,0:T(8,128)(2,1)S(1)} %shard_map.143), channel_id=1, source_target_pairs={{0,4},{4,0},{8,12},{12,8},{1,5},{5,1},{9,13},{13,9},{2,6},{6,2},{1... | collective-permute-start | bytes 393224 | tf_op jit(solution)/shard_map/ppermute | solution.py:448
  86.8 1.3 %shard_map.136.refs_0_ = bf16[64,1024]{1,0:T(8,128)(2,1)S(1)} custom-call(s32[2]{0:T(128)S(1)} %pad_add_fusion.where_ref, bf16[64,896]{1,0:T(8,128)(2,1)S(1)} %collective-permute-done.13.mine_ref, bf16[64,896]{1,0:T(8,128)(2,1)S(1)} %collective-permute-done.14.other_ref, bf16[3584,2048]{1,0:T(8,128)(2,1)S(1)} %shard_map.133.w_ref, ...), custom_call_target="tpu_custom_call" | custom-call | flops 234881024 | bytes 3670016 | tf_op jit(solution)/shard_map/pallas_call | solution.py:422
  88.1 1.3 %shard_map.142.refs_0_ = bf16[64,1024]{1,0:T(8,128)(2,1)S(1)} custom-call(s32[2]{0:T(128)S(1)} %pad_add_fusion.where_ref, bf16[64,896]{1,0:T(8,128)(2,1)S(1)} %collective-permute-done.21.mine_ref, bf16[64,896]{1,0:T(8,128)(2,1)S(1)} %collective-permute-done.22.other_ref, bf16[3584,2048]{1,0:T(8,128)(2,1)S(1)} %shard_map.133.w_ref, ...), custom_call_target="tpu_custom_call" | custom-call | flops 234881024 | bytes 3670016 | tf_op jit(solution)/shard_map/pallas_call | solution.py:422
  89.5 2.3 %collective-permute-start.18 = (bf16[64,1024]{1,0:T(8,128)(2,1)S(1)}, bf16[64,1024]{1,0:T(8,128)(2,1)S(1)}, u32[]{:S(2)}, u32[]{:S(2)}) collective-permute-start(bf16[64,1024]{1,0:T(8,128)(2,1)S(1)} %shard_map.138.refs_0_), channel_id=1, source_target_pairs={{0,8},{4,12},{8,0},{12,4},{1,9},{5,13},{9,1},{13,5},{2,10},{6,14},... | collective-permute-start | bytes 393224 | tf_op jit(solution)/shard_map/ppermute | solution.py:449
  91.9 2.6 %collective-permute-start.25 = (bf16[64,1024]{1,0:T(8,128)(2,1)S(1)}, bf16[64,1024]{1,0:T(8,128)(2,1)S(1)}, u32[]{:S(2)}, u32[]{:S(2)}) collective-permute-start(bf16[64,1024]{1,0:T(8,128)(2,1)S(1)} %shard_map.144.refs_0_), channel_id=1, source_target_pairs={{0,8},{4,12},{8,0},{12,4},{1,9},{5,13},{9,1},{13,5},{2,10},{6,14},... | collective-permute-start | bytes 393224 | tf_op jit(solution)/shard_map/ppermute | solution.py:449
  94.5 7.9 %collective-permute-done.18.refs_1_ = bf16[64,1024]{1,0:T(8,128)(2,1)S(1)} collective-permute-done((bf16[64,1024]{1,0:T(8,128)(2,1)S(1)}, bf16[64,1024]{1,0:T(8,128)(2,1)S(1)}, u32[]{:S(2)}, u32[]{:S(2)}) %collective-permute-start.18) | collective-permute-done | bytes 131104 | tf_op jit(solution)/shard_map/ppermute | solution.py:449
  102.4 0.1 collective-permute-start.19
  102.5 1.8 %collective-permute-done.25.refs_1_ = bf16[64,1024]{1,0:T(8,128)(2,1)S(1)} collective-permute-done((bf16[64,1024]{1,0:T(8,128)(2,1)S(1)}, bf16[64,1024]{1,0:T(8,128)(2,1)S(1)}, u32[]{:S(2)}, u32[]{:S(2)}) %collective-permute-start.25) | collective-permute-done | bytes 131104 | tf_op jit(solution)/shard_map/ppermute | solution.py:449
  104.4 0.3 collective-permute-start.26
  104.7 4.1 %collective-permute-done.19.refs_3_ = bf16[64,1024]{1,0:T(8,128)(2,1)S(1)} collective-permute-done((bf16[64,1024]{1,0:T(8,128)(2,1)S(1)}, bf16[64,1024]{1,0:T(8,128)(2,1)S(1)}, u32[]{:S(2)}, u32[]{:S(2)}) %collective-permute-start.19) | collective-permute-done | bytes 131104 | tf_op jit(solution)/shard_map/ppermute | solution.py:546
  108.8 1.4 %collective-permute-done.26.refs_5_ = bf16[64,1024]{1,0:T(8,128)(2,1)S(1)} collective-permute-done((bf16[64,1024]{1,0:T(8,128)(2,1)S(1)}, bf16[64,1024]{1,0:T(8,128)(2,1)S(1)}, u32[]{:S(2)}, u32[]{:S(2)}) %collective-permute-start.26) | collective-permute-done | bytes 131104 | tf_op jit(solution)/shard_map/ppermute | solution.py:546
  110.3 1.5 %shard_map.146 = bf16[2,64,2048]{2,1,0:T(8,128)(2,1)} custom-call(s32[2]{0:T(128)S(1)} %pad_add_fusion.where_ref, bf16[128,1024]{1,0:T(8,128)(2,1)S(1)} %get-tuple-element.58.refs_0_, bf16[128,1024]{1,0:T(8,128)(2,1)S(1)} %get-tuple-element.63.refs_1_, bf16[64,1024]{1,0:T(8,128)(2,1)S(1)} %shard_map.139.refs_2_, ...), custom_call_target="tpu_custom_call" | custom-call | flops 262144 | bytes 1048576 | tf_op jit(solution)/shard_map/pallas_call | solution.py:393
  (27 shorter events, 0.3 us)
Async XLA Ops:
  0.0 16.7 %copy-start.2 = (bf16[2048]{0:T(1024)(128)(2,1)S(1)}, bf16[2048]{0:T(1024)(128)(2,1)}, u32[]{:S(2)}) copy-start(bf16[2048]{0:T(1024)(128)(2,1)} %param.20) | copy-start | bytes 12292
  0.1 0.7 copy-start.1
  8.6 6.7 %collective-permute-start.1 = (bf16[32,2048]{1,0:T(8,128)(2,1)S(1)}, bf16[32,2048]{1,0:T(8,128)(2,1)S(1)}, u32[]{:S(2)}, u32[]{:S(2)}) collective-permute-start(bf16[32,2048]{1,0:T(8,128)(2,1)S(1)} %get-tuple-element.50.refs_0_), channel_id=1, source_target_pairs={{0,2},{1,3},{2,0},{3,1},{4,6},{5,7},{6,4},{7,5},{8,10},{9,11},{10,... | collective-permute-start | bytes 393224 | tf_op jit(solution)/shard_map/ppermute | solution.py:545
  11.4 3.9 %collective-permute-start = (bf16[32,2048]{1,0:T(8,128)(2,1)S(1)}, bf16[32,2048]{1,0:T(8,128)(2,1)S(1)}, u32[]{:S(2)}, u32[]{:S(2)}) collective-permute-start(bf16[32,2048]{1,0:T(8,128)(2,1)S(1)} %get-tuple-element.50.refs_0_), channel_id=1, source_target_pairs={{0,1},{1,0},{2,3},{3,2},{4,5},{5,4},{6,7},{7,6},{8,9},{9,8},{10,11... | collective-permute-start | bytes 393224 | tf_op jit(solution)/shard_map/ppermute | solution.py:544
  15.3 1.3 %collective-permute-start.2 = (bf16[32,2048]{1,0:T(8,128)(2,1)S(1)}, bf16[32,2048]{1,0:T(8,128)(2,1)S(1)}, u32[]{:S(2)}, u32[]{:S(2)}) collective-permute-start(bf16[32,2048]{1,0:T(8,128)(2,1)S(1)} %collective-permute-done.1.refs_2_), channel_id=1, source_target_pairs={{0,1},{1,0},{2,3},{3,2},{4,5},{5,4},{6,7},{7,6},{8,9},{9,8},{10,11... | collective-permute-start | bytes 393224 | tf_op jit(solution)/shard_map/ppermute | solution.py:544
  18.0 8.4 %collective-permute-start.3 = (bf16[128,1024]{1,0:T(8,128)(2,1)S(1)}, bf16[128,1024]{1,0:T(8,128)(2,1)S(1)}, u32[]{:S(2)}, u32[]{:S(2)}) collective-permute-start(bf16[128,1024]{1,0:T(8,128)(2,1)S(1)} %shard_map.120), channel_id=1, source_target_pairs={{0,4},{4,0},{8,12},{12,8},{1,5},{5,1},{9,13},{13,9},{2,6},{6,2},{1... | collective-permute-start | bytes 786440 | tf_op jit(solution)/shard_map/ppermute | solution.py:546
  26.5 15.1 %copy-start = (bf16[2,64,2048]{2,1,0:T(8,128)(2,1)S(1)}, bf16[2,64,2048]{2,1,0:T(8,128)(2,1)}, u32[]{:S(2)}) copy-start(bf16[2,64,2048]{2,1,0:T(8,128)(2,1)} %res_ref.3) | copy-start | bytes 1572868
  26.5 14.5 %collective-permute-start.4 = (bf16[128,1024]{1,0:T(8,128)(2,1)S(1)}, bf16[128,1024]{1,0:T(8,128)(2,1)S(1)}, u32[]{:S(2)}, u32[]{:S(2)}) collective-permute-start(bf16[128,1024]{1,0:T(8,128)(2,1)S(1)} %shard_map.122.refs_0_), channel_id=1, source_target_pairs={{0,8},{4,12},{8,0},{12,4},{1,9},{5,13},{9,1},{13,5},{2,10},{6,14},... | collective-permute-start | bytes 786440 | tf_op jit(solution)/shard_map/ppermute | solution.py:557
  41.1 7.7 %collective-permute-start.5 = (bf16[128,1024]{1,0:T(8,128)(2,1)S(1)}, bf16[128,1024]{1,0:T(8,128)(2,1)S(1)}, u32[]{:S(2)}, u32[]{:S(2)}) collective-permute-start(bf16[128,1024]{1,0:T(8,128)(2,1)S(1)} %shard_map.124.attn_ref), channel_id=1, source_target_pairs={{0,4},{4,0},{8,12},{12,8},{1,5},{5,1},{9,13},{13,9},{2,6},{6,2},{1... | collective-permute-start | bytes 786440 | tf_op jit(solution)/shard_map/ppermute | solution.py:546
  49.5 1.3 %collective-permute-start.6 = (f32[128,128]{1,0:T(8,128)S(1)}, f32[128,128]{1,0:T(8,128)S(1)}, u32[]{:S(2)}, u32[]{:S(2)}) collective-permute-start(f32[128,128]{1,0:T(8,128)S(1)} %shard_map.128.refs_0_), channel_id=1, source_target_pairs={{0,1},{1,0},{2,3},{3,2},{4,5},{5,4},{6,7},{7,6},{8,9},{9,8},{10,11... | collective-permute-start | bytes 196616 | tf_op jit(solution)/shard_map/ppermute | solution.py:544
  52.9 4.8 %collective-permute-start.7 = (bf16[64,1792]{1,0:T(8,128)(2,1)S(1)}, bf16[64,1792]{1,0:T(8,128)(2,1)S(1)}, u32[]{:S(2)}, u32[]{:S(2)}) collective-permute-start(bf16[64,1792]{1,0:T(8,128)(2,1)S(1)} %get-tuple-element.70), channel_id=1, source_target_pairs={{0,1},{1,0},{2,3},{3,2},{4,5},{5,4},{6,7},{7,6},{8,9},{9,8},{10,11... | collective-permute-start | bytes 688136 | tf_op jit(solution)/shard_map/ppermute | solution.py:544
  53.1 4.6 %collective-permute-start.8 = (bf16[64,1792]{1,0:T(8,128)(2,1)S(1)}, bf16[64,1792]{1,0:T(8,128)(2,1)S(1)}, u32[]{:S(2)}, u32[]{:S(2)}) collective-permute-start(bf16[64,1792]{1,0:T(8,128)(2,1)S(1)} %get-tuple-element.71), channel_id=1, source_target_pairs={{0,1},{1,0},{2,3},{3,2},{4,5},{5,4},{6,7},{7,6},{8,9},{9,8},{10,11... | collective-permute-start | bytes 688136 | tf_op jit(solution)/shard_map/ppermute | solution.py:544
  53.5 4.3 %collective-permute-start.9 = (f32[128,128]{1,0:T(8,128)S(1)}, f32[128,128]{1,0:T(8,128)S(1)}, u32[]{:S(2)}, u32[]{:S(2)}) collective-permute-start(f32[128,128]{1,0:T(8,128)S(1)} %shard_map.128.refs_0_), channel_id=1, source_target_pairs={{0,2},{1,3},{2,0},{3,1},{4,6},{5,7},{6,4},{7,5},{8,10},{9,11},{10,... | collective-permute-start | bytes 196616 | tf_op jit(solution)/shard_map/ppermute | solution.py:545
  57.8 10.1 %collective-permute-start.11 = (bf16[64,1792]{1,0:T(8,128)(2,1)S(1)}, bf16[64,1792]{1,0:T(8,128)(2,1)S(1)}, u32[]{:S(2)}, u32[]{:S(2)}) collective-permute-start(bf16[64,1792]{1,0:T(8,128)(2,1)S(1)} %shard_map.130), channel_id=1, source_target_pairs={{0,2},{1,3},{2,0},{3,1},{4,6},{5,7},{6,4},{7,5},{8,10},{9,11},{10,... | collective-permute-start | bytes 688136 | tf_op jit(solution)/shard_map/ppermute | solution.py:545
  61.6 6.4 %collective-permute-start.10 = (bf16[64,1792]{1,0:T(8,128)(2,1)S(1)}, bf16[64,1792]{1,0:T(8,128)(2,1)S(1)}, u32[]{:S(2)}, u32[]{:S(2)}) collective-permute-start(bf16[64,1792]{1,0:T(8,128)(2,1)S(1)} %get-tuple-element.76), channel_id=1, source_target_pairs={{0,1},{1,0},{2,3},{3,2},{4,5},{5,4},{6,7},{7,6},{8,9},{9,8},{10,11... | collective-permute-start | bytes 688136 | tf_op jit(solution)/shard_map/ppermute | solution.py:544
  61.7 13.7 %collective-permute-start.15 = (bf16[64,1792]{1,0:T(8,128)(2,1)S(1)}, bf16[64,1792]{1,0:T(8,128)(2,1)S(1)}, u32[]{:S(2)}, u32[]{:S(2)}) collective-permute-start(bf16[64,1792]{1,0:T(8,128)(2,1)S(1)} %shard_map.131), channel_id=1, source_target_pairs={{0,2},{1,3},{2,0},{3,1},{4,6},{5,7},{6,4},{7,5},{8,10},{9,11},{10,... | collective-permute-start | bytes 688136 | tf_op jit(solution)/shard_map/ppermute | solution.py:545
  62.1 13.3 %collective-permute-start.20 = (bf16[64,1792]{1,0:T(8,128)(2,1)S(1)}, bf16[64,1792]{1,0:T(8,128)(2,1)S(1)}, u32[]{:S(2)}, u32[]{:S(2)}) collective-permute-start(bf16[64,1792]{1,0:T(8,128)(2,1)S(1)} %get-tuple-element.82), channel_id=1, source_target_pairs={{0,1},{1,0},{2,3},{3,2},{4,5},{5,4},{6,7},{7,6},{8,9},{9,8},{10,11... | collective-permute-start | bytes 688136 | tf_op jit(solution)/shard_map/ppermute | solution.py:544
  62.3 5.7 %collective-permute-start.12 = (f32[128,128]{1,0:T(8,128)S(1)}, f32[128,128]{1,0:T(8,128)S(1)}, u32[]{:S(2)}, u32[]{:S(2)}) collective-permute-start(f32[128,128]{1,0:T(8,128)S(1)} %collective-permute-done.9.refs_2_), channel_id=1, source_target_pairs={{0,1},{1,0},{2,3},{3,2},{4,5},{5,4},{6,7},{7,6},{8,9},{9,8},{10,11... | collective-permute-start | bytes 196616 | tf_op jit(solution)/shard_map/ppermute | solution.py:544
  68.2 5.3 %collective-permute-start.13 = (bf16[64,896]{1,0:T(8,128)(2,1)S(1)}, bf16[64,896]{1,0:T(8,128)(2,1)S(1)}, u32[]{:S(2)}, u32[]{:S(2)}) collective-permute-start(bf16[64,896]{1,0:T(8,128)(2,1)S(1)} %shard_map.134.mine_ref), channel_id=1, source_target_pairs={{0,2},{1,3},{2,0},{3,1},{4,6},{5,7},{6,4},{7,5},{8,10},{9,11},{10,... | collective-permute-start | bytes 344072 | tf_op jit(solution)/shard_map/ppermute | solution.py:545
  69.9 3.6 %collective-permute-start.16 = (bf16[64,896]{1,0:T(8,128)(2,1)S(1)}, bf16[64,896]{1,0:T(8,128)(2,1)S(1)}, u32[]{:S(2)}, u32[]{:S(2)}) collective-permute-start(bf16[64,896]{1,0:T(8,128)(2,1)S(1)} %shard_map.134.mine_ref), channel_id=1, source_target_pairs={{0,1},{1,0},{2,3},{3,2},{4,5},{5,4},{6,7},{7,6},{8,9},{9,8},{10,11... | collective-permute-start | bytes 344072 | tf_op jit(solution)/shard_map/ppermute | solution.py:544
  73.5 4.3 %collective-permute-start.14 = (bf16[64,896]{1,0:T(8,128)(2,1)S(1)}, bf16[64,896]{1,0:T(8,128)(2,1)S(1)}, u32[]{:S(2)}, u32[]{:S(2)}) collective-permute-start(bf16[64,896]{1,0:T(8,128)(2,1)S(1)} %collective-permute-done.13.mine_ref), channel_id=1, source_target_pairs={{0,1},{1,0},{2,3},{3,2},{4,5},{5,4},{6,7},{7,6},{8,9},{9,8},{10,11... | collective-permute-start | bytes 344072 | tf_op jit(solution)/shard_map/ppermute | solution.py:544
  75.8 5.6 %collective-permute-start.21 = (bf16[64,896]{1,0:T(8,128)(2,1)S(1)}, bf16[64,896]{1,0:T(8,128)(2,1)S(1)}, u32[]{:S(2)}, u32[]{:S(2)}) collective-permute-start(bf16[64,896]{1,0:T(8,128)(2,1)S(1)} %shard_map.140.mine_ref), channel_id=1, source_target_pairs={{0,2},{1,3},{2,0},{3,1},{4,6},{5,7},{6,4},{7,5},{8,10},{9,11},{10,... | collective-permute-start | bytes 344072 | tf_op jit(solution)/shard_map/ppermute | solution.py:545
  77.5 4.5 %collective-permute-start.23 = (bf16[64,896]{1,0:T(8,128)(2,1)S(1)}, bf16[64,896]{1,0:T(8,128)(2,1)S(1)}, u32[]{:S(2)}, u32[]{:S(2)}) collective-permute-start(bf16[64,896]{1,0:T(8,128)(2,1)S(1)} %shard_map.140.mine_ref), channel_id=1, source_target_pairs={{0,1},{1,0},{2,3},{3,2},{4,5},{5,4},{6,7},{7,6},{8,9},{9,8},{10,11... | collective-permute-start | bytes 344072 | tf_op jit(solution)/shard_map/ppermute | solution.py:544
  81.4 2.6 %collective-permute-start.22 = (bf16[64,896]{1,0:T(8,128)(2,1)S(1)}, bf16[64,896]{1,0:T(8,128)(2,1)S(1)}, u32[]{:S(2)}, u32[]{:S(2)}) collective-permute-start(bf16[64,896]{1,0:T(8,128)(2,1)S(1)} %collective-permute-done.21.mine_ref), channel_id=1, source_target_pairs={{0,1},{1,0},{2,3},{3,2},{4,5},{5,4},{6,7},{7,6},{8,9},{9,8},{10,11... | collective-permute-start | bytes 344072 | tf_op jit(solution)/shard_map/ppermute | solution.py:544
  81.4 8.0 %collective-permute-start.17 = (bf16[64,1024]{1,0:T(8,128)(2,1)S(1)}, bf16[64,1024]{1,0:T(8,128)(2,1)S(1)}, u32[]{:S(2)}, u32[]{:S(2)}) collective-permute-start(bf16[64,1024]{1,0:T(8,128)(2,1)S(1)} %shard_map.137), channel_id=1, source_target_pairs={{0,4},{4,0},{8,12},{12,8},{1,5},{5,1},{9,13},{13,9},{2,6},{6,2},{1... | collective-permute-start | bytes 393224 | tf_op jit(solution)/shard_map/ppermute | solution.py:448
  85.4 6.5 %collective-permute-start.24 = (bf16[64,1024]{1,0:T(8,128)(2,1)S(1)}, bf16[64,1024]{1,0:T(8,128)(2,1)S(1)}, u32[]{:S(2)}, u32[]{:S(2)}) collective-permute-start(bf16[64,1024]{1,0:T(8,128)(2,1)S(1)} %shard_map.143), channel_id=1, source_target_pairs={{0,4},{4,0},{8,12},{12,8},{1,5},{5,1},{9,13},{13,9},{2,6},{6,2},{1... | collective-permute-start | bytes 393224 | tf_op jit(solution)/shard_map/ppermute | solution.py:448
  89.5 12.9 %collective-permute-start.18 = (bf16[64,1024]{1,0:T(8,128)(2,1)S(1)}, bf16[64,1024]{1,0:T(8,128)(2,1)S(1)}, u32[]{:S(2)}, u32[]{:S(2)}) collective-permute-start(bf16[64,1024]{1,0:T(8,128)(2,1)S(1)} %shard_map.138.refs_0_), channel_id=1, source_target_pairs={{0,8},{4,12},{8,0},{12,4},{1,9},{5,13},{9,1},{13,5},{2,10},{6,14},... | collective-permute-start | bytes 393224 | tf_op jit(solution)/shard_map/ppermute | solution.py:449
  91.9 12.5 %collective-permute-start.25 = (bf16[64,1024]{1,0:T(8,128)(2,1)S(1)}, bf16[64,1024]{1,0:T(8,128)(2,1)S(1)}, u32[]{:S(2)}, u32[]{:S(2)}) collective-permute-start(bf16[64,1024]{1,0:T(8,128)(2,1)S(1)} %shard_map.144.refs_0_), channel_id=1, source_target_pairs={{0,8},{4,12},{8,0},{12,4},{1,9},{5,13},{9,1},{13,5},{2,10},{6,14},... | collective-permute-start | bytes 393224 | tf_op jit(solution)/shard_map/ppermute | solution.py:449
  102.4 6.4 %collective-permute-start.19 = (bf16[64,1024]{1,0:T(8,128)(2,1)S(1)}, bf16[64,1024]{1,0:T(8,128)(2,1)S(1)}, u32[]{:S(2)}, u32[]{:S(2)}) collective-permute-start(bf16[64,1024]{1,0:T(8,128)(2,1)S(1)} %shard_map.139.refs_2_), channel_id=1, source_target_pairs={{0,4},{4,0},{8,12},{12,8},{1,5},{5,1},{9,13},{13,9},{2,6},{6,2},{1... | collective-permute-start | bytes 393224 | tf_op jit(solution)/shard_map/ppermute | solution.py:546
  104.4 5.9 %collective-permute-start.26 = (bf16[64,1024]{1,0:T(8,128)(2,1)S(1)}, bf16[64,1024]{1,0:T(8,128)(2,1)S(1)}, u32[]{:S(2)}, u32[]{:S(2)}) collective-permute-start(bf16[64,1024]{1,0:T(8,128)(2,1)S(1)} %shard_map.145.refs_4_), channel_id=1, source_target_pairs={{0,4},{4,0},{8,12},{12,8},{1,5},{5,1},{9,13},{13,9},{2,6},{6,2},{1... | collective-permute-start | bytes 393224 | tf_op jit(solution)/shard_map/ppermute | solution.py:546

commit v3 on v2

--- a/solution.py
+++ b/solution.py
@@ -34,14 +34,15 @@
 
 
 def cost(flops, read):
-    return pl.CostEstimate(flops=flops, bytes_accessed=read, transcendentals=0)
-
-
-def attention_kernel(first, count, len_ref, q_hbm, k_hbm, v_hbm, nk_hbm, nv_hbm, w_hbm, *refs):
-    o_ref, w_ref, q_ref, nk_ref, nv_ref, k_buf, v_buf, out_buf, sem, small_sem, w_sem = refs
+    return pl.CostEstimate(flops=flops // 1000, bytes_accessed=read // 1000, transcendentals=0)
+
+
+def attention_kernel(first, count, len_hbm, q_hbm, k_hbm, v_hbm, nk_hbm, nv_hbm, *refs):
+    o_ref, len_ref, q_ref, nk_ref, nv_ref = refs[:5]
+    k_buf, v_buf, out_buf, sem, small_sem = refs[5:]
+    ends = ((len_hbm, len_ref), (q_hbm, q_ref), (nk_hbm, nk_ref), (nv_hbm, nv_ref))
     small = [
-        pltpu.make_async_copy(src, dst, small_sem.at[k])
-        for k, (src, dst) in enumerate(((q_hbm, q_ref), (nk_hbm, nk_ref), (nv_hbm, nv_ref)))
+        pltpu.make_async_copy(src, dst, small_sem.at[k]) for k, (src, dst) in enumerate(ends)
     ]
     for move in small:
         move.start()
@@ -72,16 +73,17 @@
         for move in moves(b, c):
             move.wait()
 
+    start(0, 0)
+    small[0].wait()
     for b in range(count):
-        start(b, 0)
+        if b:
+            start(b, 0)
         for c in range(1, parts):
             live = len_ref[first + b] > c * part
             pl.when(live)(functools.partial(start, b, c))
             pl.when(jnp.logical_not(live))(functools.partial(clear, b, c))
 
-    weight = pltpu.make_async_copy(w_hbm, w_ref, w_sem)
-    weight.start()
-    for move in small:
+    for move in small[1:]:
         move.wait()
     slot = lax.broadcasted_iota(jnp.int32, (rows, slots), 1)
     step = lax.broadcasted_iota(jnp.int32, (rows, 1), 0) // group
@@ -136,27 +138,24 @@
                     at = s * count + b
                     out_buf[at : at + 1, cols] = out[s * group + j : s * group + j + 1, :]
     o_ref[...] = out_buf[...].astype(BF16)
-    weight.wait()
-
-
-def attention(queries, new_keys, new_values, key_cache, value_cache, lengths, weight):
+
+
+def attention(queries, new_keys, new_values, key_cache, value_cache, lengths):
     first, count = 0, queries.shape[1]
     steps, _, deep = queries.shape
     _, copies, slots, head = key_cache.shape
     vmem = pl.BlockSpec(memory_space=pltpu.VMEM)
     hbm = pl.BlockSpec(memory_space=pl.ANY)
     buffer = pltpu.VMEM((count, copies, slots, head), BF16)
-    moved = [queries, key_cache, value_cache, new_keys, new_values, weight]
+    moved = [lengths, queries, key_cache, value_cache, new_keys, new_values]
     moved = [pltpu.with_memory_space_constraint(x, pltpu.HBM) for x in moved]
     return pl.pallas_call(
         functools.partial(attention_kernel, first, count),
-        in_specs=[pl.BlockSpec(memory_space=pltpu.SMEM)] + [hbm] * 6,
-        out_specs=[vmem, vmem],
-        out_shape=[
-            jax.ShapeDtypeStruct((steps * count, deep), BF16),
-            pltpu.VMEM(weight.shape, weight.dtype),
-        ],
+        in_specs=[hbm] * 6,
+        out_specs=vmem,
+        out_shape=jax.ShapeDtypeStruct((steps * count, deep), BF16),
         scratch_shapes=[
+            pltpu.SMEM(lengths.shape, lengths.dtype),
             pltpu.VMEM(queries.shape, BF16),
             pltpu.VMEM(new_keys.shape, BF16),
             pltpu.VMEM(new_values.shape, BF16),
@@ -164,77 +163,87 @@
             buffer,
             pltpu.VMEM((steps * count, deep), F32),
             pltpu.SemaphoreType.DMA((2, count)),
-            pltpu.SemaphoreType.DMA((3,)),
-            pltpu.SemaphoreType.DMA(()),
+            pltpu.SemaphoreType.DMA((4,)),
         ],
         cost_estimate=cost(4 * steps * count * slots * deep, 4 * count * copies * slots * head),
-        compiler_params=pltpu.CompilerParams(vmem_limit_bytes=40 * MIB),
-    )(lengths, *moved)
-
-
-def fetch_kernel(after, pieces, src_ref, *refs):
-    o_ref, sem = refs[after], refs[-1]
-    step = src_ref.shape[0] // pieces
-    moves = [
-        pltpu.make_async_copy(
-            src_ref.at[pl.ds(k * step, step)], o_ref.at[pl.ds(k * step, step)], sem.at[k]
+        compiler_params=pltpu.CompilerParams(vmem_limit_bytes=20 * MIB),
+    )(*moved)
+
+
+def fetch_kernel(axis, flip, pieces, where_ref, src_ref, *refs):
+    o_ref, sem = refs[-2:]
+    cut = [pl.ds(0, n) for n in src_ref.shape]
+    cut[axis] = half_of(where_ref, flip, o_ref.shape[axis])
+    if axis == 0:
+        start, step = cut[0].start, o_ref.shape[0] // pieces
+    else:
+        start, step = 0, src_ref.shape[0] // pieces
+    moves = []
+    for k in range(pieces):
+        from_ref = src_ref.at[pl.ds(pl.multiple_of(start + k * step, 16), step), cut[1]]
+        moves.append(
+            pltpu.make_async_copy(from_ref, o_ref.at[pl.ds(k * step, step)], sem.at[k])
         )
-        for k in range(pieces)
-    ]
     for move in moves:
         move.start()
     for move in moves:
         move.wait()
 
 
-def fetch(weight, after):
+def fetch(where, weight, axis, flip, after):
     src = pltpu.with_memory_space_constraint(weight, pltpu.HBM)
     hbm = pl.BlockSpec(memory_space=pl.ANY)
     pieces = 8
-    return pl.pallas_call(
-        functools.partial(fetch_kernel, len(after), pieces),
-        in_specs=[hbm] * (1 + len(after)),
+    shape = list(weight.shape)
+    shape[axis] //= 2
+    return pl.pallas_call(
+        functools.partial(fetch_kernel, axis, flip, pieces),
+        in_specs=[pl.BlockSpec(memory_space=pltpu.SMEM)] + [hbm] * (1 + len(after)),
         out_specs=pl.BlockSpec(memory_space=pltpu.VMEM),
-        out_shape=pltpu.VMEM(weight.shape, weight.dtype),
+        out_shape=pltpu.VMEM(tuple(shape), weight.dtype),
         scratch_shapes=[pltpu.SemaphoreType.DMA((pieces,))],
-        cost_estimate=cost(0, 2 * weight.size),
+        cost_estimate=cost(0, weight.size),
         compiler_params=pltpu.CompilerParams(vmem_limit_bytes=1 * MIB),
-    )(src, *after)
+    )(where, src, *after)
 
 
 def half_of(where_ref, flip, length):
     return pl.ds(pl.multiple_of((where_ref[1] ^ flip) * length, 128), length)
 
 
-def product_kernel(flip, where_ref, *refs):
-    block_refs, (w_ref, o_ref, x_buf) = refs[:-3], refs[-3:]
+def product_kernel(flip, groups, where_ref, *refs):
+    x_buf, o_refs = refs[-1], refs[-1 - groups : -1]
+    block_refs, w_ref = refs[: -2 - groups], refs[-2 - groups]
     count = block_refs[0].shape[0]
     for k, block_ref in enumerate(block_refs):
         at = pl.multiple_of((where_ref[0] ^ k) * count, count)
         x_buf[pl.ds(at, count), :] = block_ref[...]
-    cols = half_of(where_ref, flip, o_ref.shape[1])
-    o_ref[...] = jnp.dot(x_buf[...], w_ref[:, cols], preferred_element_type=F32).astype(BF16)
-
-
-def product(where, blocks, w, flip):
+    rows, wide = o_refs[0].shape
+    cols = half_of(where_ref, flip, wide)
+    out = jnp.dot(x_buf[...], w_ref[:, cols], preferred_element_type=F32).astype(BF16)
+    for n, o_ref in enumerate(o_refs):
+        o_ref[...] = out[n * rows : (n + 1) * rows]
+
+
+def product(where, blocks, w, flip, groups):
     wide = w.shape[1] // 2
     count, deep = blocks[0].shape
     rows = count * len(blocks)
     vmem = pl.BlockSpec(memory_space=pltpu.VMEM)
     return pl.pallas_call(
-        functools.partial(product_kernel, flip),
+        functools.partial(product_kernel, flip, groups),
         in_specs=[pl.BlockSpec(memory_space=pltpu.SMEM)] + [vmem] * (len(blocks) + 1),
-        out_specs=vmem,
-        out_shape=jax.ShapeDtypeStruct((rows, wide), BF16),
+        out_specs=[vmem] * groups,
+        out_shape=[jax.ShapeDtypeStruct((rows // groups, wide), BF16)] * groups,
         scratch_shapes=[pltpu.VMEM((rows, deep), BF16)],
         cost_estimate=cost(2 * rows * deep * wide, 2 * deep * wide),
         compiler_params=pltpu.CompilerParams(vmem_limit_bytes=4 * MIB),
     )(where, *blocks, w)
 
 
-def middle_kernel(flip, where_ref, attn_ref, res_ref, gain_ref, *o_refs):
-    mid_ref, normed_ref, sq_ref = o_refs
-    steps, seqs, _ = res_ref.shape
+def middle_kernel(flip, groups, where_ref, *refs):
+    attn_refs, (res_ref, gain_ref, mid_ref, normed_ref) = refs[:groups], refs[groups : groups + 4]
+    steps = res_ref.shape[0]
     rows, wide = mid_ref.shape
     count = rows // (steps * 4)
     cols = half_of(where_ref, flip, wide)
@@ -242,37 +251,39 @@
     for d in range(4):
         for s in range(steps):
             parts.append(res_ref[s, d * count : (d + 1) * count, cols].astype(F32))
-    mid = (jnp.concatenate(parts, axis=0) + attn_ref[...].astype(F32)).astype(BF16)
+    attn = jnp.concatenate([ref[...].astype(F32) for ref in attn_refs], axis=0)
+    mid = (jnp.concatenate(parts, axis=0) + attn).astype(BF16)
     whole = mid.astype(F32)
     mid_ref[...] = mid
     normed_ref[...] = (whole * gain_ref[:1, cols].astype(F32)).astype(BF16)
-    sq_ref[...] = jnp.broadcast_to(jnp.sum(whole * whole, axis=1, keepdims=True), sq_ref.shape)
+    for sq_ref in refs[groups + 4 :]:
+        squares = jnp.broadcast_to(jnp.sum(whole * whole, axis=1, keepdims=True), (rows, rows))
+        sq_ref[...] = jnp.transpose(squares)[: sq_ref.shape[0]]
 
 
 def middle_part(where, flip, attn, residual, gain):
-    rows, wide = attn.shape
-    vmem = pl.BlockSpec(memory_space=pltpu.VMEM)
-    return pl.pallas_call(
-        functools.partial(middle_kernel, flip),
-        in_specs=[pl.BlockSpec(memory_space=pltpu.SMEM)] + [vmem] * 3,
-        out_specs=[vmem] * 3,
-        out_shape=[
-            jax.ShapeDtypeStruct((rows, wide), BF16),
-            jax.ShapeDtypeStruct((rows, wide), BF16),
-            jax.ShapeDtypeStruct((rows, 128), F32),
-        ],
+    rows, wide = attn[0].shape[0] * len(attn), attn[0].shape[1]
+    vmem = pl.BlockSpec(memory_space=pltpu.VMEM)
+    outs = [jax.ShapeDtypeStruct((rows, wide), BF16)] * 2
+    if not flip:
+        outs.append(jax.ShapeDtypeStruct((8, rows), F32))
+    return pl.pallas_call(
+        functools.partial(middle_kernel, flip, len(attn)),
+        in_specs=[pl.BlockSpec(memory_space=pltpu.SMEM)] + [vmem] * (len(attn) + 2),
+        out_specs=[vmem] * len(outs),
+        out_shape=outs,
         cost_estimate=cost(8 * rows * wide, 8 * rows * wide),
         compiler_params=pltpu.CompilerParams(vmem_limit_bytes=6 * MIB),
-    )(where, attn, residual, gain)
+    )(where, *attn, residual, gain)
 
 
 def first_kernel(wide, where_ref, x_ref, g_ref, u_ref, o_ref):
-    deep = half_of(where_ref, 0, x_ref.shape[1])
+    deep, all_rows = half_of(where_ref, 0, x_ref.shape[1]), slice(None)
     length = g_ref.shape[1]
     for k, w_ref in enumerate((g_ref, u_ref)):
         for at in range(0, length, wide):
             here = slice(at, at + wide)
-            out = jnp.dot(x_ref[...], w_ref[deep, here], preferred_element_type=F32)
+            out = jnp.dot(x_ref[...], w_ref[deep if k else all_rows, here], preferred_element_type=F32)
             o_ref[:, k * length + at : k * length + at + wide] = out
 
 
@@ -293,13 +304,13 @@
 def second_kernel(chip, groups, where_ref, x_ref, f_ref, g_ref, u_ref, *refs):
     give_refs, (keep_ref, buf) = refs[:groups], refs[groups:]
     me = where_ref[0]
-    deep = half_of(where_ref, 1, x_ref.shape[1])
+    deep, all_rows = half_of(where_ref, 1, x_ref.shape[1]), slice(None)
     length = g_ref.shape[1]
     own = length // 4
     rows = give_refs[0].shape[0]
     start = pl.multiple_of(((me // 2) ^ chip) * (2 * own), 128)
     for k, w_ref in enumerate((g_ref, u_ref)):
-        out = jnp.dot(x_ref[...], w_ref[deep, pl.ds(start, 2 * own)], preferred_element_type=F32)
+        out = jnp.dot(x_ref[...], w_ref[deep if k else all_rows, pl.ds(start, 2 * own)], preferred_element_type=F32)
         buf[...] = out + f_ref[:, pl.ds(pl.multiple_of(k * length + start, 128), 2 * own)]
         mine = pl.ds(pl.multiple_of((me % 2) * own, 128), own)
         other = pl.ds(pl.multiple_of((1 - me % 2) * own, 128), own)
@@ -348,7 +359,9 @@
 def act_kernel(n, full, near_ref, got_ref, far_ref, *refs):
     sq_refs, o_ref = refs[:-1], refs[-1]
     rows, cols = o_ref.shape
-    total = functools.reduce(jnp.add, [sq[n * rows : (n + 1) * rows, :1] for sq in sq_refs])
+    total = functools.reduce(jnp.add, [sq[:1, :] for sq in sq_refs])
+    total = jnp.transpose(jnp.broadcast_to(total, (total.shape[1], total.shape[1])))
+    total = total[n * rows : (n + 1) * rows, :1]
     inv_norm = lax.rsqrt(total / full + 1e-05)
     here = slice(n * rows, (n + 1) * rows)
     both = near_ref[here, :] + got_ref[...].astype(F32) + far_ref[...].astype(F32)
@@ -400,27 +413,27 @@
     )(where, *flat)
 
 
-def down_kernel(chip, flip, has_sum, where_ref, mine_ref, other_ref, w_ref, *refs):
+def down_kernel(chip, flip, where_ref, mine_ref, other_ref, w_ref, *refs):
     o_ref, buf = refs[-2:]
     own = mine_ref.shape[1]
     me = where_ref[0]
     buf[:, pl.ds(pl.multiple_of((me % 2) * own, 128), own)] = mine_ref[...]
     buf[:, pl.ds(pl.multiple_of((1 - me % 2) * own, 128), own)] = other_ref[...]
     at = pl.ds(pl.multiple_of(((me // 2) ^ chip) * (2 * own), 128), 2 * own)
-    cols = slice(None) if flip is None else half_of(where_ref, flip, o_ref.shape[1])
-    total = jnp.dot(buf[...], w_ref[at, cols], preferred_element_type=F32)
-    if has_sum:
-        total = total + refs[0][:, cols]
+    total = jnp.dot(buf[...], w_ref[at, half_of(where_ref, flip, o_ref.shape[1])], preferred_element_type=F32)
+    for ref in refs[:-2]:
+        total = total + ref[...]
     o_ref[...] = total.astype(o_ref.dtype)
 
 
-def down(where, mine, other, chip, weight, flip=None, total=None, dtype=F32):
+def down(where, mine, other, chip, weight, flip, total=None):
     rows, own = mine.shape
-    wide = weight.shape[1] // (1 if flip is None else 2)
+    wide = weight.shape[1] // 2
+    dtype = F32 if total is None else BF16
     vmem = pl.BlockSpec(memory_space=pltpu.VMEM)
     args = [where, mine, other, weight] + ([] if total is None else [total])
     return pl.pallas_call(
-        functools.partial(down_kernel, chip, flip, total is not None),
+        functools.partial(down_kernel, chip, flip),
         in_specs=[pl.BlockSpec(memory_space=pltpu.SMEM)] + [vmem] * (len(args) - 1),
         out_specs=vmem,
         out_shape=jax.ShapeDtypeStruct((rows, wide), dtype),
@@ -442,15 +455,6 @@
 
 def levels(size):
     return [1 << k for k in range(size.bit_length() - 1)]
-
-
-def sum_tensor(send, keep, during=None):
-    held = total_of(keep, lax.ppermute(send, "tensor", pairs(4, 1)))
-    got = lax.ppermute(held, "tensor", pairs(4, 2))
-    beside = None if during is None else during(held)
-    if beside is not None:
-        got, beside = lax.optimization_barrier((got, beside))
-    return total_of(held, got), beside
 
 
 def gather_rows(block, size):
@@ -523,17 +527,15 @@
     steps, all_seqs, width = residual.shape
     local_seqs = queries.shape[1]
     where = jnp.stack([lax.axis_index("dp"), lax.axis_index("tensor") % 2])
-    where, lengths = lax.optimization_barrier((where, lengths))
-    heads, out_w = attention(
-        queries, new_keys, new_values, key_cache, value_cache, lengths, out_weight
-    )
+    where, queries = lax.optimization_barrier((where, queries))
+    heads = attention(queries, new_keys, new_values, key_cache, value_cache, lengths)
     if dp == 4 and tensor == 4:
         weights = gate_weight, up_weight, down_weight
         gain, heads = lax.optimization_barrier((norm_gain, heads))
-        return fast(where, heads, residual, gain, out_w, *weights)
+        return fast(where, heads, residual, gain, out_weight, *weights)
     row_count = steps * all_seqs
     resid = residual.reshape(steps, dp, local_seqs, width).swapaxes(0, 1)
-    weights = out_w, norm_gain, gate_weight, up_weight, down_weight
+    weights = out_weight, norm_gain, gate_weight, up_weight, down_weight
     out = plain(gather_rows(heads, dp), resid.reshape(row_count, width), *weights, dp)
     return out.reshape(dp, steps, local_seqs, width).swapaxes(0, 1).reshape(residual.shape)
 
@@ -545,58 +547,100 @@
     across = lambda value: lax.ppermute(value, "dp", pairs(4, 2))
     swap = lambda value: lax.ppermute(value, "tensor", pairs(4, 1))
     gain = jnp.broadcast_to(gain[None, :], (16, width))
+    after = lambda value, *others: lax.optimization_barrier((value, *others))[0]
+
+    def sum_tensor(sends, keeps, during=lambda n, held: None):
+        gots = [swap(send) for send in sends]
+        helds, crosses = [None, None], [None, None]
+        for n in range(2):
+            if n:
+                gots[n] = after(gots[n], helds[0])
+            keep, gots[n] = keeps(n, helds[0], gots[n])
+            helds[n] = total_of(keep, gots[n])
+            crosses[n] = lax.ppermute(helds[n], "tensor", pairs(4, 2))
+        others = [None, None]
+        for n in range(2):
+            beside = during(n, helds[1 - n])
+            if beside is not None:
+                crosses[n] = after(crosses[n], beside)
+            helds[n] = total_of(helds[n], crosses[n])
+            others[n] = swap(helds[n])
+            if n == 0:
+                crosses[1] = after(crosses[1], helds[0])
+        return helds, others
+
+    out_w, up_w, down_w = [
+        pltpu.with_memory_space_constraint(w, pltpu.VMEM) for w in (out_w, up_weight, down_weight)
+    ]
+    gate_own = fetch(where, gate_weight, 0, 0, [heads])
     far = across(heads)
-    blocks = [heads, core(heads), far, core(far)]
+    near = core(heads)
+    far, near, gate_own = lax.optimization_barrier((far, near, gate_own))
+    blocks = [heads, near, far, core(far)]
     blocks, gain = lax.optimization_barrier((blocks, gain))
-    send = product(where, blocks, out_w, 1)
-    keep = product(where, blocks, out_w, 0)
-    gate_w = fetch(gate_weight, [keep])
-    got = swap(send)
-    got, gate_w = lax.optimization_barrier((got, gate_w))
-    held = total_of(keep, got)
-    got = lax.ppermute(held, "tensor", pairs(4, 2))
-    up_w = fetch(up_weight, [held])
-    got, up_w = lax.optimization_barrier((got, up_w))
-    held = total_of(held, got)
-    other = swap(held)
-    weights = gate_w, up_w
-    mid, normed, sq = middle_part(where, 0, held, residual, gain)
-    first = gate_up_first(where, normed, weights)
-    other, first = lax.optimization_barrier((other, first))
-    mid_other, normed, sq_other = middle_part(where, 1, other, residual, gain)
-    sq = total_of(sq, sq_other, dtype=F32)
-    sq_far = across(sq)
-    normed, sq_core = lax.optimization_barrier((normed, core(sq)))
+    sends = product(where, blocks, out_w, 1, groups)
+    kept = product(where, blocks, out_w, 0, groups)
+
+    gate_far = []
+
+    def keeps(n, held, got):
+        return kept[n], got
+
+    def during(n, held):
+        if n == 0:
+            gate_far.append(fetch(where, gate_weight, 0, 1, [held]))
+            return gate_far[0]
+
+    helds, others = sum_tensor(sends, keeps, during)
+    mid, normed, sq = middle_part(where, 0, helds, residual, gain)
+    sq_core = core(sq)
+    first = gate_up_first(where, normed, (gate_own, up_w))
+    sq_chip = total_of(sq, sq_core, dtype=F32)
+    sq_sum = total_of(sq_chip, across(sq_chip), dtype=F32)
+    others, first, sq_sum = lax.optimization_barrier((others, first, sq_sum))
+    squares = [sq_sum, swap(sq_sum)]
+    mid_other, normed = middle_part(where, 1, others, residual, gain)
+    weights = gate_far[0], up_w
     give, keep = gate_up_second(where, normed, first, weights, 1, groups)
     far = [core(x) for x in give]
-    far, sq_far = lax.optimization_barrier((far, sq_far))
-    squares = [sq, sq_core, sq_far, core(sq_far)]
     relayed = [relay(n, keep, x) for n, x in enumerate(far)]
     far = [across(x) for x in relayed]
     normed, relayed = lax.optimization_barrier((normed, relayed))
     give, near = gate_up_second(where, normed, first, weights, 0, groups)
     got = [core(x) for x in give]
-    down_w = fetch(down_weight, [near])
-    far[0], down_w = lax.optimization_barrier((far[0], down_w))
-    mine, mine_far, other, totals, outs = [], [], [], [], []
-    for n in range(groups):
-        if n:
-            far[n], totals[0] = lax.optimization_barrier((far[n], totals[0]))
-        mine.append(act(n, near, got[n], far[n], squares, width * 4))
-        mine_far.append(across(mine[n]))
-        other.append(core(mine[n]))
-        totals.append(down(where, mine[n], other[n], 0, down_w))
-    for n in range(groups):
-        last = lambda flip: down(
-            where, mine_far[n], other_far, 1, down_w, flip, totals[n], BF16
-        )
-        if n:
-            mine_far[n], send = lax.optimization_barrier((mine_far[n], send))
-        other_far = core(mine_far[n])
-        send = last(1)
-        keep = last(0)
-        held, _ = sum_tensor(send, keep)
-        outs.append((held, swap(held)))
+    far[0], near, got = lax.optimization_barrier((far[0], near, got))
+
+    def activated(n):
+        mine = act(n, near, got[n], far[n], squares, width * 4)
+        other = core(mine)
+        return mine, across(mine), other
+
+    def early(n):
+        return [down(where, mine[n], other[n], 0, down_w, flip) for flip in (1, 0)]
+
+    mine, mine_far, other, totals, other_far = [0] * 2, [0] * 2, [0] * 2, [0] * 2, [0] * 2
+    mine[0], mine_far[0], other[0] = activated(0)
+    totals[0] = early(0)
+    far[1] = after(far[1], totals[0])
+    mine[1], mine_far[1], other[1] = activated(1)
+    mine_far[0] = after(mine_far[0], mine[1])
+    other_far[0] = core(mine_far[0])
+    totals[1] = early(1)
+    other_far[0] = after(other_far[0], totals[1])
+    send_a = down(where, mine_far[0], other_far[0], 1, down_w, 1, totals[0][0])
+    keep_a = down(where, mine_far[0], other_far[0], 1, down_w, 0, totals[0][1])
+    mine_far[1] = after(mine_far[1], keep_a)
+    other_far[1] = core(mine_far[1])
+    send_b = down(where, mine_far[1], other_far[1], 1, down_w, 1, totals[1][0])
+
+    def keeps(n, held, got):
+        if n == 0:
+            return keep_a, after(got, send_b)
+        total = after(totals[1][1], held)
+        return down(where, mine_far[1], other_far[1], 1, down_w, 0, total), got
+
+    helds, others = sum_tensor([send_a, send_b], keeps)
+    outs = list(zip(helds, others))
     return final(where, [mid, mid_other], outs, residual.shape)
 
 

time: 112 us -> 99.9 us (0.89)
  Pallas kernels: 46.1 us -> 37.9 us
  waiting for transfers between devices: 40.8 us -> 35 us
  starting transfers between devices: 23.8 us -> 26.1 us
    pallas_call x13 -> x14, Pallas kernels: 29.2 us -> 22.1 us  [the longest x8 10.6 us: down(): pl.pallas_call(functools.partial(down_kernel, chip, flip), in_specs=[pl.B...]
    ppermute x6, waiting for transfers between devices: 12.4 us -> 6.27 us  [fast(): across = lambda value: lax.ppermute(value, 'dp', pairs(4, 2))]
    ppermute x4 -> x9, starting transfers between devices: 2.49 us -> 7.18 us  [fast(): swap = lambda value: lax.ppermute(value, 'tensor', pairs(4, 1))]
    ppermute x5 -> x4, waiting for transfers between devices: 16.3 us -> 13.6 us  [sum_tensor(): crosses[n] = lax.ppermute(helds[n], 'tensor', pairs(4, 2))]
    ppermute x6, starting transfers between devices: 10.1 us -> 7.57 us  [fast(): across = lambda value: lax.ppermute(value, 'dp', pairs(4, 2))]
    ppermute x4 -> x9, waiting for transfers between devices: 9.54 us -> 11.3 us  [fast(): swap = lambda value: lax.ppermute(value, 'tensor', pairs(4, 1))]
    ppermute x12 -> x11, waiting for transfers between devices: 2.61 us -> 3.86 us  [fast(): core = lambda value: lax.ppermute(value, 'dp', pairs(4, 1))]
    ppermute x5 -> x4, starting transfers between devices: 9.73 us -> 9.35 us  [sum_tensor(): crosses[n] = lax.ppermute(helds[n], 'tensor', pairs(4, 2))]
  transfers between devices with their start and end apart: 27 -> 30, of which waited for: 13 -> 17; matrix products, arithmetic and copies ran while one was open for 0% -> 0% of each run, Pallas kernels for 29% -> 26%
where the time goes in v3:
time: 99.9 us; the launch traced here: 99.6 us
  Pallas kernels  37.9 us (38%)
  waiting for transfers between devices  35 us (35%)
  starting transfers between devices  26.1 us (26%)
    ppermute x4, waiting for transfers between devices, sum_tensor(): crosses[n] = lax.ppermute(helds[n], 'tensor', pairs(4, 2))  13.6 us
    ppermute x9, waiting for transfers between devices, fast(): swap = lambda value: lax.ppermute(value, 'tensor', pairs(4, 1))  11.3 us
    pallas_call x8, Pallas kernels, down(): pl.pallas_call(functools.partial(down_kernel, chip, flip), in_specs=[pl.B...  10.6 us
    ppermute x4, starting transfers between devices, sum_tensor(): crosses[n] = lax.ppermute(helds[n], 'tensor', pairs(4, 2))  9.35 us
    ppermute x6, starting transfers between devices, fast(): across = lambda value: lax.ppermute(value, 'dp', pairs(4, 2))  7.57 us
    pallas_call x2, Pallas kernels, fetch(): pl.pallas_call(functools.partial(fetch_kernel, axis, flip, pieces), in_sp...  7.43 us
    ppermute x9, starting transfers between devices, fast(): swap = lambda value: lax.ppermute(value, 'tensor', pairs(4, 1))  7.18 us
    pallas_call x1, Pallas kernels, attention(): pl.pallas_call(functools.partial(attention_kernel, first, count), in_spec...  6.92 us
  transfers between devices with their start and end apart: 30, of which 17 were waited for; matrix products, arithmetic and copies ran while one was open for 0% of the time, Pallas kernels for 26%

profile of v3, /device:TPU:0, one launch (start us, length us, event | category | flops | bytes accessed | tf_op | source)
XLA Modules:
  0.0 99.6 jit_solution(17337906347944756839)
XLA Ops:
  0.0 0.1 pad_add_fusion.where_ref
  0.1 6.9 %shard_map.118.refs_0_ = bf16[32,2048]{1,0:T(8,128)(2,1)S(1)} custom-call(s32[16]{0:T(128)} %len_hbm.1, bf16[2,16,2048]{2,1,0:T(8,128)(2,1)} %q_hbm, bf16[16,2,1024,128]{3,2,1,0:T(8,128)(2,1)} %k_hbm.1, bf16[16,2,1024,128]{3,2,1,0:T(8,128)(2,1)} %v_hbm.1, bf16[2,16,2,128]{3,2,1,0:T(2,128)(2,1)} %nk_hbm.1, bf16[2,16,2,128]{3,2,1,0:T(2,128)(2,1)} %nv_hbm.1), custom_call_target="tpu_custom_call" | custom-call | flops 268435 | bytes 16777 | tf_op jit(solution)/shard_map/pallas_call | solution.py:152
  7.0 0.7 collective-permute-start.1
  7.7 2.2 %collective-permute-start = (bf16[32,2048]{1,0:T(8,128)(2,1)S(1)}, bf16[32,2048]{1,0:T(8,128)(2,1)S(1)}, u32[]{:S(2)}, u32[]{:S(2)}) collective-permute-start(bf16[32,2048]{1,0:T(8,128)(2,1)S(1)} %shard_map.118.refs_0_), channel_id=1, source_target_pairs={{0,2},{1,3},{2,0},{3,1},{4,6},{5,7},{6,4},{7,5},{8,10},{9,11},{10,... | collective-permute-start | bytes 393224 | tf_op jit(solution)/shard_map/ppermute | solution.py:547
  9.9 3.7 %shard_map.119.g_ref = bf16[1024,3584]{1,0:T(8,128)(2,1)S(1)} custom-call(s32[2]{0:T(128)S(1)} %pad_add_fusion.where_ref, bf16[2048,3584]{1,0:T(8,128)(2,1)} %src_ref.3, bf16[32,2048]{1,0:T(8,128)(2,1)S(1)} %shard_map.118.refs_0_), custom_call_target="tpu_custom_call" | custom-call | bytes 7340 | tf_op jit(solution)/shard_map/pallas_call | solution.py:199
  13.6 0.4 collective-permute-done.refs_2_
  14.0 1.3 %collective-permute-done.2.refs_3_ = bf16[32,2048]{1,0:T(8,128)(2,1)S(1)} collective-permute-done((bf16[32,2048]{1,0:T(8,128)(2,1)S(1)}, bf16[32,2048]{1,0:T(8,128)(2,1)S(1)}, u32[]{:S(2)}, u32[]{:S(2)}) %collective-permute-start.2) | collective-permute-done | bytes 131104 | tf_op jit(solution)/shard_map/ppermute | solution.py:546
  15.4 1.3 %shard_map.121 = (bf16[64,1024]{1,0:T(8,128)(2,1)S(1)}, bf16[64,1024]{1,0:T(8,128)(2,1)S(1)}) custom-call(s32[2]{0:T(128)S(1)} %pad_add_fusion.where_ref, bf16[32,2048]{1,0:T(8,128)(2,1)S(1)} %shard_map.118.refs_0_, bf16[32,2048]{1,0:T(8,128)(2,1)S(1)} %collective-permute-done.1.refs_1_, bf16[32,2048]{1,0:T(8,128)(2,1)S(1)} %collective-permute-done.refs_2_, ...), custom_call_target="tpu_custom_call" | custom-call | flops 536870 | bytes 4194 | tf_op jit(solution)/shard_map/pallas_call | solution.py:233
  16.7 2.1 %collective-permute-start.3 = (bf16[64,1024]{1,0:T(8,128)(2,1)S(1)}, bf16[64,1024]{1,0:T(8,128)(2,1)S(1)}, u32[]{:S(2)}, u32[]{:S(2)}) collective-permute-start(bf16[64,1024]{1,0:T(8,128)(2,1)S(1)} %get-tuple-element.63), channel_id=1, source_target_pairs={{0,4},{4,0},{8,12},{12,8},{1,5},{5,1},{9,13},{13,9},{2,6},{6,2},{1... | collective-permute-start | bytes 393224 | tf_op jit(solution)/shard_map/ppermute | solution.py:548
  18.8 0.1 collective-permute-start.5
  18.9 1.3 %shard_map.120 = (bf16[64,1024]{1,0:T(8,128)(2,1)S(1)}, bf16[64,1024]{1,0:T(8,128)(2,1)S(1)}) custom-call(s32[2]{0:T(128)S(1)} %pad_add_fusion.where_ref, bf16[32,2048]{1,0:T(8,128)(2,1)S(1)} %shard_map.118.refs_0_, bf16[32,2048]{1,0:T(8,128)(2,1)S(1)} %collective-permute-done.1.refs_1_, bf16[32,2048]{1,0:T(8,128)(2,1)S(1)} %collective-permute-done.refs_2_, ...), custom_call_target="tpu_custom_call" | custom-call | flops 536870 | bytes 4194 | tf_op jit(solution)/shard_map/pallas_call | solution.py:233
  20.2 2.9 %collective-permute-done.3.refs_1_ = bf16[64,1024]{1,0:T(8,128)(2,1)S(1)} collective-permute-done((bf16[64,1024]{1,0:T(8,128)(2,1)S(1)}, bf16[64,1024]{1,0:T(8,128)(2,1)S(1)}, u32[]{:S(2)}, u32[]{:S(2)}) %collective-permute-start.3) | collective-permute-done | bytes 131104 | tf_op jit(solution)/shard_map/ppermute | solution.py:548
  23.1 3.1 %collective-permute-start.4 = (bf16[64,1024]{1,0:T(8,128)(2,1)S(1)}, bf16[64,1024]{1,0:T(8,128)(2,1)S(1)}, u32[]{:S(2)}, u32[]{:S(2)}) collective-permute-start(bf16[64,1024]{1,0:T(8,128)(2,1)S(1)} %shard_map.122.refs_0_), channel_id=1, source_target_pairs={{0,8},{4,12},{8,0},{12,4},{1,9},{5,13},{9,1},{13,5},{2,10},{6,14},... | collective-permute-start | bytes 393224 | tf_op jit(solution)/shard_map/ppermute | solution.py:560
  26.3 2.8 %collective-permute-start.6 = (bf16[64,1024]{1,0:T(8,128)(2,1)S(1)}, bf16[64,1024]{1,0:T(8,128)(2,1)S(1)}, u32[]{:S(2)}, u32[]{:S(2)}) collective-permute-start(bf16[64,1024]{1,0:T(8,128)(2,1)S(1)} %shard_map.123.refs_0_), channel_id=1, source_target_pairs={{0,8},{4,12},{8,0},{12,4},{1,9},{5,13},{9,1},{13,5},{2,10},{6,14},... | collective-permute-start | bytes 393224 | tf_op jit(solution)/shard_map/ppermute | solution.py:560
  29.1 3.7 %shard_map.124.g_ref = bf16[1024,3584]{1,0:T(8,128)(2,1)S(1)} custom-call(s32[2]{0:T(128)S(1)} %pad_add_fusion.where_ref, bf16[2048,3584]{1,0:T(8,128)(2,1)} %src_ref.3, bf16[64,1024]{1,0:T(8,128)(2,1)S(1)} %shard_map.123.refs_0_), custom_call_target="tpu_custom_call" | custom-call | bytes 7340 | tf_op jit(solution)/shard_map/pallas_call | solution.py:199
  32.8 2.5 %collective-permute-done.4.refs_1_ = bf16[64,1024]{1,0:T(8,128)(2,1)S(1)} collective-permute-done((bf16[64,1024]{1,0:T(8,128)(2,1)S(1)}, bf16[64,1024]{1,0:T(8,128)(2,1)S(1)}, u32[]{:S(2)}, u32[]{:S(2)}) %collective-permute-start.4) | collective-permute-done | bytes 131104 | tf_op jit(solution)/shard_map/ppermute | solution.py:560
  35.4 1.8 %collective-permute-done.6.refs_1_ = bf16[64,1024]{1,0:T(8,128)(2,1)S(1)} collective-permute-done((bf16[64,1024]{1,0:T(8,128)(2,1)S(1)}, bf16[64,1024]{1,0:T(8,128)(2,1)S(1)}, u32[]{:S(2)}, u32[]{:S(2)}) %collective-permute-start.6) | collective-permute-done | bytes 131104 | tf_op jit(solution)/shard_map/ppermute | solution.py:560
  37.2 0.5 collective-permute-start.8
  37.7 1.6 %collective-permute-start.7 = (bf16[64,1024]{1,0:T(8,128)(2,1)S(1)}, bf16[64,1024]{1,0:T(8,128)(2,1)S(1)}, u32[]{:S(2)}, u32[]{:S(2)}) collective-permute-start(bf16[64,1024]{1,0:T(8,128)(2,1)S(1)} %shard_map.125.refs_0_), channel_id=1, source_target_pairs={{0,4},{4,0},{8,12},{12,8},{1,5},{5,1},{9,13},{13,9},{2,6},{6,2},{1... | collective-permute-start | bytes 393224 | tf_op jit(solution)/shard_map/ppermute | solution.py:548
  39.3 0.8 shard_map.127
  40.1 1.2 %collective-permute-done.9.refs_1_ = f32[8,128]{1,0:T(8,128)S(1)} collective-permute-done((f32[8,128]{1,0:T(8,128)S(1)}, f32[8,128]{1,0:T(8,128)S(1)}, u32[]{:S(2)}, u32[]{:S(2)}) %collective-permute-start.9) | collective-permute-done | bytes 4128 | tf_op jit(solution)/shard_map/ppermute | solution.py:546
  41.3 1.4 %collective-permute-start.10 = (f32[8,128]{1,0:T(8,128)S(1)}, f32[8,128]{1,0:T(8,128)S(1)}, u32[]{:S(2)}, u32[]{:S(2)}) collective-permute-start(f32[8,128]{1,0:T(8,128)S(1)} %shard_map.129.refs_0_), channel_id=1, source_target_pairs={{0,2},{1,3},{2,0},{3,1},{4,6},{5,7},{6,4},{7,5},{8,10},{9,11},{10,... | collective-permute-start | bytes 12296 | tf_op jit(solution)/shard_map/ppermute | solution.py:547
  42.7 2.6 %shard_map.128.f_ref = f32[128,7168]{1,0:T(8,128)S(1)} custom-call(s32[2]{0:T(128)S(1)} %pad_add_fusion.where_ref, bf16[128,1024]{1,0:T(8,128)(2,1)S(1)} %get-tuple-element.71.x_ref, bf16[1024,3584]{1,0:T(8,128)(2,1)S(1)} %shard_map.119.g_ref, bf16[2048,3584]{1,0:T(8,128)(2,1)S(1)} %bitcast.5), custom_call_target="tpu_custom_call" | custom-call | flops 1879048 | bytes 14680 | tf_op jit(solution)/shard_map/pallas_call | solution.py:294
  45.4 0.7 shard_map.131
  46.0 2.0 %shard_map.132 = (bf16[64,1792]{1,0:T(8,128)(2,1)S(1)}, bf16[64,1792]{1,0:T(8,128)(2,1)S(1)}, f32[128,1792]{1,0:T(8,128)S(1)}) custom-call(s32[2]{0:T(128)S(1)} %pad_add_fusion.where_ref, bf16[128,1024]{1,0:T(8,128)(2,1)S(1)} %get-tuple-element.82.x_ref, f32[128,7168]{1,0:T(8,128)S(1)} %shard_map.128.f_ref, bf16[1024,3584]{1,0:T(8,128)(2,1)S(1)} %shard_map.124.g_ref, ...), custom_call_target="tpu_custom_call" | custom-call | flops 939524 | bytes 7340 | tf_op jit(solution)/shard_map/pallas_call | solution.py:328
  48.1 0.1 collective-permute-start.11
  48.2 0.5 collective-permute-start.13
  48.7 1.0 collective-permute-done.11.got_ref
  49.7 0.9 collective-permute-start.12
  50.7 2.0 %shard_map.135 = (bf16[64,1792]{1,0:T(8,128)(2,1)S(1)}, bf16[64,1792]{1,0:T(8,128)(2,1)S(1)}, f32[128,1792]{1,0:T(8,128)S(1)}) custom-call(s32[2]{0:T(128)S(1)} %pad_add_fusion.where_ref, bf16[128,1024]{1,0:T(8,128)(2,1)S(1)} %get-tuple-element.82.x_ref, f32[128,7168]{1,0:T(8,128)S(1)} %shard_map.128.f_ref, bf16[1024,3584]{1,0:T(8,128)(2,1)S(1)} %shard_map.124.g_ref, ...), custom_call_target="tpu_custom_call" | custom-call | flops 939524 | bytes 7340 | tf_op jit(solution)/shard_map/pallas_call | solution.py:328
  52.8 0.5 collective-permute-start.15
  53.3 1.2 %collective-permute-start.18 = (bf16[64,1792]{1,0:T(8,128)(2,1)S(1)}, bf16[64,1792]{1,0:T(8,128)(2,1)S(1)}, u32[]{:S(2)}, u32[]{:S(2)}) collective-permute-start(bf16[64,1792]{1,0:T(8,128)(2,1)S(1)} %shard_map.134), channel_id=1, source_target_pairs={{0,2},{1,3},{2,0},{3,1},{4,6},{5,7},{6,4},{7,5},{8,10},{9,11},{10,... | collective-permute-start | bytes 688136 | tf_op jit(solution)/shard_map/ppermute | solution.py:547
  54.5 0.3 collective-permute-start.16
  54.8 3.4 %collective-permute-done.12.far_ref = bf16[64,1792]{1,0:T(8,128)(2,1)S(1)} collective-permute-done((bf16[64,1792]{1,0:T(8,128)(2,1)S(1)}, bf16[64,1792]{1,0:T(8,128)(2,1)S(1)}, u32[]{:S(2)}, u32[]{:S(2)}) %collective-permute-start.12) | collective-permute-done | bytes 229408 | tf_op jit(solution)/shard_map/ppermute | solution.py:547
  58.2 0.2 shard_map.136.mine_ref
  58.4 0.1 collective-permute-start.19
  58.5 0.9 collective-permute-start.17
  59.5 0.4 collective-permute-done.19.other_ref
  59.9 1.3 %shard_map.138.refs_0_ = f32[64,1024]{1,0:T(8,128)S(1)} custom-call(s32[2]{0:T(128)S(1)} %pad_add_fusion.where_ref, bf16[64,896]{1,0:T(8,128)(2,1)S(1)} %shard_map.136.mine_ref, bf16[64,896]{1,0:T(8,128)(2,1)S(1)} %collective-permute-done.19.other_ref, bf16[3584,2048]{1,0:T(8,128)(2,1)S(1)} %bitcast.3), custom_call_target="tpu_custom_call" | custom-call | flops 234881 | bytes 3670 | tf_op jit(solution)/shard_map/pallas_call | solution.py:435
  61.2 1.5 %shard_map.137.refs_0_ = f32[64,1024]{1,0:T(8,128)S(1)} custom-call(s32[2]{0:T(128)S(1)} %pad_add_fusion.where_ref, bf16[64,896]{1,0:T(8,128)(2,1)S(1)} %shard_map.136.mine_ref, bf16[64,896]{1,0:T(8,128)(2,1)S(1)} %collective-permute-done.19.other_ref, bf16[3584,2048]{1,0:T(8,128)(2,1)S(1)} %bitcast.3), custom_call_target="tpu_custom_call" | custom-call | flops 234881 | bytes 3670 | tf_op jit(solution)/shard_map/pallas_call | solution.py:435
  62.7 0.3 collective-permute-done.18.far_ref
  62.9 0.2 shard_map.139.mine_ref
  63.2 0.1 collective-permute-start.21
  63.3 1.5 %collective-permute-done.17.mine_ref = bf16[64,896]{1,0:T(8,128)(2,1)S(1)} collective-permute-done((bf16[64,896]{1,0:T(8,128)(2,1)S(1)}, bf16[64,896]{1,0:T(8,128)(2,1)S(1)}, u32[]{:S(2)}, u32[]{:S(2)}) %collective-permute-start.17) | collective-permute-done | bytes 114720 | tf_op jit(solution)/shard_map/ppermute | solution.py:547
  64.8 0.9 collective-permute-start.23
  65.7 1.3 %shard_map.141.refs_0_ = f32[64,1024]{1,0:T(8,128)S(1)} custom-call(s32[2]{0:T(128)S(1)} %pad_add_fusion.where_ref, bf16[64,896]{1,0:T(8,128)(2,1)S(1)} %shard_map.139.mine_ref, bf16[64,896]{1,0:T(8,128)(2,1)S(1)} %collective-permute-done.21.other_ref, bf16[3584,2048]{1,0:T(8,128)(2,1)S(1)} %bitcast.3), custom_call_target="tpu_custom_call" | custom-call | flops 234881 | bytes 3670 | tf_op jit(solution)/shard_map/pallas_call | solution.py:435
  67.0 1.3 %shard_map.140.refs_0_ = f32[64,1024]{1,0:T(8,128)S(1)} custom-call(s32[2]{0:T(128)S(1)} %pad_add_fusion.where_ref, bf16[64,896]{1,0:T(8,128)(2,1)S(1)} %shard_map.139.mine_ref, bf16[64,896]{1,0:T(8,128)(2,1)S(1)} %collective-permute-done.21.other_ref, bf16[3584,2048]{1,0:T(8,128)(2,1)S(1)} %bitcast.3), custom_call_target="tpu_custom_call" | custom-call | flops 234881 | bytes 3670 | tf_op jit(solution)/shard_map/pallas_call | solution.py:435
  68.3 1.3 %shard_map.142.refs_0_ = bf16[64,1024]{1,0:T(8,128)(2,1)S(1)} custom-call(s32[2]{0:T(128)S(1)} %pad_add_fusion.where_ref, bf16[64,896]{1,0:T(8,128)(2,1)S(1)} %collective-permute-done.17.mine_ref, bf16[64,896]{1,0:T(8,128)(2,1)S(1)} %collective-permute-done.20.other_ref, bf16[3584,2048]{1,0:T(8,128)(2,1)S(1)} %bitcast.3, f32[64,1024]{1,0:T(8,128)S(1)} %shard_map.138.refs_0_), custom_call_target="tpu_custom_call" | custom-call | flops 234881 | bytes 3670 | tf_op jit(solution)/shard_map/pallas_call | solution.py:435
  69.6 0.7 collective-permute-done.23.mine_ref
  70.3 1.3 %shard_map.143 = bf16[64,1024]{1,0:T(8,128)(2,1)S(1)} custom-call(s32[2]{0:T(128)S(1)} %pad_add_fusion.where_ref, bf16[64,896]{1,0:T(8,128)(2,1)S(1)} %collective-permute-done.17.mine_ref, bf16[64,896]{1,0:T(8,128)(2,1)S(1)} %collective-permute-done.20.other_ref, bf16[3584,2048]{1,0:T(8,128)(2,1)S(1)} %bitcast.3, f32[64,1024]{1,0:T(8,128)S(1)} %shard_map.137.refs_0_), custom_call_target="tpu_custom_call" | custom-call | flops 234881 | bytes 3670 | tf_op jit(solution)/shard_map/pallas_call | solution.py:435
  71.7 0.4 collective-permute-start.22
  72.0 1.3 %shard_map.144 = bf16[64,1024]{1,0:T(8,128)(2,1)S(1)} custom-call(s32[2]{0:T(128)S(1)} %pad_add_fusion.where_ref, bf16[64,896]{1,0:T(8,128)(2,1)S(1)} %collective-permute-done.23.mine_ref, bf16[64,896]{1,0:T(8,128)(2,1)S(1)} %collective-permute-done.24.other_ref, bf16[3584,2048]{1,0:T(8,128)(2,1)S(1)} %bitcast.3, f32[64,1024]{1,0:T(8,128)S(1)} %shard_map.140.refs_0_), custom_call_target="tpu_custom_call" | custom-call | flops 234881 | bytes 3670 | tf_op jit(solution)/shard_map/pallas_call | solution.py:435
  73.3 1.8 %collective-permute-start.27 = (bf16[64,1024]{1,0:T(8,128)(2,1)S(1)}, bf16[64,1024]{1,0:T(8,128)(2,1)S(1)}, u32[]{:S(2)}, u32[]{:S(2)}) collective-permute-start(bf16[64,1024]{1,0:T(8,128)(2,1)S(1)} %shard_map.144), channel_id=1, source_target_pairs={{0,4},{4,0},{8,12},{12,8},{1,5},{5,1},{9,13},{13,9},{2,6},{6,2},{1... | collective-permute-start | bytes 393224 | tf_op jit(solution)/shard_map/ppermute | solution.py:548
  75.1 2.9 %collective-permute-done.22.refs_1_ = bf16[64,1024]{1,0:T(8,128)(2,1)S(1)} collective-permute-done((bf16[64,1024]{1,0:T(8,128)(2,1)S(1)}, bf16[64,1024]{1,0:T(8,128)(2,1)S(1)}, u32[]{:S(2)}, u32[]{:S(2)}) %collective-permute-start.22) | collective-permute-done | bytes 131104 | tf_op jit(solution)/shard_map/ppermute | solution.py:548
  78.1 1.6 %collective-permute-start.25 = (bf16[64,1024]{1,0:T(8,128)(2,1)S(1)}, bf16[64,1024]{1,0:T(8,128)(2,1)S(1)}, u32[]{:S(2)}, u32[]{:S(2)}) collective-permute-start(bf16[64,1024]{1,0:T(8,128)(2,1)S(1)} %shard_map.145.refs_0_), channel_id=1, source_target_pairs={{0,8},{4,12},{8,0},{12,4},{1,9},{5,13},{9,1},{13,5},{2,10},{6,14},... | collective-permute-start | bytes 393224 | tf_op jit(solution)/shard_map/ppermute | solution.py:560
  79.7 1.3 %shard_map.147.refs_0_ = bf16[64,1024]{1,0:T(8,128)(2,1)S(1)} custom-call(s32[2]{0:T(128)S(1)} %pad_add_fusion.where_ref, bf16[64,896]{1,0:T(8,128)(2,1)S(1)} %collective-permute-done.23.mine_ref, bf16[64,896]{1,0:T(8,128)(2,1)S(1)} %collective-permute-done.24.other_ref, bf16[3584,2048]{1,0:T(8,128)(2,1)S(1)} %bitcast.3, f32[64,1024]{1,0:T(8,128)S(1)} %shard_map.141.refs_0_), custom_call_target="tpu_custom_call" | custom-call | flops 234881 | bytes 3670 | tf_op jit(solution)/shard_map/pallas_call | solution.py:435
  81.0 1.8 %collective-permute-start.28 = (bf16[64,1024]{1,0:T(8,128)(2,1)S(1)}, bf16[64,1024]{1,0:T(8,128)(2,1)S(1)}, u32[]{:S(2)}, u32[]{:S(2)}) collective-permute-start(bf16[64,1024]{1,0:T(8,128)(2,1)S(1)} %shard_map.148.refs_0_), channel_id=1, source_target_pairs={{0,8},{4,12},{8,0},{12,4},{1,9},{5,13},{9,1},{13,5},{2,10},{6,14},... | collective-permute-start | bytes 393224 | tf_op jit(solution)/shard_map/ppermute | solution.py:560
  82.9 7.6 %collective-permute-done.25.refs_1_ = bf16[64,1024]{1,0:T(8,128)(2,1)S(1)} collective-permute-done((bf16[64,1024]{1,0:T(8,128)(2,1)S(1)}, bf16[64,1024]{1,0:T(8,128)(2,1)S(1)}, u32[]{:S(2)}, u32[]{:S(2)}) %collective-permute-start.25) | collective-permute-done | bytes 131104 | tf_op jit(solution)/shard_map/ppermute | solution.py:560
  90.5 0.1 collective-permute-start.26
  90.6 1.7 %collective-permute-done.28.refs_1_ = bf16[64,1024]{1,0:T(8,128)(2,1)S(1)} collective-permute-done((bf16[64,1024]{1,0:T(8,128)(2,1)S(1)}, bf16[64,1024]{1,0:T(8,128)(2,1)S(1)}, u32[]{:S(2)}, u32[]{:S(2)}) %collective-permute-start.28) | collective-permute-done | bytes 131104 | tf_op jit(solution)/shard_map/ppermute | solution.py:560
  92.3 0.3 collective-permute-start.29
  92.7 4.1 %collective-permute-done.26.refs_3_ = bf16[64,1024]{1,0:T(8,128)(2,1)S(1)} collective-permute-done((bf16[64,1024]{1,0:T(8,128)(2,1)S(1)}, bf16[64,1024]{1,0:T(8,128)(2,1)S(1)}, u32[]{:S(2)}, u32[]{:S(2)}) %collective-permute-start.26) | collective-permute-done | bytes 131104 | tf_op jit(solution)/shard_map/ppermute | solution.py:548
  96.7 1.4 %collective-permute-done.29.refs_5_ = bf16[64,1024]{1,0:T(8,128)(2,1)S(1)} collective-permute-done((bf16[64,1024]{1,0:T(8,128)(2,1)S(1)}, bf16[64,1024]{1,0:T(8,128)(2,1)S(1)}, u32[]{:S(2)}, u32[]{:S(2)}) %collective-permute-start.29) | collective-permute-done | bytes 131104 | tf_op jit(solution)/shard_map/ppermute | solution.py:548
  98.1 1.5 %shard_map.150 = bf16[2,64,2048]{2,1,0:T(8,128)(2,1)} custom-call(s32[2]{0:T(128)S(1)} %pad_add_fusion.where_ref, bf16[128,1024]{1,0:T(8,128)(2,1)S(1)} %get-tuple-element.70.refs_0_, bf16[128,1024]{1,0:T(8,128)(2,1)S(1)} %get-tuple-element.76.refs_1_, bf16[64,1024]{1,0:T(8,128)(2,1)S(1)} %shard_map.146.refs_2_, ...), custom_call_target="tpu_custom_call" | custom-call | flops 262 | bytes 1048 | tf_op jit(solution)/shard_map/pallas_call | solution.py:406
  (58 shorter events, 0.6 us)
Async XLA Ops:
  0.1 15.3 %slice-start.8 = ((s8[8388608]{0:T(1024)(128)(4,1)}), s8[4194304]{0:T(1024)(128)(4,1)S(1)}, s32[]{:S(2)}) async-start(s8[8388608]{0:T(1024)(128)(4,1)} %bitcast.6), calls=%async_computation.8 | async-start | bytes 8388608
  7.0 8.3 %copy-start.1 = (bf16[2048]{0:T(1024)(128)(2,1)S(1)}, bf16[2048]{0:T(1024)(128)(2,1)}, u32[]{:S(2)}) copy-start(bf16[2048]{0:T(1024)(128)(2,1)} %param.20) | copy-start | bytes 12292
  7.0 8.3 %slice-start.9 = ((s8[8388608]{0:T(1024)(128)(4,1)}), s8[4194304]{0:T(1024)(128)(4,1)S(1)}, s32[]{:S(2)}) async-start(s8[8388608]{0:T(1024)(128)(4,1)} %bitcast.6), calls=%async_computation.9 | async-start | bytes 8388608
  7.0 6.6 %collective-permute-start.1 = (bf16[32,2048]{1,0:T(8,128)(2,1)S(1)}, bf16[32,2048]{1,0:T(8,128)(2,1)S(1)}, u32[]{:S(2)}, u32[]{:S(2)}) collective-permute-start(bf16[32,2048]{1,0:T(8,128)(2,1)S(1)} %shard_map.118.refs_0_), channel_id=1, source_target_pairs={{0,1},{1,0},{2,3},{3,2},{4,5},{5,4},{6,7},{7,6},{8,9},{9,8},{10,11... | collective-permute-start | bytes 393224 | tf_op jit(solution)/shard_map/ppermute | solution.py:546
  7.7 6.3 %collective-permute-start = (bf16[32,2048]{1,0:T(8,128)(2,1)S(1)}, bf16[32,2048]{1,0:T(8,128)(2,1)S(1)}, u32[]{:S(2)}, u32[]{:S(2)}) collective-permute-start(bf16[32,2048]{1,0:T(8,128)(2,1)S(1)} %shard_map.118.refs_0_), channel_id=1, source_target_pairs={{0,2},{1,3},{2,0},{3,1},{4,6},{5,7},{6,4},{7,5},{8,10},{9,11},{10,... | collective-permute-start | bytes 393224 | tf_op jit(solution)/shard_map/ppermute | solution.py:547
  14.0 1.3 %collective-permute-start.2 = (bf16[32,2048]{1,0:T(8,128)(2,1)S(1)}, bf16[32,2048]{1,0:T(8,128)(2,1)S(1)}, u32[]{:S(2)}, u32[]{:S(2)}) collective-permute-start(bf16[32,2048]{1,0:T(8,128)(2,1)S(1)} %collective-permute-done.refs_2_), channel_id=1, source_target_pairs={{0,1},{1,0},{2,3},{3,2},{4,5},{5,4},{6,7},{7,6},{8,9},{9,8},{10,11... | collective-permute-start | bytes 393224 | tf_op jit(solution)/shard_map/ppermute | solution.py:546
  16.7 6.4 %collective-permute-start.3 = (bf16[64,1024]{1,0:T(8,128)(2,1)S(1)}, bf16[64,1024]{1,0:T(8,128)(2,1)S(1)}, u32[]{:S(2)}, u32[]{:S(2)}) collective-permute-start(bf16[64,1024]{1,0:T(8,128)(2,1)S(1)} %get-tuple-element.63), channel_id=1, source_target_pairs={{0,4},{4,0},{8,12},{12,8},{1,5},{5,1},{9,13},{13,9},{2,6},{6,2},{1... | collective-permute-start | bytes 393224 | tf_op jit(solution)/shard_map/ppermute | solution.py:548
  18.8 7.5 %collective-permute-start.5 = (bf16[64,1024]{1,0:T(8,128)(2,1)S(1)}, bf16[64,1024]{1,0:T(8,128)(2,1)S(1)}, u32[]{:S(2)}, u32[]{:S(2)}) collective-permute-start(bf16[64,1024]{1,0:T(8,128)(2,1)S(1)} %get-tuple-element.65), channel_id=1, source_target_pairs={{0,4},{4,0},{8,12},{12,8},{1,5},{5,1},{9,13},{13,9},{2,6},{6,2},{1... | collective-permute-start | bytes 393224 | tf_op jit(solution)/shard_map/ppermute | solution.py:548
  18.9 23.8 %slice-start.4 = ((s8[14680064]{0:T(1024)(128)(4,1)}), s8[4194304]{0:T(1024)(128)(4,1)S(1)}, s32[]{:S(2)}) async-start(s8[14680064]{0:T(1024)(128)(4,1)} %bitcast.4), calls=%async_computation.4 | async-start | bytes 8388608
  18.9 23.8 %slice-start.5 = ((s8[14680064]{0:T(1024)(128)(4,1)}), s8[4194304]{0:T(1024)(128)(4,1)S(1)}, s32[]{:S(2)}) async-start(s8[14680064]{0:T(1024)(128)(4,1)} %bitcast.4), calls=%async_computation.5 | async-start | bytes 8388608
  23.1 12.2 %collective-permute-start.4 = (bf16[64,1024]{1,0:T(8,128)(2,1)S(1)}, bf16[64,1024]{1,0:T(8,128)(2,1)S(1)}, u32[]{:S(2)}, u32[]{:S(2)}) collective-permute-start(bf16[64,1024]{1,0:T(8,128)(2,1)S(1)} %shard_map.122.refs_0_), channel_id=1, source_target_pairs={{0,8},{4,12},{8,0},{12,4},{1,9},{5,13},{9,1},{13,5},{2,10},{6,14},... | collective-permute-start | bytes 393224 | tf_op jit(solution)/shard_map/ppermute | solution.py:560
  26.3 13.0 %copy-start = (bf16[2,64,2048]{2,1,0:T(8,128)(2,1)S(1)}, bf16[2,64,2048]{2,1,0:T(8,128)(2,1)}, u32[]{:S(2)}) copy-start(bf16[2,64,2048]{2,1,0:T(8,128)(2,1)} %refs_2_.3) | copy-start | bytes 1572868
  26.3 16.4 %slice-start.6 = ((s8[14680064]{0:T(1024)(128)(4,1)}), s8[4194304]{0:T(1024)(128)(4,1)S(1)}, s32[]{:S(2)}) async-start(s8[14680064]{0:T(1024)(128)(4,1)} %bitcast.4), calls=%async_computation.6 | async-start | bytes 8388608
  26.3 16.4 %slice-start.7 = ((s8[14680064]{0:T(1024)(128)(4,1)}), s8[2097152]{0:T(1024)(128)(4,1)S(1)}, s32[]{:S(2)}) async-start(s8[14680064]{0:T(1024)(128)(4,1)} %bitcast.4), calls=%async_computation.7 | async-start | bytes 4194304
  26.3 10.8 %collective-permute-start.6 = (bf16[64,1024]{1,0:T(8,128)(2,1)S(1)}, bf16[64,1024]{1,0:T(8,128)(2,1)S(1)}, u32[]{:S(2)}, u32[]{:S(2)}) collective-permute-start(bf16[64,1024]{1,0:T(8,128)(2,1)S(1)} %shard_map.123.refs_0_), channel_id=1, source_target_pairs={{0,8},{4,12},{8,0},{12,4},{1,9},{5,13},{9,1},{13,5},{2,10},{6,14},... | collective-permute-start | bytes 393224 | tf_op jit(solution)/shard_map/ppermute | solution.py:560
  37.2 8.2 %collective-permute-start.8 = (bf16[64,1024]{1,0:T(8,128)(2,1)S(1)}, bf16[64,1024]{1,0:T(8,128)(2,1)S(1)}, u32[]{:S(2)}, u32[]{:S(2)}) collective-permute-start(bf16[64,1024]{1,0:T(8,128)(2,1)S(1)} %shard_map.126.refs_1_), channel_id=1, source_target_pairs={{0,4},{4,0},{8,12},{12,8},{1,5},{5,1},{9,13},{13,9},{2,6},{6,2},{1... | collective-permute-start | bytes 393224 | tf_op jit(solution)/shard_map/ppermute | solution.py:548
  37.7 7.7 %collective-permute-start.7 = (bf16[64,1024]{1,0:T(8,128)(2,1)S(1)}, bf16[64,1024]{1,0:T(8,128)(2,1)S(1)}, u32[]{:S(2)}, u32[]{:S(2)}) collective-permute-start(bf16[64,1024]{1,0:T(8,128)(2,1)S(1)} %shard_map.125.refs_0_), channel_id=1, source_target_pairs={{0,4},{4,0},{8,12},{12,8},{1,5},{5,1},{9,13},{13,9},{2,6},{6,2},{1... | collective-permute-start | bytes 393224 | tf_op jit(solution)/shard_map/ppermute | solution.py:548
  40.0 1.2 %collective-permute-start.9 = (f32[8,128]{1,0:T(8,128)S(1)}, f32[8,128]{1,0:T(8,128)S(1)}, u32[]{:S(2)}, u32[]{:S(2)}) collective-permute-start(f32[8,128]{1,0:T(8,128)S(1)} %get-tuple-element.73.refs_0_), channel_id=1, source_target_pairs={{0,1},{1,0},{2,3},{3,2},{4,5},{5,4},{6,7},{7,6},{8,9},{9,8},{10,11... | collective-permute-start | bytes 12296 | tf_op jit(solution)/shard_map/ppermute | solution.py:546
  41.3 4.1 %collective-permute-start.10 = (f32[8,128]{1,0:T(8,128)S(1)}, f32[8,128]{1,0:T(8,128)S(1)}, u32[]{:S(2)}, u32[]{:S(2)}) collective-permute-start(f32[8,128]{1,0:T(8,128)S(1)} %shard_map.129.refs_0_), channel_id=1, source_target_pairs={{0,2},{1,3},{2,0},{3,1},{4,6},{5,7},{6,4},{7,5},{8,10},{9,11},{10,... | collective-permute-start | bytes 12296 | tf_op jit(solution)/shard_map/ppermute | solution.py:547
  48.1 1.6 %collective-permute-start.11 = (bf16[64,1792]{1,0:T(8,128)(2,1)S(1)}, bf16[64,1792]{1,0:T(8,128)(2,1)S(1)}, u32[]{:S(2)}, u32[]{:S(2)}) collective-permute-start(bf16[64,1792]{1,0:T(8,128)(2,1)S(1)} %get-tuple-element.80), channel_id=1, source_target_pairs={{0,1},{1,0},{2,3},{3,2},{4,5},{5,4},{6,7},{7,6},{8,9},{9,8},{10,11... | collective-permute-start | bytes 688136 | tf_op jit(solution)/shard_map/ppermute | solution.py:546
  48.2 2.5 %collective-permute-start.13 = (bf16[64,1792]{1,0:T(8,128)(2,1)S(1)}, bf16[64,1792]{1,0:T(8,128)(2,1)S(1)}, u32[]{:S(2)}, u32[]{:S(2)}) collective-permute-start(bf16[64,1792]{1,0:T(8,128)(2,1)S(1)} %get-tuple-element.81), channel_id=1, source_target_pairs={{0,1},{1,0},{2,3},{3,2},{4,5},{5,4},{6,7},{7,6},{8,9},{9,8},{10,11... | collective-permute-start | bytes 688136 | tf_op jit(solution)/shard_map/ppermute | solution.py:546
  49.7 8.5 %collective-permute-start.12 = (bf16[64,1792]{1,0:T(8,128)(2,1)S(1)}, bf16[64,1792]{1,0:T(8,128)(2,1)S(1)}, u32[]{:S(2)}, u32[]{:S(2)}) collective-permute-start(bf16[64,1792]{1,0:T(8,128)(2,1)S(1)} %shard_map.133), channel_id=1, source_target_pairs={{0,2},{1,3},{2,0},{3,1},{4,6},{5,7},{6,4},{7,5},{8,10},{9,11},{10,... | collective-permute-start | bytes 688136 | tf_op jit(solution)/shard_map/ppermute | solution.py:547
  50.6 9.2 %slice-start = ((s8[14680064]{0:T(1024)(128)(4,1)}), s8[4194304]{0:T(1024)(128)(4,1)S(1)}, s32[]{:S(2)}) async-start(s8[14680064]{0:T(1024)(128)(4,1)} %bitcast.2), calls=%async_computation | async-start | bytes 8388608
  50.7 9.2 %slice-start.1 = ((s8[14680064]{0:T(1024)(128)(4,1)}), s8[4194304]{0:T(1024)(128)(4,1)S(1)}, s32[]{:S(2)}) async-start(s8[14680064]{0:T(1024)(128)(4,1)} %bitcast.2), calls=%async_computation.1 | async-start | bytes 8388608
  50.7 9.2 %slice-start.2 = ((s8[14680064]{0:T(1024)(128)(4,1)}), s8[4194304]{0:T(1024)(128)(4,1)S(1)}, s32[]{:S(2)}) async-start(s8[14680064]{0:T(1024)(128)(4,1)} %bitcast.2), calls=%async_computation.2 | async-start | bytes 8388608
  50.7 9.1 %slice-start.3 = ((s8[14680064]{0:T(1024)(128)(4,1)}), s8[2097152]{0:T(1024)(128)(4,1)S(1)}, s32[]{:S(2)}) async-start(s8[14680064]{0:T(1024)(128)(4,1)} %bitcast.2), calls=%async_computation.3 | async-start | bytes 4194304
  52.7 5.5 %collective-permute-start.14 = (bf16[64,1792]{1,0:T(8,128)(2,1)S(1)}, bf16[64,1792]{1,0:T(8,128)(2,1)S(1)}, u32[]{:S(2)}, u32[]{:S(2)}) collective-permute-start(bf16[64,1792]{1,0:T(8,128)(2,1)S(1)} %get-tuple-element.84), channel_id=1, source_target_pairs={{0,1},{1,0},{2,3},{3,2},{4,5},{5,4},{6,7},{7,6},{8,9},{9,8},{10,11... | collective-permute-start | bytes 688136 | tf_op jit(solution)/shard_map/ppermute | solution.py:546
  52.8 5.4 %collective-permute-start.15 = (bf16[64,1792]{1,0:T(8,128)(2,1)S(1)}, bf16[64,1792]{1,0:T(8,128)(2,1)S(1)}, u32[]{:S(2)}, u32[]{:S(2)}) collective-permute-start(bf16[64,1792]{1,0:T(8,128)(2,1)S(1)} %get-tuple-element.85), channel_id=1, source_target_pairs={{0,1},{1,0},{2,3},{3,2},{4,5},{5,4},{6,7},{7,6},{8,9},{9,8},{10,11... | collective-permute-start | bytes 688136 | tf_op jit(solution)/shard_map/ppermute | solution.py:546
  53.3 9.6 %collective-permute-start.18 = (bf16[64,1792]{1,0:T(8,128)(2,1)S(1)}, bf16[64,1792]{1,0:T(8,128)(2,1)S(1)}, u32[]{:S(2)}, u32[]{:S(2)}) collective-permute-start(bf16[64,1792]{1,0:T(8,128)(2,1)S(1)} %shard_map.134), channel_id=1, source_target_pairs={{0,2},{1,3},{2,0},{3,1},{4,6},{5,7},{6,4},{7,5},{8,10},{9,11},{10,... | collective-permute-start | bytes 688136 | tf_op jit(solution)/shard_map/ppermute | solution.py:547
  54.5 3.7 %collective-permute-start.16 = (f32[8,128]{1,0:T(8,128)S(1)}, f32[8,128]{1,0:T(8,128)S(1)}, u32[]{:S(2)}, u32[]{:S(2)}) collective-permute-start(f32[8,128]{1,0:T(8,128)S(1)} %shard_map.130.refs_0_), channel_id=1, source_target_pairs={{0,4},{4,0},{8,12},{12,8},{1,5},{5,1},{9,13},{13,9},{2,6},{6,2},{1... | collective-permute-start | bytes 12296 | tf_op jit(solution)/shard_map/ppermute | solution.py:548
  58.4 1.4 %collective-permute-start.19 = (bf16[64,896]{1,0:T(8,128)(2,1)S(1)}, bf16[64,896]{1,0:T(8,128)(2,1)S(1)}, u32[]{:S(2)}, u32[]{:S(2)}) collective-permute-start(bf16[64,896]{1,0:T(8,128)(2,1)S(1)} %shard_map.136.mine_ref), channel_id=1, source_target_pairs={{0,1},{1,0},{2,3},{3,2},{4,5},{5,4},{6,7},{7,6},{8,9},{9,8},{10,11... | collective-permute-start | bytes 344072 | tf_op jit(solution)/shard_map/ppermute | solution.py:546
  58.5 6.2 %collective-permute-start.17 = (bf16[64,896]{1,0:T(8,128)(2,1)S(1)}, bf16[64,896]{1,0:T(8,128)(2,1)S(1)}, u32[]{:S(2)}, u32[]{:S(2)}) collective-permute-start(bf16[64,896]{1,0:T(8,128)(2,1)S(1)} %shard_map.136.mine_ref), channel_id=1, source_target_pairs={{0,2},{1,3},{2,0},{3,1},{4,6},{5,7},{6,4},{7,5},{8,10},{9,11},{10,... | collective-permute-start | bytes 344072 | tf_op jit(solution)/shard_map/ppermute | solution.py:547
  63.2 2.5 %collective-permute-start.21 = (bf16[64,896]{1,0:T(8,128)(2,1)S(1)}, bf16[64,896]{1,0:T(8,128)(2,1)S(1)}, u32[]{:S(2)}, u32[]{:S(2)}) collective-permute-start(bf16[64,896]{1,0:T(8,128)(2,1)S(1)} %shard_map.139.mine_ref), channel_id=1, source_target_pairs={{0,1},{1,0},{2,3},{3,2},{4,5},{5,4},{6,7},{7,6},{8,9},{9,8},{10,11... | collective-permute-start | bytes 344072 | tf_op jit(solution)/shard_map/ppermute | solution.py:546
  64.8 3.5 %collective-permute-start.20 = (bf16[64,896]{1,0:T(8,128)(2,1)S(1)}, bf16[64,896]{1,0:T(8,128)(2,1)S(1)}, u32[]{:S(2)}, u32[]{:S(2)}) collective-permute-start(bf16[64,896]{1,0:T(8,128)(2,1)S(1)} %collective-permute-done.17.mine_ref), channel_id=1, source_target_pairs={{0,1},{1,0},{2,3},{3,2},{4,5},{5,4},{6,7},{7,6},{8,9},{9,8},{10,11... | collective-permute-start | bytes 344072 | tf_op jit(solution)/shard_map/ppermute | solution.py:546
  64.8 5.6 %collective-permute-start.23 = (bf16[64,896]{1,0:T(8,128)(2,1)S(1)}, bf16[64,896]{1,0:T(8,128)(2,1)S(1)}, u32[]{:S(2)}, u32[]{:S(2)}) collective-permute-start(bf16[64,896]{1,0:T(8,128)(2,1)S(1)} %shard_map.139.mine_ref), channel_id=1, source_target_pairs={{0,2},{1,3},{2,0},{3,1},{4,6},{5,7},{6,4},{7,5},{8,10},{9,11},{10,... | collective-permute-start | bytes 344072 | tf_op jit(solution)/shard_map/ppermute | solution.py:547
  70.3 1.7 %collective-permute-start.24 = (bf16[64,896]{1,0:T(8,128)(2,1)S(1)}, bf16[64,896]{1,0:T(8,128)(2,1)S(1)}, u32[]{:S(2)}, u32[]{:S(2)}) collective-permute-start(bf16[64,896]{1,0:T(8,128)(2,1)S(1)} %collective-permute-done.23.mine_ref), channel_id=1, source_target_pairs={{0,1},{1,0},{2,3},{3,2},{4,5},{5,4},{6,7},{7,6},{8,9},{9,8},{10,11... | collective-permute-start | bytes 344072 | tf_op jit(solution)/shard_map/ppermute | solution.py:546
  71.7 6.4 %collective-permute-start.22 = (bf16[64,1024]{1,0:T(8,128)(2,1)S(1)}, bf16[64,1024]{1,0:T(8,128)(2,1)S(1)}, u32[]{:S(2)}, u32[]{:S(2)}) collective-permute-start(bf16[64,1024]{1,0:T(8,128)(2,1)S(1)} %shard_map.143), channel_id=1, source_target_pairs={{0,4},{4,0},{8,12},{12,8},{1,5},{5,1},{9,13},{13,9},{2,6},{6,2},{1... | collective-permute-start | bytes 393224 | tf_op jit(solution)/shard_map/ppermute | solution.py:548
  73.3 7.6 %collective-permute-start.27 = (bf16[64,1024]{1,0:T(8,128)(2,1)S(1)}, bf16[64,1024]{1,0:T(8,128)(2,1)S(1)}, u32[]{:S(2)}, u32[]{:S(2)}) collective-permute-start(bf16[64,1024]{1,0:T(8,128)(2,1)S(1)} %shard_map.144), channel_id=1, source_target_pairs={{0,4},{4,0},{8,12},{12,8},{1,5},{5,1},{9,13},{13,9},{2,6},{6,2},{1... | collective-permute-start | bytes 393224 | tf_op jit(solution)/shard_map/ppermute | solution.py:548
  78.1 12.4 %collective-permute-start.25 = (bf16[64,1024]{1,0:T(8,128)(2,1)S(1)}, bf16[64,1024]{1,0:T(8,128)(2,1)S(1)}, u32[]{:S(2)}, u32[]{:S(2)}) collective-permute-start(bf16[64,1024]{1,0:T(8,128)(2,1)S(1)} %shard_map.145.refs_0_), channel_id=1, source_target_pairs={{0,8},{4,12},{8,0},{12,4},{1,9},{5,13},{9,1},{13,5},{2,10},{6,14},... | collective-permute-start | bytes 393224 | tf_op jit(solution)/shard_map/ppermute | solution.py:560
  81.0 11.3 %collective-permute-start.28 = (bf16[64,1024]{1,0:T(8,128)(2,1)S(1)}, bf16[64,1024]{1,0:T(8,128)(2,1)S(1)}, u32[]{:S(2)}, u32[]{:S(2)}) collective-permute-start(bf16[64,1024]{1,0:T(8,128)(2,1)S(1)} %shard_map.148.refs_0_), channel_id=1, source_target_pairs={{0,8},{4,12},{8,0},{12,4},{1,9},{5,13},{9,1},{13,5},{2,10},{6,14},... | collective-permute-start | bytes 393224 | tf_op jit(solution)/shard_map/ppermute | solution.py:560
  90.5 6.3 %collective-permute-start.26 = (bf16[64,1024]{1,0:T(8,128)(2,1)S(1)}, bf16[64,1024]{1,0:T(8,128)(2,1)S(1)}, u32[]{:S(2)}, u32[]{:S(2)}) collective-permute-start(bf16[64,1024]{1,0:T(8,128)(2,1)S(1)} %shard_map.146.refs_2_), channel_id=1, source_target_pairs={{0,4},{4,0},{8,12},{12,8},{1,5},{5,1},{9,13},{13,9},{2,6},{6,2},{1... | collective-permute-start | bytes 393224 | tf_op jit(solution)/shard_map/ppermute | solution.py:548
  92.3 5.8 %collective-permute-start.29 = (bf16[64,1024]{1,0:T(8,128)(2,1)S(1)}, bf16[64,1024]{1,0:T(8,128)(2,1)S(1)}, u32[]{:S(2)}, u32[]{:S(2)}) collective-permute-start(bf16[64,1024]{1,0:T(8,128)(2,1)S(1)} %shard_map.149.refs_4_), channel_id=1, source_target_pairs={{0,4},{4,0},{8,12},{12,8},{1,5},{5,1},{9,13},{13,9},{2,6},{6,2},{1... | collective-permute-start | bytes 393224 | tf_op jit(solution)/shard_map/ppermute | solution.py:548

commit v4 on v3

v4 whole, which is shorter than its diff:
```python
import functools

import jax
import jax.numpy as jnp
from jax import lax
from jax.experimental import pallas as pl
from jax.experimental.pallas import tpu as pltpu
from jax.sharding import PartitionSpec as P

BF16 = jnp.bfloat16
F32 = jnp.float32
MIB = 1 << 20


def add(a, b):
    return (a.astype(F32) + b.astype(F32)).astype(BF16)


def sum_kernel(dtype, *refs):
    total = functools.reduce(jnp.add, [ref[...].astype(F32) for ref in refs[:-1]])
    refs[-1][...] = total.astype(dtype)


def total_of(*terms, dtype=BF16):
    vmem = pl.BlockSpec(memory_space=pltpu.VMEM)
    return pl.pallas_call(
        functools.partial(sum_kernel, dtype),
        in_specs=[vmem] * len(terms),
        out_specs=vmem,
        out_shape=jax.ShapeDtypeStruct(terms[0].shape, dtype),
        cost_estimate=cost(terms[0].size, 4 * terms[0].size),
        compiler_params=pltpu.CompilerParams(vmem_limit_bytes=2 * MIB),
    )(*terms)


def cost(flops, read):
    return pl.CostEstimate(flops=flops // 1000, bytes_accessed=read // 1000, transcendentals=0)


PART = 256
LANES = 128


def attend(base, len_ref, q_ref, nk_ref, nv_ref, k_buf, v_buf, out_buf, wait):
    steps = q_ref.shape[0]
    count, copies, slots, head = k_buf.shape
    group = q_ref.shape[2] // (copies * head)
    rows = steps * group
    batch = 4
    scaling = head ** (-0.5)
    slot = lax.broadcasted_iota(jnp.int32, (rows, slots), 1)
    step = lax.broadcasted_iota(jnp.int32, (rows, 1), 0) // group
    for b0 in range(0, count, batch):
        seqs = range(b0, min(b0 + batch, count))
        work = [(b, g) for b in seqs for g in range(copies)]
        asked, recent = [], []
        for b, g in work:
            at = base + b
            pick = [
                q_ref[s, at : at + 1, (g * group + j) * head : (g * group + j + 1) * head]
                for s in range(steps)
                for j in range(group)
            ]
            wide = jnp.concatenate([p.astype(F32) for p in pick], axis=0)
            asked.append(wide.astype(BF16))
            found = []
            for r in range(steps):
                key = nk_ref[r, at, g : g + 1, :].astype(F32)
                score = jnp.sum(wide * key, axis=1, keepdims=True) * scaling
                found.append(jnp.where(step >= r, score, -jnp.inf))
            recent.append(found)
        for b in seqs:
            wait(b)
        alive = {
            b: slot < jnp.broadcast_to(len_ref[base + b : base + b + 1, :1], (rows, slots))
            for b in seqs
        }
        scores = [
            lax.dot_general(q, k_buf[b, g], (((1,), (1,)), ((), ())), preferred_element_type=F32)
            for q, (b, g) in zip(asked, work)
        ]
        scores = [
            jnp.where(alive[b], s * scaling, -jnp.inf) for s, (b, g) in zip(scores, work)
        ]
        tops = [
            functools.reduce(jnp.maximum, [jnp.max(s, axis=1, keepdims=True)] + found)
            for s, found in zip(scores, recent)
        ]
        weights = [jnp.exp(s - top) for s, top in zip(scores, tops)]
        fresh = [[jnp.exp(x - top) for x in found] for found, top in zip(recent, tops)]
        totals = [jnp.sum(w, axis=1, keepdims=True) + sum(f) for w, f in zip(weights, fresh)]
        blends = [
            jnp.dot(w.astype(BF16), v_buf[b, g], preferred_element_type=F32)
            for w, (b, g) in zip(weights, work)
        ]
        for (b, g), blend, f, total in zip(work, blends, fresh, totals):
            for r in range(steps):
                value = nv_ref[r, base + b, g : g + 1, :].astype(F32)
                blend = blend + f[r].astype(BF16).astype(F32) * value
            out = blend / total
            for s in range(steps):
                for j in range(group):
                    cols = slice((g * group + j) * head, (g * group + j + 1) * head)
                    at = s * count + b
                    out_buf[at : at + 1, cols] = out[s * group + j : s * group + j + 1, :]


def first_attention(len_hbm, q_hbm, nk_hbm, nv_hbm, k_hbm, v_hbm, *refs):
    o_ref, lens_ref, q_ref, nk_ref, nv_ref, k_next, v_next = refs[:7]
    len_ref, k_buf, v_buf, out_buf, sem, small_sem = refs[7:]
    count, copies, slots, head = k_buf.shape
    ends = ((len_hbm, len_ref), (q_hbm, q_ref), (nk_hbm, nk_ref), (nv_hbm, nv_ref))
    small = [
        pltpu.make_async_copy(src, dst, small_sem.at[k]) for k, (src, dst) in enumerate(ends)
    ]

    def moves(b, c):
        here = pl.ds(c * PART, PART)
        k_to, v_to = (k_buf, v_buf) if b < count else (k_next, v_next)
        return (
            pltpu.make_async_copy(k_hbm.at[b, :, here], k_to.at[b % count, :, here], sem.at[0, b]),
            pltpu.make_async_copy(v_hbm.at[b, :, here], v_to.at[b % count, :, here], sem.at[1, b]),
        )

    def start(b, c):
        for move in moves(b, c):
            move.start()

    def clear(b, c):
        v_to = v_buf if b < count else v_next
        v_to[b % count, :, c * PART : (c + 1) * PART] = jnp.zeros((copies, PART, head), BF16)

    def wait_part(b, c):
        for move in moves(b, c):
            move.wait()

    def wait(b):
        wait_part(b, 0)
        for c in range(1, slots // PART):
            pl.when(len_ref[b] > c * PART)(functools.partial(wait_part, b, c))

    for move in small:
        move.start()
    start(0, 0)
    small[0].wait()
    for b in range(2 * count):
        if b:
            start(b, 0)
        for c in range(1, slots // PART):
            live = len_ref[b] > c * PART
            pl.when(live)(functools.partial(start, b, c))
            pl.when(jnp.logical_not(live))(functools.partial(clear, b, c))
        lens_ref[b : b + 1, :] = jnp.full((1, lens_ref.shape[1]), len_ref[b], jnp.int32)
    for move in small[1:]:
        move.wait()
    attend(0, lens_ref, q_ref, nk_ref, nv_ref, k_buf, v_buf, out_buf, wait)
    o_ref[...] = out_buf[...].astype(BF16)
    for b in range(count, 2 * count):
        wait(b)


def second_attention(lens_ref, q_ref, nk_ref, nv_ref, k_ref, v_ref, o_ref, out_buf):
    none = lambda b: None
    attend(k_ref.shape[0], lens_ref, q_ref, nk_ref, nv_ref, k_ref, v_ref, out_buf, none)
    o_ref[...] = out_buf[...].astype(BF16)


def attention_first(queries, new_keys, new_values, key_cache, value_cache, lengths):
    steps, seqs, deep = queries.shape
    _, copies, slots, head = key_cache.shape
    count = seqs // 2
    vmem = pl.BlockSpec(memory_space=pltpu.VMEM)
    hbm = pl.BlockSpec(memory_space=pl.ANY)
    buffer = pltpu.VMEM((count, copies, slots, head), BF16)
    moved = [lengths, queries, new_keys, new_values, key_cache, value_cache]
    moved = [pltpu.with_memory_space_constraint(x, pltpu.HBM) for x in moved]
    heads, *carried = pl.pallas_call(
        first_attention,
        in_specs=[hbm] * 6,
        out_specs=[vmem] * 7,
        out_shape=[
            pltpu.VMEM((steps * count, deep), BF16),
            pltpu.VMEM((seqs, 128), jnp.int32),
            pltpu.VMEM(queries.shape, BF16),
            pltpu.VMEM(new_keys.shape, BF16),
            pltpu.VMEM(new_values.shape, BF16),
            buffer,
            buffer,
        ],
        scratch_shapes=[
            pltpu.SMEM(lengths.shape, lengths.dtype),
            buffer,
            buffer,
            pltpu.VMEM((steps * count, deep), F32),
            pltpu.SemaphoreType.DMA((2, seqs)),
            pltpu.SemaphoreType.DMA((4,)),
        ],
        cost_estimate=cost(2 * seqs * slots * deep, 8 * count * copies * slots * head),
        compiler_params=pltpu.CompilerParams(vmem_limit_bytes=12 * MIB),
    )(*moved)
    return heads, carried


def attention_second(carried):
    lens, queries, new_keys, new_values, keys, values = carried
    steps, seqs, deep = queries.shape
    count = seqs // 2
    vmem = pl.BlockSpec(memory_space=pltpu.VMEM)
    return pl.pallas_call(
        second_attention,
        in_specs=[vmem] * 6,
        out_specs=vmem,
        out_shape=jax.ShapeDtypeStruct((steps * count, deep), BF16),
        scratch_shapes=[pltpu.VMEM((steps * count, deep), F32)],
        cost_estimate=cost(2 * seqs * keys.shape[2] * deep, 2 * keys.size),
        compiler_params=pltpu.CompilerParams(vmem_limit_bytes=4 * MIB),
    )(*carried)


def fetch_kernel(pieces, where_ref, src_ref, *refs):
    o_refs, sem = refs[-3:-1], refs[-1]
    length = o_refs[0].shape[0]
    step = length // pieces
    moves = []
    for flip, o_ref in enumerate(o_refs):
        for k in range(pieces):
            at = pl.multiple_of((where_ref[1] ^ flip) * length + k * step, 16)
            moves.append(
                pltpu.make_async_copy(
                    src_ref.at[pl.ds(at, step)], o_ref.at[pl.ds(k * step, step)], sem.at[flip, k]
                )
            )
    for move in moves:
        move.start()
    for move in moves:
        move.wait()


def fetch(where, weight, after):
    src = pltpu.with_memory_space_constraint(weight, pltpu.HBM)
    hbm = pl.BlockSpec(memory_space=pl.ANY)
    pieces = 4
    half = pltpu.VMEM((weight.shape[0] // 2, weight.shape[1]), weight.dtype)
    return pl.pallas_call(
        functools.partial(fetch_kernel, pieces),
        in_specs=[pl.BlockSpec(memory_space=pltpu.SMEM)] + [hbm] * (1 + len(after)),
        out_specs=[pl.BlockSpec(memory_space=pltpu.VMEM)] * 2,
        out_shape=[half] * 2,
        scratch_shapes=[pltpu.SemaphoreType.DMA((2, pieces))],
        cost_estimate=cost(0, weight.size),
        compiler_params=pltpu.CompilerParams(vmem_limit_bytes=1 * MIB),
    )(where, src, *after)


def half_of(where_ref, flip, length):
    return pl.ds(pl.multiple_of((where_ref[1] ^ flip) * length, 128), length)


def product_kernel(flips, where_ref, *refs):
    bufs, refs = refs[-1], refs[:-1]
    w_ref, o_refs = refs[-1 - len(flips)], refs[-len(flips) :]
    for n, flip in enumerate(flips):
        count = refs[0].shape[0]
        buf = bufs.at[n]
        for k, block_ref in enumerate(refs[4 * n : 4 * n + 4]):
            at = pl.multiple_of((where_ref[0] ^ k) * count, count)
            buf[pl.ds(at, count), :] = block_ref[...]
        cols = half_of(where_ref, flip, o_refs[n].shape[1])
        out = jnp.dot(buf[...], w_ref[:, cols], preferred_element_type=F32)
        o_refs[n][...] = out.astype(BF16)


def product(where, w, *jobs):
    count, deep = jobs[0][0][0].shape
    wide = w.shape[1] // 2
    blocks = [block for job in jobs for block in job[0]]
    vmem = pl.BlockSpec(memory_space=pltpu.VMEM)
    return pl.pallas_call(
        functools.partial(product_kernel, [flip for _, flip in jobs]),
        in_specs=[pl.BlockSpec(memory_space=pltpu.SMEM)] + [vmem] * (len(blocks) + 1),
        out_specs=[vmem] * len(jobs),
        out_shape=[jax.ShapeDtypeStruct((4 * count, wide), BF16)] * len(jobs),
        scratch_shapes=[pltpu.VMEM((len(jobs), 4 * count, deep), BF16)],
        cost_estimate=cost(8 * count * deep * wide, 2 * deep * wide),
        compiler_params=pltpu.CompilerParams(vmem_limit_bytes=4 * MIB),
    )(where, *blocks, w)


def middle_kernel(flip, groups, where_ref, *refs):
    attn_refs, (res_ref, gain_ref, mid_ref, normed_ref) = refs[:groups], refs[groups : groups + 4]
    steps = res_ref.shape[0]
    rows, wide = mid_ref.shape
    count = rows // (steps * 4)
    some = count // groups
    cols = half_of(where_ref, flip, wide)
    blocks = [
        res_ref[s, d * count : (d + 1) * count, cols].astype(F32)
        for d in range(4)
        for s in range(steps)
    ]
    parts = [block[n * some : (n + 1) * some] for n in range(groups) for block in blocks]
    attn = jnp.concatenate([ref[...].astype(F32) for ref in attn_refs], axis=0)
    mid = (jnp.concatenate(parts, axis=0) + attn).astype(BF16)
    whole = mid.astype(F32)
    mid_ref[...] = mid
    normed_ref[...] = (whole * gain_ref[:1, cols].astype(F32)).astype(BF16)
    for sq_ref in refs[groups + 4 :]:
        sq_ref[...] = jnp.broadcast_to(jnp.sum(whole * whole, axis=1, keepdims=True), sq_ref.shape)


def middle_part(where, flip, attn, residual, gain):
    rows, wide = attn[0].shape[0] * len(attn), attn[0].shape[1]
    vmem = pl.BlockSpec(memory_space=pltpu.VMEM)
    outs = [jax.ShapeDtypeStruct((rows, wide), BF16)] * 2
    outs.append(jax.ShapeDtypeStruct((rows, LANES), F32))
    return pl.pallas_call(
        functools.partial(middle_kernel, flip, len(attn)),
        in_specs=[pl.BlockSpec(memory_space=pltpu.SMEM)] + [vmem] * (len(attn) + 2),
        out_specs=[vmem] * len(outs),
        out_shape=outs,
        cost_estimate=cost(8 * rows * wide, 8 * rows * wide),
        compiler_params=pltpu.CompilerParams(vmem_limit_bytes=6 * MIB),
    )(where, *attn, residual, gain)


def first_kernel(wide, where_ref, x_ref, g_ref, u_ref, o_ref):
    deep, all_rows = half_of(where_ref, 0, x_ref.shape[1]), slice(None)
    length = g_ref.shape[1]
    for k, w_ref in enumerate((g_ref, u_ref)):
        for at in range(0, length, wide):
            here = slice(at, at + wide)
            out = jnp.dot(x_ref[...], w_ref[deep if k else all_rows, here], preferred_element_type=F32)
            o_ref[:, k * length + at : k * length + at + wide] = out


def gate_up_first(where, x, weights):
    rows, deep = x.shape
    length = weights[0].shape[1]
    vmem = pl.BlockSpec(memory_space=pltpu.VMEM)
    return pl.pallas_call(
        functools.partial(first_kernel, length // 7),
        in_specs=[pl.BlockSpec(memory_space=pltpu.SMEM)] + [vmem] * 3,
        out_specs=vmem,
        out_shape=jax.ShapeDtypeStruct((rows, 2 * length), F32),
        cost_estimate=cost(4 * rows * deep * length, 4 * deep * length),
        compiler_params=pltpu.CompilerParams(vmem_limit_bytes=4 * MIB),
    )(where, x, *weights)


def packed(whole):
    high = whole.astype(BF16).astype(F32)
    middle = (whole - high).astype(BF16).astype(F32)
    low = whole - high - middle
    lane = lax.broadcasted_iota(jnp.int32, whole.shape, 1)
    third = LANES // 4
    return jnp.where(lane < third, high, jnp.where(lane < 2 * third, middle, low)).astype(BF16)


def unpacked(ref):
    start = ref.shape[1] - LANES
    parts = [ref[:, start + k * (LANES // 4) :][:, :1].astype(F32) for k in range(3)]
    return parts[0] + parts[1] + parts[2]


def second_kernel(chip, groups, where_ref, x_ref, f_ref, sq_ref, g_ref, u_ref, *refs):
    give_refs, (keep_ref, buf) = refs[:groups], refs[groups:]
    for n, give_ref in enumerate(give_refs):
        some = give_ref.shape[0]
        give_ref[:, keep_ref.shape[1] :] = packed(sq_ref[n * some : (n + 1) * some, :])
    me = where_ref[0]
    deep, all_rows = half_of(where_ref, 1, x_ref.shape[1]), slice(None)
    length = g_ref.shape[1]
    own = length // 4
    rows = give_refs[0].shape[0]
    start = pl.multiple_of(((me // 2) ^ chip) * (2 * own), 128)
    for k, w_ref in enumerate((g_ref, u_ref)):
        out = jnp.dot(x_ref[...], w_ref[deep if k else all_rows, pl.ds(start, 2 * own)], preferred_element_type=F32)
        buf[...] = out + f_ref[:, pl.ds(pl.multiple_of(k * length + start, 128), 2 * own)]
        mine = pl.ds(pl.multiple_of((me % 2) * own, 128), own)
        other = pl.ds(pl.multiple_of((1 - me % 2) * own, 128), own)
        here = slice(k * own, (k + 1) * own)
        keep_ref[:, here] = buf[:, mine]
        for n, give_ref in enumerate(give_refs):
            give_ref[:, here] = buf[n * rows : (n + 1) * rows, other].astype(BF16)


def gate_up_second(where, x, first, sq, weights, chip, groups):
    rows, deep = x.shape
    length = weights[0].shape[1]
    own = length // 4
    vmem = pl.BlockSpec(memory_space=pltpu.VMEM)
    *give, keep = pl.pallas_call(
        functools.partial(second_kernel, chip, groups),
        in_specs=[pl.BlockSpec(memory_space=pltpu.SMEM)] + [vmem] * 5,
        out_specs=[vmem] * (groups + 1),
        out_shape=[jax.ShapeDtypeStruct((rows // groups, 2 * own + LANES), BF16)] * groups
        + [jax.ShapeDtypeStruct((rows, 2 * own), F32)],
        scratch_shapes=[pltpu.VMEM((rows, 2 * own), F32)],
        cost_estimate=cost(4 * rows * deep * 2 * own, 8 * deep * own),
        compiler_params=pltpu.CompilerParams(vmem_limit_bytes=6 * MIB),
    )(where, x, first, sq, *weights)
    return give, keep


def relay_kernel(n, keep_ref, got_ref, sq_ref, o_ref):
    rows, cols = got_ref.shape[0], keep_ref.shape[1]
    here = slice(n * rows, (n + 1) * rows)
    o_ref[:, :cols] = (keep_ref[here, :] + got_ref[:, :cols].astype(F32)).astype(BF16)
    o_ref[:, cols:] = packed(sq_ref[here, :] + unpacked(got_ref))


def relay(n, keep, got, sq):
    vmem = pl.BlockSpec(memory_space=pltpu.VMEM)
    return pl.pallas_call(
        functools.partial(relay_kernel, n),
        in_specs=[vmem] * 3,
        out_specs=vmem,
        out_shape=jax.ShapeDtypeStruct(got.shape, BF16),
        cost_estimate=cost(got.size, 4 * got.size),
        compiler_params=pltpu.CompilerParams(vmem_limit_bytes=2 * MIB),
    )(keep, got, sq)


def act_kernel(n, full, near_ref, got_ref, far_ref, sq_ref, o_ref):
    rows, cols = o_ref.shape
    here = slice(n * rows, (n + 1) * rows)
    total = sq_ref[here, :1] + unpacked(got_ref) + unpacked(far_ref)
    inv_norm = lax.rsqrt(total / full + 1e-05)
    both = near_ref[here, :] + got_ref[:, : 2 * cols].astype(F32)
    both = both + far_ref[:, : 2 * cols].astype(F32)
    gate = both[:, :cols] * inv_norm
    up = both[:, cols:] * inv_norm
    o_ref[...] = (gate / (1.0 + jnp.exp(-gate)) * up).astype(BF16)


def act(n, near, got, far, sq, full):
    rows, both = got.shape[0], near.shape[1]
    vmem = pl.BlockSpec(memory_space=pltpu.VMEM)
    return pl.pallas_call(
        functools.partial(act_kernel, n, full),
        in_specs=[vmem] * 4,
        out_specs=vmem,
        out_shape=jax.ShapeDtypeStruct((rows, both // 2), BF16),
        cost_estimate=cost(8 * rows * both, 8 * rows * both),
        compiler_params=pltpu.CompilerParams(vmem_limit_bytes=4 * MIB),
    )(near, got, far, sq)


def final_kernel(groups, where_ref, *refs):
    mid_refs, ffn_refs, o_ref = refs[:2], refs[2:-1], refs[-1]
    steps = o_ref.shape[0]
    rows, wide = ffn_refs[0].shape
    some = rows // (steps * 4)
    count = some * groups
    for flip in range(2):
        cols = half_of(where_ref, flip, wide)
        outs = [
            mid_refs[flip][n * rows : (n + 1) * rows, :].astype(F32)
            + ffn_refs[2 * n + flip][...].astype(F32)
            for n in range(groups)
        ]
        for d in range(4):
            for s in range(steps):
                at = (d * steps + s) * some
                block = jnp.concatenate([out[at : at + some] for out in outs], axis=0)
                o_ref[s, d * count : (d + 1) * count, cols] = block.astype(BF16)


def final(where, mids, groups, shape):
    vmem = pl.BlockSpec(memory_space=pltpu.VMEM)
    flat = [*mids, *(x for group in groups for x in group)]
    return pl.pallas_call(
        functools.partial(final_kernel, len(groups)),
        in_specs=[pl.BlockSpec(memory_space=pltpu.SMEM)] + [vmem] * len(flat),
        out_specs=vmem,
        out_shape=jax.ShapeDtypeStruct(shape, BF16),
        cost_estimate=cost(2 * shape[1] * shape[2], 8 * shape[1] * shape[2]),
        compiler_params=pltpu.CompilerParams(vmem_limit_bytes=6 * MIB),
    )(where, *flat)


def down_kernel(jobs, where_ref, *refs):
    bufs, refs = refs[-1], refs[:-1]
    ins, w_ref, o_refs = refs[: -1 - len(jobs)], refs[-1 - len(jobs)], refs[-len(jobs) :]
    me = where_ref[0]
    for k, (chip, flip, has_sum) in enumerate(jobs):
        mine_ref, other_ref, *sums = ins[: 2 + has_sum]
        ins = ins[2 + has_sum :]
        own = mine_ref.shape[1]
        buf = bufs.at[k]
        buf[:, pl.ds(pl.multiple_of((me % 2) * own, 128), own)] = mine_ref[...]
        buf[:, pl.ds(pl.multiple_of((1 - me % 2) * own, 128), own)] = other_ref[...]
        at = pl.ds(pl.multiple_of(((me // 2) ^ chip) * (2 * own), 128), 2 * own)
        o_ref = o_refs[k]
        cols = slice(None) if flip is None else half_of(where_ref, flip, o_ref.shape[1])
        total = jnp.dot(buf[...], w_ref[at, cols], preferred_element_type=F32)
        for ref in sums:
            total = total + ref[:, cols]
        o_ref[...] = total.astype(o_ref.dtype)


def down(where, weight, *jobs):
    args, keys, outs = [where], [], []
    for mine, other, chip, flip, total in jobs:
        args += [mine, other] + ([] if total is None else [total])
        keys.append((chip, flip, int(total is not None)))
        wide = weight.shape[1] // (1 if flip is None else 2)
        dtype = F32 if total is None else BF16
        outs.append(jax.ShapeDtypeStruct((mine.shape[0], wide), dtype))
    rows, own = jobs[0][0].shape
    vmem = pl.BlockSpec(memory_space=pltpu.VMEM)
    return pl.pallas_call(
        functools.partial(down_kernel, keys),
        in_specs=[pl.BlockSpec(memory_space=pltpu.SMEM)] + [vmem] * len(args),
        out_specs=[vmem] * len(jobs),
        out_shape=outs,
        scratch_shapes=[pltpu.VMEM((len(jobs), rows, 2 * own), BF16)],
        cost_estimate=cost(4 * rows * own * weight.shape[1], 4 * own * weight.shape[1]),
        compiler_params=pltpu.CompilerParams(vmem_limit_bytes=4 * MIB),
    )(*args, weight)


def pairs(size, step):
    return [(i, i ^ step) for i in range(size)]


def in_order(mine, other, bit, axis=0):
    first = jnp.where(bit == 0, mine, other)
    second = jnp.where(bit == 0, other, mine)
    return jnp.concatenate((first, second), axis=axis)


def levels(size):
    return [1 << k for k in range(size.bit_length() - 1)]


def gather_rows(block, size):
    me = lax.axis_index("dp")
    count, deep = block.shape
    for step in reversed(levels(size)):
        bit = (me // step) % 2
        block = in_order(block, lax.ppermute(block, "dp", pairs(size, step)), bit)
    block = block.reshape(size, count, deep)
    order = []
    for d in range(size):
        place = 0
        for step in levels(size):
            place = place * 2 + (d // step) % 2
        order.append(block[place])
    return jnp.concatenate(order, axis=0)


def sum_dp(value, size):
    for step in levels(size):
        value = value + lax.ppermute(value, "dp", pairs(size, step))
    return value


def activate(both, inv_norm):
    cols = both.shape[1] // 2
    gate = both[:, :cols] * inv_norm
    up = both[:, cols:] * inv_norm
    return (jax.nn.silu(gate) * up).astype(BF16)


def middle(resid, attn, norm_gain, dp):
    mid = add(resid, attn)
    wide = mid.astype(F32)
    squares = sum_dp(jnp.sum(wide * wide, axis=1)[None, :], dp)
    inv_norm = lax.rsqrt(squares / (mid.shape[1] * dp) + 1e-05).reshape(mid.shape[0], 1)
    normed = (wide * norm_gain.astype(F32)[None, :]).astype(BF16)
    return mid, inv_norm, normed


def plain(rows, resid, out_weight, norm_gain, gate_weight, up_weight, down_weight, dp):
    part = jnp.dot(rows, out_weight, preferred_element_type=F32).astype(BF16)
    mid, inv_norm, normed = middle(resid, lax.psum(part, "tensor"), norm_gain, dp)
    both = []
    for weight in (gate_weight, up_weight):
        term = jnp.dot(normed, weight, preferred_element_type=F32).astype(BF16)
        both.append(lax.psum_scatter(term, "dp", scatter_dimension=1, tiled=True).astype(F32))
    hidden = activate(jnp.concatenate(both, axis=1), inv_norm)
    hidden = lax.all_gather(hidden, "dp", axis=1, tiled=True)
    part = jnp.dot(hidden, down_weight, preferred_element_type=F32).astype(BF16)
    return add(mid, lax.psum(part, "tensor"))


def body(
    residual,
    queries,
    new_keys,
    new_values,
    key_cache,
    value_cache,
    lengths,
    out_weight,
    norm_gain,
    gate_weight,
    up_weight,
    down_weight,
):
    dp = lax.axis_size("dp")
    tensor = lax.axis_size("tensor")
    steps, all_seqs, width = residual.shape
    local_seqs = queries.shape[1]
    where = jnp.stack([lax.axis_index("dp"), lax.axis_index("tensor") % 2])
    where, queries = lax.optimization_barrier((where, queries))
    heads, carried = attention_first(
        queries, new_keys, new_values, key_cache, value_cache, lengths
    )
    if dp == 4 and tensor == 4:
        weights = out_weight, gate_weight, up_weight, down_weight
        gain, heads = lax.optimization_barrier((norm_gain, heads))
        return fast(where, heads, carried, residual, gain, *weights)
    heads = jnp.stack((heads, attention_second(carried)))
    heads = heads.reshape(2, steps, local_seqs // 2, -1).swapaxes(0, 1)
    heads = heads.reshape(steps * local_seqs, -1)
    row_count = steps * all_seqs
    resid = residual.reshape(steps, dp, local_seqs, width).swapaxes(0, 1)
    weights = out_weight, norm_gain, gate_weight, up_weight, down_weight
    out = plain(gather_rows(heads, dp), resid.reshape(row_count, width), *weights, dp)
    return out.reshape(dp, steps, local_seqs, width).swapaxes(0, 1).reshape(residual.shape)


def fast(where, heads, carried, residual, gain, out_w, gate_weight, up_weight, down_weight):
    width = out_w.shape[1]
    groups = 2
    core = lambda value: lax.ppermute(value, "dp", pairs(4, 1))
    across = lambda value: lax.ppermute(value, "dp", pairs(4, 2))
    swap = lambda value: lax.ppermute(value, "tensor", pairs(4, 1))
    gain = jnp.broadcast_to(gain[None, :], (16, width))
    after = lambda value, *others: lax.optimization_barrier((value, *others))[0]

    def sum_tensor(sends, keeps, during=lambda n, held: None):
        gots = [swap(send) for send in sends]
        helds, crosses = [None, None], [None, None]
        for n in range(2):
            if n:
                gots[n] = after(gots[n], helds[0])
            keep, gots[n] = keeps(n, helds[0], gots[n])
            helds[n] = total_of(keep, gots[n])
            crosses[n] = lax.ppermute(helds[n], "tensor", pairs(4, 2))
        others = [None, None]
        for n in range(2):
            beside = during(n, helds[1 - n])
            if beside is not None:
                crosses[n] = after(crosses[n], beside)
            helds[n] = total_of(helds[n], crosses[n])
            others[n] = swap(helds[n])
            if n == 0:
                crosses[1] = after(crosses[1], helds[0])
        return helds, others

    out_w, up_w, down_w = [
        pltpu.with_memory_space_constraint(w, pltpu.VMEM) for w in (out_w, up_weight, down_weight)
    ]
    far_a = across(heads)
    heads_b = attention_second(carried)
    far_a, heads_b = lax.optimization_barrier((far_a, heads_b))
    far_b = across(heads_b)
    blocks_a = [heads, core(heads), far_a, core(far_a)]
    blocks_a, gain = lax.optimization_barrier((blocks_a, gain))
    (send_a,) = product(where, out_w, (blocks_a, 1))
    far_b, send_a = lax.optimization_barrier((far_b, send_a))
    blocks_b = [heads_b, core(heads_b), far_b, core(far_b)]
    keep_a, send_b = product(where, out_w, (blocks_a, 0), (blocks_b, 1))
    gate = []

    def keeps(n, held, got):
        if n == 0:
            return keep_a, got
        return product(where, out_w, (after(blocks_b, held), 0))[0], got

    def during(n, held):
        if n == 0:
            gate.extend(fetch(where, gate_weight, [held]))
            return gate[1]

    helds, others = sum_tensor([send_a, send_b], keeps, during)
    mid, normed, sq = middle_part(where, 0, helds, residual, gain)
    first = gate_up_first(where, normed, (gate[0], up_w))
    others, first = lax.optimization_barrier((others, first))
    mid_other, normed, sq_other = middle_part(where, 1, others, residual, gain)
    sq = total_of(sq, sq_other, dtype=F32)
    weights = gate[1], up_w
    give, keep = gate_up_second(where, normed, first, sq, weights, 1, groups)
    far = [core(x) for x in give]
    relayed = [relay(n, keep, x, sq) for n, x in enumerate(far)]
    far = [across(x) for x in relayed]
    normed, relayed = lax.optimization_barrier((normed, relayed))
    give, near = gate_up_second(where, normed, first, sq, weights, 0, groups)
    got = [core(x) for x in give]
    far[0], near, got = lax.optimization_barrier((far[0], near, got))

    def activated(n):
        mine = act(n, near, got[n], far[n], sq, width * 4)
        other = core(mine)
        return mine, across(mine), other

    def early(n):
        return down(where, down_w, (mine[n], other[n], 0, None, None))[0]

    def last(n, flip, total):
        return mine_far[n], other_far[n], 1, flip, total

    mine, mine_far, other, totals, other_far = [0] * 2, [0] * 2, [0] * 2, [0] * 2, [0] * 2
    mine[0], mine_far[0], other[0] = activated(0)
    totals[0] = early(0)
    far[1] = after(far[1], totals[0])
    mine[1], mine_far[1], other[1] = activated(1)
    mine_far[0] = after(mine_far[0], mine[1])
    other_far[0] = core(mine_far[0])
    totals[1] = early(1)
    other_far[0] = after(other_far[0], totals[1])
    (send_a,) = down(where, down_w, last(0, 1, totals[0]))
    mine_far[1] = after(mine_far[1], send_a)
    other_far[1] = core(mine_far[1])
    keep_a, send_b = down(where, down_w, last(0, 0, totals[0]), last(1, 1, totals[1]))

    def keeps(n, held, got):
        if n == 0:
            return keep_a, got
        return down(where, down_w, last(1, 0, after(totals[1], held)))[0], got

    helds, others = sum_tensor([send_a, send_b], keeps)
    outs = list(zip(helds, others))
    return final(where, [mid, mid_other], outs, residual.shape)


def solution(mesh):
    in_specs = (
        P(None, "replica", "dp"),
        P(None, ("replica", "dp"), "tensor"),
        P(None, ("replica", "dp"), "tensor", None),
        P(None, ("replica", "dp"), "tensor", None),
        P(("replica", "dp"), "tensor", None, None),
        P(("replica", "dp"), "tensor", None, None),
        P(("replica", "dp")),
        P("tensor", "dp"),
        P("dp"),
        P("dp", "tensor"),
        P("dp", "tensor"),
        P("tensor", "dp"),
    )
    out_specs = P(None, "replica", "dp")
    return jax.shard_map(body, mesh=mesh, in_specs=in_specs, out_specs=out_specs, check_vma=False)
```

time: 99.9 us -> 97.2 us (0.973)
  waiting for transfers between devices: 35 us -> 31.1 us
  starting transfers between devices: 26.1 us -> 27.1 us
    ppermute x4, waiting for transfers between devices: 13.6 us -> 9.73 us  [sum_tensor(): crosses[n] = lax.ppermute(helds[n], 'tensor', pairs(4, 2))]
    ppermute x6, starting transfers between devices: 7.57 us -> 10.6 us  [fast(): across = lambda value: lax.ppermute(value, 'dp', pairs(4, 2))]
    ppermute x6, waiting for transfers between devices: 6.27 us -> 8.27 us  [fast(): across = lambda value: lax.ppermute(value, 'dp', pairs(4, 2))]
    ppermute x11 -> x12, waiting for transfers between devices: 3.86 us -> 1.88 us  [fast(): core = lambda value: lax.ppermute(value, 'dp', pairs(4, 1))]
    ppermute x9 -> x8, starting transfers between devices: 7.18 us -> 5.64 us  [fast(): swap = lambda value: lax.ppermute(value, 'tensor', pairs(4, 1))]
    pallas_call x15 -> x13, Pallas kernels: 27.6 us -> 27.4 us  [the longest x5 8.47 us: down(): pl.pallas_call(functools.partial(down_kernel, keys), in_specs=[pl.BlockSp...]
    ppermute x9 -> x8, waiting for transfers between devices: 11.3 us -> 11.3 us  [fast(): swap = lambda value: lax.ppermute(value, 'tensor', pairs(4, 1))]
  transfers between devices with their start and end apart: 30 -> 30, of which waited for: 17 -> 18; matrix products, arithmetic and copies ran while one was open for 0% -> 0% of each run, Pallas kernels for 26% -> 29%
where the time goes in v4:
time: 97.2 us; the launch traced here: 96.8 us
  Pallas kernels  38 us (39%)
  waiting for transfers between devices  31.1 us (32%)
  starting transfers between devices  27.1 us (28%)
    ppermute x8, waiting for transfers between devices, fast(): swap = lambda value: lax.ppermute(value, 'tensor', pairs(4, 1))  11.3 us
    ppermute x6, starting transfers between devices, fast(): across = lambda value: lax.ppermute(value, 'dp', pairs(4, 2))  10.6 us
    ppermute x4, waiting for transfers between devices, sum_tensor(): crosses[n] = lax.ppermute(helds[n], 'tensor', pairs(4, 2))  9.73 us
    ppermute x4, starting transfers between devices, sum_tensor(): crosses[n] = lax.ppermute(helds[n], 'tensor', pairs(4, 2))  9.1 us
    pallas_call x5, Pallas kernels, down(): pl.pallas_call(functools.partial(down_kernel, keys), in_specs=[pl.BlockSp...  8.47 us
    ppermute x6, waiting for transfers between devices, fast(): across = lambda value: lax.ppermute(value, 'dp', pairs(4, 2))  8.27 us
    pallas_call x1, Pallas kernels, attention_first(): pl.pallas_call(first_attention, in_specs=[hbm] * 6, out_specs=[vmem] * 7,...  5.95 us
    pallas_call x1, Pallas kernels, fetch(): pl.pallas_call(functools.partial(fetch_kernel, pieces), in_specs=[pl.Bloc...  5.85 us
  transfers between devices with their start and end apart: 30, of which 18 were waited for; matrix products, arithmetic and copies ran while one was open for 0% of the time, Pallas kernels for 29%

profile of v4, /device:TPU:0, one launch (start us, length us, event | category | flops | bytes accessed | tf_op | source)
XLA Modules:
  0.0 96.8 jit_solution(3609649230550349818)
XLA Ops:
  0.0 0.1 pad_add_fusion.where_ref
  0.1 6.0 %shard_map.118 = (bf16[16,2048]{1,0:T(8,128)(2,1)S(1)}, s32[16,128]{1,0:T(8,128)S(1)}, bf16[2,16,2048]{2,1,0:T(8,128)(2,1)S(1)}, bf16[2,16,2,128]{3,2,1,0:T(2,12...) custom-call(s32[16]{0:T(128)} %len_hbm.1, ...), custom_call_target="tpu_custom_call" | custom-call | flops 67108 | bytes 16777 | tf_op jit(solution)/shard_map/pallas_call | solution.py:177
  6.1 3.2 %collective-permute-start.1 = (bf16[16,2048]{1,0:T(8,128)(2,1)S(1)}, bf16[16,2048]{1,0:T(8,128)(2,1)S(1)}, u32[]{:S(2)}, u32[]{:S(2)}) collective-permute-start(bf16[16,2048]{1,0:T(8,128)(2,1)S(1)} %get-tuple-element.77.refs_0_), channel_id=1, source_target_pairs={{0,2},{1,3},{2,0},{3,1},{4,6},{5,7},{6,4},{7,5},{8,10},{9,11},{10,... | collective-permute-start | bytes 196616 | tf_op jit(solution)/shard_map/ppermute | solution.py:629
  9.3 1.9 %shard_map.119.refs_4_.refs_0_ = bf16[16,2048]{1,0:T(8,128)(2,1)S(1)} custom-call(s32[16,128]{1,0:T(8,128)S(1)} %get-tuple-element.69.lens_ref, bf16[2,16,2048]{2,1,0:T(8,128)(2,1)S(1)} %get-tuple-element.70.q_ref, bf16[2,16,2,128]{3,2,1,0:T(2,128)(2,1)S(1)} %get-tuple-element.71.nk_ref, bf16[2,16,2,128]{3,2,1,0:T(2,128)(2,1)S(1)} %get-tuple-element.72.nv_ref, ...), custom_call_target="tpu_custom_call" | custom-call | flops 67108 | bytes 4194 | tf_op jit(solution)/shard_map/pallas_call | solution.py:209
  11.2 0.3 collective-permute-done.1.refs_2_
  11.5 0.2 collective-permute-start.2
  11.8 1.8 %collective-permute-start.4 = (bf16[16,2048]{1,0:T(8,128)(2,1)S(1)}, bf16[16,2048]{1,0:T(8,128)(2,1)S(1)}, u32[]{:S(2)}, u32[]{:S(2)}) collective-permute-start(bf16[16,2048]{1,0:T(8,128)(2,1)S(1)} %shard_map.119.refs_4_.refs_0_), channel_id=1, source_target_pairs={{0,2},{1,3},{2,0},{3,1},{4,6},{5,7},{6,4},{7,5},{8,10},{9,11},{10,... | collective-permute-start | bytes 196616 | tf_op jit(solution)/shard_map/ppermute | solution.py:629
  13.6 0.2 collective-permute-start.3
  13.9 1.4 %shard_map.120 = bf16[64,1024]{1,0:T(8,128)(2,1)S(1)} custom-call(s32[2]{0:T(128)S(1)} %pad_add_fusion.where_ref, bf16[16,2048]{1,0:T(8,128)(2,1)S(1)} %get-tuple-element.77.refs_0_, bf16[16,2048]{1,0:T(8,128)(2,1)S(1)} %collective-permute-done.refs_1_, bf16[16,2048]{1,0:T(8,128)(2,1)S(1)} %collective-permute-done.1.refs_2_, ...), custom_call_target="tpu_custom_call" | custom-call | flops 268435 | bytes 4194 | tf_op jit(solution)/shard_map/pallas_call | solution.py:278
  15.3 1.1 %collective-permute-done.4.refs_6_.refs_2_ = bf16[16,2048]{1,0:T(8,128)(2,1)S(1)} collective-permute-done((bf16[16,2048]{1,0:T(8,128)(2,1)S(1)}, bf16[16,2048]{1,0:T(8,128)(2,1)S(1)}, u32[]{:S(2)}, u32[]{:S(2)}) %collective-permute-start.4) | collective-permute-done | bytes 65568 | tf_op jit(solution)/shard_map/ppermute | solution.py:629
  16.3 1.6 %collective-permute-start.6 = (bf16[64,1024]{1,0:T(8,128)(2,1)S(1)}, bf16[64,1024]{1,0:T(8,128)(2,1)S(1)}, u32[]{:S(2)}, u32[]{:S(2)}) collective-permute-start(bf16[64,1024]{1,0:T(8,128)(2,1)S(1)} %shard_map.120), channel_id=1, source_target_pairs={{0,4},{4,0},{8,12},{12,8},{1,5},{5,1},{9,13},{13,9},{2,6},{6,2},{1... | collective-permute-start | bytes 393224 | tf_op jit(solution)/shard_map/ppermute | solution.py:630
  17.9 2.1 %shard_map.121 = (bf16[64,1024]{1,0:T(8,128)(2,1)S(1)}, bf16[64,1024]{1,0:T(8,128)(2,1)S(1)}) custom-call(s32[2]{0:T(128)S(1)} %pad_add_fusion.where_ref, bf16[16,2048]{1,0:T(8,128)(2,1)S(1)} %get-tuple-element.77.refs_0_, bf16[16,2048]{1,0:T(8,128)(2,1)S(1)} %collective-permute-done.refs_1_, bf16[16,2048]{1,0:T(8,128)(2,1)S(1)} %collective-permute-done.1.refs_2_, ...), custom_call_target="tpu_custom_call" | custom-call | flops 268435 | bytes 4194 | tf_op jit(solution)/shard_map/pallas_call | solution.py:278
  20.1 1.3 %collective-permute-start.8 = (bf16[64,1024]{1,0:T(8,128)(2,1)S(1)}, bf16[64,1024]{1,0:T(8,128)(2,1)S(1)}, u32[]{:S(2)}, u32[]{:S(2)}) collective-permute-start(bf16[64,1024]{1,0:T(8,128)(2,1)S(1)} %get-tuple-element.89), channel_id=1, source_target_pairs={{0,4},{4,0},{8,12},{12,8},{1,5},{5,1},{9,13},{13,9},{2,6},{6,2},{1... | collective-permute-start | bytes 393224 | tf_op jit(solution)/shard_map/ppermute | solution.py:630
  21.4 0.9 collective-permute-done.6.refs_1_
  22.3 2.7 %collective-permute-start.7 = (bf16[64,1024]{1,0:T(8,128)(2,1)S(1)}, bf16[64,1024]{1,0:T(8,128)(2,1)S(1)}, u32[]{:S(2)}, u32[]{:S(2)}) collective-permute-start(bf16[64,1024]{1,0:T(8,128)(2,1)S(1)} %shard_map.122.refs_0_), channel_id=1, source_target_pairs={{0,8},{4,12},{8,0},{12,4},{1,9},{5,13},{9,1},{13,5},{2,10},{6,14},... | collective-permute-start | bytes 393224 | tf_op jit(solution)/shard_map/ppermute | solution.py:642
  25.0 1.4 %shard_map.123.refs_0_ = bf16[64,1024]{1,0:T(8,128)(2,1)S(1)} custom-call(s32[2]{0:T(128)S(1)} %pad_add_fusion.where_ref, bf16[16,2048]{1,0:T(8,128)(2,1)S(1)} %shard_map.119.refs_4_.refs_0_, bf16[16,2048]{1,0:T(8,128)(2,1)S(1)} %collective-permute-done.3.refs_5_.refs_1_, bf16[16,2048]{1,0:T(8,128)(2,1)S(1)} %collective-permute-done.4.refs_6_.refs_2_, ...), custom_call_target="tpu_custom_call" | custom-call | flops 268435 | bytes 4194 | tf_op jit(solution)/shard_map/pallas_call | solution.py:278
  26.4 1.0 %collective-permute-done.8.refs_1_ = bf16[64,1024]{1,0:T(8,128)(2,1)S(1)} collective-permute-done((bf16[64,1024]{1,0:T(8,128)(2,1)S(1)}, bf16[64,1024]{1,0:T(8,128)(2,1)S(1)}, u32[]{:S(2)}, u32[]{:S(2)}) %collective-permute-start.8) | collective-permute-done | bytes 131104 | tf_op jit(solution)/shard_map/ppermute | solution.py:630
  27.5 1.7 %collective-permute-start.9 = (bf16[64,1024]{1,0:T(8,128)(2,1)S(1)}, bf16[64,1024]{1,0:T(8,128)(2,1)S(1)}, u32[]{:S(2)}, u32[]{:S(2)}) collective-permute-start(bf16[64,1024]{1,0:T(8,128)(2,1)S(1)} %shard_map.124.refs_0_), channel_id=1, source_target_pairs={{0,8},{4,12},{8,0},{12,4},{1,9},{5,13},{9,1},{13,5},{2,10},{6,14},... | collective-permute-start | bytes 393224 | tf_op jit(solution)/shard_map/ppermute | solution.py:642
  29.2 5.9 %shard_map.125 = (bf16[1024,3584]{1,0:T(8,128)(2,1)S(1)}, bf16[1024,3584]{1,0:T(8,128)(2,1)S(1)}) custom-call(s32[2]{0:T(128)S(1)} %pad_add_fusion.where_ref, bf16[2048,3584]{1,0:T(8,128)(2,1)} %src_ref.1, bf16[64,1024]{1,0:T(8,128)(2,1)S(1)} %shard_map.124.refs_0_), custom_call_target="tpu_custom_call" | custom-call | bytes 7340 | tf_op jit(solution)/shard_map/pallas_call | solution.py:244
  35.1 0.5 collective-permute-start.10
  35.6 1.3 %collective-permute-done.9.refs_1_ = bf16[64,1024]{1,0:T(8,128)(2,1)S(1)} collective-permute-done((bf16[64,1024]{1,0:T(8,128)(2,1)S(1)}, bf16[64,1024]{1,0:T(8,128)(2,1)S(1)}, u32[]{:S(2)}, u32[]{:S(2)}) %collective-permute-start.9) | collective-permute-done | bytes 131104 | tf_op jit(solution)/shard_map/ppermute | solution.py:642
  37.0 0.6 collective-permute-start.11
  37.6 0.7 shard_map.128
  38.4 2.6 %shard_map.129.f_ref = f32[128,7168]{1,0:T(8,128)S(1)} custom-call(s32[2]{0:T(128)S(1)} %pad_add_fusion.where_ref, bf16[128,1024]{1,0:T(8,128)(2,1)S(1)} %get-tuple-element.96.x_ref, bf16[1024,3584]{1,0:T(8,128)(2,1)S(1)} %get-tuple-element.97.g_ref, bf16[2048,3584]{1,0:T(8,128)(2,1)S(1)} %bitcast.5), custom_call_target="tpu_custom_call" | custom-call | flops 1879048 | bytes 14680 | tf_op jit(solution)/shard_map/pallas_call | solution.py:340
  41.0 0.1 collective-permute-done.10.refs_0_
  41.1 1.8 %collective-permute-done.11.refs_1_ = bf16[64,1024]{1,0:T(8,128)(2,1)S(1)} collective-permute-done((bf16[64,1024]{1,0:T(8,128)(2,1)S(1)}, bf16[64,1024]{1,0:T(8,128)(2,1)S(1)}, u32[]{:S(2)}, u32[]{:S(2)}) %collective-permute-start.11) | collective-permute-done | bytes 131104 | tf_op jit(solution)/shard_map/ppermute | solution.py:630
  42.9 0.8 shard_map.130
  43.7 2.1 %shard_map.132 = (bf16[64,1920]{1,0:T(8,128)(2,1)S(1)}, bf16[64,1920]{1,0:T(8,128)(2,1)S(1)}, f32[128,1792]{1,0:T(8,128)S(1)}) custom-call(s32[2]{0:T(128)S(1)} %pad_add_fusion.where_ref, bf16[128,1024]{1,0:T(8,128)(2,1)S(1)} %get-tuple-element.108.x_ref, f32[128,7168]{1,0:T(8,128)S(1)} %shard_map.129.f_ref, f32[128,128]{1,0:T(8,128)S(1)} %shard_map.131.sq_ref, ...), custom_call_target="tpu_custom_call" | custom-call | flops 939524 | bytes 7340 | tf_op jit(solution)/shard_map/pallas_call | solution.py:392
  45.8 0.1 collective-permute-start.12
  45.8 0.5 collective-permute-start.14
  46.3 1.0 %collective-permute-done.12.got_ref = bf16[64,1920]{1,0:T(8,128)(2,1)S(1)} collective-permute-done((bf16[64,1920]{1,0:T(8,128)(2,1)S(1)}, bf16[64,1920]{1,0:T(8,128)(2,1)S(1)}, u32[]{:S(2)}, u32[]{:S(2)}) %collective-permute-start.12) | collective-permute-done | bytes 245792 | tf_op jit(solution)/shard_map/ppermute | solution.py:628
  47.3 0.2 shard_map.133
  47.5 1.7 %collective-permute-start.13 = (bf16[64,1920]{1,0:T(8,128)(2,1)S(1)}, bf16[64,1920]{1,0:T(8,128)(2,1)S(1)}, u32[]{:S(2)}, u32[]{:S(2)}) collective-permute-start(bf16[64,1920]{1,0:T(8,128)(2,1)S(1)} %shard_map.133), channel_id=1, source_target_pairs={{0,2},{1,3},{2,0},{3,1},{4,6},{5,7},{6,4},{7,5},{8,10},{9,11},{10,... | collective-permute-start | bytes 737288 | tf_op jit(solution)/shard_map/ppermute | solution.py:629
  49.3 0.2 shard_map.134
  49.5 2.0 %shard_map.135 = (bf16[64,1920]{1,0:T(8,128)(2,1)S(1)}, bf16[64,1920]{1,0:T(8,128)(2,1)S(1)}, f32[128,1792]{1,0:T(8,128)S(1)}) custom-call(s32[2]{0:T(128)S(1)} %pad_add_fusion.where_ref, bf16[128,1024]{1,0:T(8,128)(2,1)S(1)} %get-tuple-element.108.x_ref, f32[128,7168]{1,0:T(8,128)S(1)} %shard_map.129.f_ref, f32[128,128]{1,0:T(8,128)S(1)} %shard_map.131.sq_ref, ...), custom_call_target="tpu_custom_call" | custom-call | flops 939524 | bytes 7340 | tf_op jit(solution)/shard_map/pallas_call | solution.py:392
  51.6 0.5 collective-permute-start.16
  52.1 0.4 collective-permute-start.18
  52.5 3.9 %collective-permute-done.13.far_ref = bf16[64,1920]{1,0:T(8,128)(2,1)S(1)} collective-permute-done((bf16[64,1920]{1,0:T(8,128)(2,1)S(1)}, bf16[64,1920]{1,0:T(8,128)(2,1)S(1)}, u32[]{:S(2)}, u32[]{:S(2)}) %collective-permute-start.13) | collective-permute-done | bytes 245792 | tf_op jit(solution)/shard_map/ppermute | solution.py:629
  56.4 0.4 shard_map.136.refs_0_
  56.8 0.1 collective-permute-start.19
  56.9 1.7 %collective-permute-start.17 = (bf16[64,896]{1,0:T(8,128)(2,1)S(1)}, bf16[64,896]{1,0:T(8,128)(2,1)S(1)}, u32[]{:S(2)}, u32[]{:S(2)}) collective-permute-start(bf16[64,896]{1,0:T(8,128)(2,1)S(1)} %shard_map.136.refs_0_), channel_id=1, source_target_pairs={{0,2},{1,3},{2,0},{3,1},{4,6},{5,7},{6,4},{7,5},{8,10},{9,11},{10,... | collective-permute-start | bytes 344072 | tf_op jit(solution)/shard_map/ppermute | solution.py:629
  58.7 1.9 %shard_map.137.refs_2_ = f32[64,2048]{1,0:T(8,128)S(1)} custom-call(s32[2]{0:T(128)S(1)} %pad_add_fusion.where_ref, bf16[64,896]{1,0:T(8,128)(2,1)S(1)} %shard_map.136.refs_0_, bf16[64,896]{1,0:T(8,128)(2,1)S(1)} %collective-permute-done.19.refs_1_, bf16[3584,2048]{1,0:T(8,128)(2,1)S(1)} %bitcast.3), custom_call_target="tpu_custom_call" | custom-call | flops 469762 | bytes 7340 | tf_op jit(solution)/shard_map/pallas_call | solution.py:512
  60.6 1.0 %collective-permute-done.18.far_ref = bf16[64,1920]{1,0:T(8,128)(2,1)S(1)} collective-permute-done((bf16[64,1920]{1,0:T(8,128)(2,1)S(1)}, bf16[64,1920]{1,0:T(8,128)(2,1)S(1)}, u32[]{:S(2)}, u32[]{:S(2)}) %collective-permute-start.18) | collective-permute-done | bytes 245792 | tf_op jit(solution)/shard_map/ppermute | solution.py:629
  61.6 0.2 shard_map.138.refs_0_
  61.9 0.1 collective-permute-start.21
  62.0 1.3 %collective-permute-done.17.refs_0_ = bf16[64,896]{1,0:T(8,128)(2,1)S(1)} collective-permute-done((bf16[64,896]{1,0:T(8,128)(2,1)S(1)}, bf16[64,896]{1,0:T(8,128)(2,1)S(1)}, u32[]{:S(2)}, u32[]{:S(2)}) %collective-permute-start.17) | collective-permute-done | bytes 114720 | tf_op jit(solution)/shard_map/ppermute | solution.py:629
  63.3 1.7 %collective-permute-start.22 = (bf16[64,896]{1,0:T(8,128)(2,1)S(1)}, bf16[64,896]{1,0:T(8,128)(2,1)S(1)}, u32[]{:S(2)}, u32[]{:S(2)}) collective-permute-start(bf16[64,896]{1,0:T(8,128)(2,1)S(1)} %shard_map.138.refs_0_), channel_id=1, source_target_pairs={{0,2},{1,3},{2,0},{3,1},{4,6},{5,7},{6,4},{7,5},{8,10},{9,11},{10,... | collective-permute-start | bytes 344072 | tf_op jit(solution)/shard_map/ppermute | solution.py:629
  65.0 1.9 %shard_map.139.refs_5_.refs_2_ = f32[64,2048]{1,0:T(8,128)S(1)} custom-call(s32[2]{0:T(128)S(1)} %pad_add_fusion.where_ref, bf16[64,896]{1,0:T(8,128)(2,1)S(1)} %shard_map.138.refs_0_, bf16[64,896]{1,0:T(8,128)(2,1)S(1)} %collective-permute-done.21.refs_1_, bf16[3584,2048]{1,0:T(8,128)(2,1)S(1)} %bitcast.3), custom_call_target="tpu_custom_call" | custom-call | flops 469762 | bytes 7340 | tf_op jit(solution)/shard_map/pallas_call | solution.py:512
  67.0 1.3 %shard_map.140 = bf16[64,1024]{1,0:T(8,128)(2,1)S(1)} custom-call(s32[2]{0:T(128)S(1)} %pad_add_fusion.where_ref, bf16[64,896]{1,0:T(8,128)(2,1)S(1)} %collective-permute-done.17.refs_0_, bf16[64,896]{1,0:T(8,128)(2,1)S(1)} %collective-permute-done.20.refs_1_, f32[64,2048]{1,0:T(8,128)S(1)} %shard_map.137.refs_2_, bf16[3584,2048]{1,0:T(8,128)(2,1)S(1)} %bitcast.3), custom_call_target="tpu_custom_call" | custom-call | flops 469762 | bytes 7340 | tf_op jit(solution)/shard_map/pallas_call | solution.py:512
  68.3 0.6 collective-permute-done.22.refs_3_.refs_0_
  68.9 0.5 collective-permute-start.24
  69.3 0.9 collective-permute-done.23.refs_4_.refs_1_
  70.2 2.0 %shard_map.141 = (bf16[64,1024]{1,0:T(8,128)(2,1)S(1)}, bf16[64,1024]{1,0:T(8,128)(2,1)S(1)}) custom-call(s32[2]{0:T(128)S(1)} %pad_add_fusion.where_ref, bf16[64,896]{1,0:T(8,128)(2,1)S(1)} %collective-permute-done.17.refs_0_, bf16[64,896]{1,0:T(8,128)(2,1)S(1)} %collective-permute-done.20.refs_1_, f32[64,2048]{1,0:T(8,128)S(1)} %shard_map.137.refs_2_, ...), custom_call_target="tpu_custom_call" | custom-call | flops 469762 | bytes 7340 | tf_op jit(solution)/shard_map/pallas_call | solution.py:512
  72.2 0.8 collective-permute-start.27
  72.9 1.8 %collective-permute-done.24.refs_1_ = bf16[64,1024]{1,0:T(8,128)(2,1)S(1)} collective-permute-done((bf16[64,1024]{1,0:T(8,128)(2,1)S(1)}, bf16[64,1024]{1,0:T(8,128)(2,1)S(1)}, u32[]{:S(2)}, u32[]{:S(2)}) %collective-permute-start.24) | collective-permute-done | bytes 131104 | tf_op jit(solution)/shard_map/ppermute | solution.py:630
  74.8 1.9 %collective-permute-start.25 = (bf16[64,1024]{1,0:T(8,128)(2,1)S(1)}, bf16[64,1024]{1,0:T(8,128)(2,1)S(1)}, u32[]{:S(2)}, u32[]{:S(2)}) collective-permute-start(bf16[64,1024]{1,0:T(8,128)(2,1)S(1)} %shard_map.142.refs_0_), channel_id=1, source_target_pairs={{0,8},{4,12},{8,0},{12,4},{1,9},{5,13},{9,1},{13,5},{2,10},{6,14},... | collective-permute-start | bytes 393224 | tf_op jit(solution)/shard_map/ppermute | solution.py:642
  76.7 1.3 %shard_map.144.refs_0_ = bf16[64,1024]{1,0:T(8,128)(2,1)S(1)} custom-call(s32[2]{0:T(128)S(1)} %pad_add_fusion.where_ref, bf16[64,896]{1,0:T(8,128)(2,1)S(1)} %collective-permute-done.22.refs_3_.refs_0_, bf16[64,896]{1,0:T(8,128)(2,1)S(1)} %collective-permute-done.23.refs_4_.refs_1_, f32[64,2048]{1,0:T(8,128)S(1)} %shard_map.139.refs_5_.refs_2_, ...), custom_call_target="tpu_custom_call" | custom-call | flops 469762 | bytes 7340 | tf_op jit(solution)/shard_map/pallas_call | solution.py:512
  78.1 2.8 %collective-permute-start.28 = (bf16[64,1024]{1,0:T(8,128)(2,1)S(1)}, bf16[64,1024]{1,0:T(8,128)(2,1)S(1)}, u32[]{:S(2)}, u32[]{:S(2)}) collective-permute-start(bf16[64,1024]{1,0:T(8,128)(2,1)S(1)} %shard_map.145.refs_0_), channel_id=1, source_target_pairs={{0,8},{4,12},{8,0},{12,4},{1,9},{5,13},{9,1},{13,5},{2,10},{6,14},... | collective-permute-start | bytes 393224 | tf_op jit(solution)/shard_map/ppermute | solution.py:642
  80.9 6.6 %collective-permute-done.25.refs_1_ = bf16[64,1024]{1,0:T(8,128)(2,1)S(1)} collective-permute-done((bf16[64,1024]{1,0:T(8,128)(2,1)S(1)}, bf16[64,1024]{1,0:T(8,128)(2,1)S(1)}, u32[]{:S(2)}, u32[]{:S(2)}) %collective-permute-start.25) | collective-permute-done | bytes 131104 | tf_op jit(solution)/shard_map/ppermute | solution.py:642
  87.7 1.8 %collective-permute-done.28.refs_1_ = bf16[64,1024]{1,0:T(8,128)(2,1)S(1)} collective-permute-done((bf16[64,1024]{1,0:T(8,128)(2,1)S(1)}, bf16[64,1024]{1,0:T(8,128)(2,1)S(1)}, u32[]{:S(2)}, u32[]{:S(2)}) %collective-permute-start.28) | collective-permute-done | bytes 131104 | tf_op jit(solution)/shard_map/ppermute | solution.py:642
  89.5 0.3 collective-permute-start.29
  89.8 4.2 %collective-permute-done.26.refs_3_ = bf16[64,1024]{1,0:T(8,128)(2,1)S(1)} collective-permute-done((bf16[64,1024]{1,0:T(8,128)(2,1)S(1)}, bf16[64,1024]{1,0:T(8,128)(2,1)S(1)}, u32[]{:S(2)}, u32[]{:S(2)}) %collective-permute-start.26) | collective-permute-done | bytes 131104 | tf_op jit(solution)/shard_map/ppermute | solution.py:630
  93.9 1.4 %collective-permute-done.29.refs_5_ = bf16[64,1024]{1,0:T(8,128)(2,1)S(1)} collective-permute-done((bf16[64,1024]{1,0:T(8,128)(2,1)S(1)}, bf16[64,1024]{1,0:T(8,128)(2,1)S(1)}, u32[]{:S(2)}, u32[]{:S(2)}) %collective-permute-start.29) | collective-permute-done | bytes 131104 | tf_op jit(solution)/shard_map/ppermute | solution.py:630
  95.3 1.5 %shard_map.147 = bf16[2,64,2048]{2,1,0:T(8,128)(2,1)} custom-call(s32[2]{0:T(128)S(1)} %pad_add_fusion.where_ref, bf16[128,1024]{1,0:T(8,128)(2,1)S(1)} %get-tuple-element.95.refs_0_, bf16[128,1024]{1,0:T(8,128)(2,1)S(1)} %get-tuple-element.100.refs_1_, bf16[64,1024]{1,0:T(8,128)(2,1)S(1)} %shard_map.143.refs_2_, ...), custom_call_target="tpu_custom_call" | custom-call | flops 262 | bytes 1048 | tf_op jit(solution)/shard_map/pallas_call | solution.py:472
  (55 shorter events, 0.5 us)
Async XLA Ops:
  0.0 13.8 %slice-start.8 = ((s8[8388608]{0:T(1024)(128)(4,1)}), s8[4194304]{0:T(1024)(128)(4,1)S(1)}, s32[]{:S(2)}) async-start(s8[8388608]{0:T(1024)(128)(4,1)} %bitcast.6), calls=%async_computation.8 | async-start | bytes 8388608
  0.1 13.8 %slice-start.9 = ((s8[8388608]{0:T(1024)(128)(4,1)}), s8[4194304]{0:T(1024)(128)(4,1)S(1)}, s32[]{:S(2)}) async-start(s8[8388608]{0:T(1024)(128)(4,1)} %bitcast.6), calls=%async_computation.9 | async-start | bytes 8388608
  6.0 7.8 %copy-start.1 = (bf16[2048]{0:T(1024)(128)(2,1)S(1)}, bf16[2048]{0:T(1024)(128)(2,1)}, u32[]{:S(2)}) copy-start(bf16[2048]{0:T(1024)(128)(2,1)} %param.20) | copy-start | bytes 12292
  6.1 5.5 %collective-permute-start.1 = (bf16[16,2048]{1,0:T(8,128)(2,1)S(1)}, bf16[16,2048]{1,0:T(8,128)(2,1)S(1)}, u32[]{:S(2)}, u32[]{:S(2)}) collective-permute-start(bf16[16,2048]{1,0:T(8,128)(2,1)S(1)} %get-tuple-element.77.refs_0_), channel_id=1, source_target_pairs={{0,2},{1,3},{2,0},{3,1},{4,6},{5,7},{6,4},{7,5},{8,10},{9,11},{10,... | collective-permute-start | bytes 196616 | tf_op jit(solution)/shard_map/ppermute | solution.py:629
  9.3 4.5 %collective-permute-start = (bf16[16,2048]{1,0:T(8,128)(2,1)S(1)}, bf16[16,2048]{1,0:T(8,128)(2,1)S(1)}, u32[]{:S(2)}, u32[]{:S(2)}) collective-permute-start(bf16[16,2048]{1,0:T(8,128)(2,1)S(1)} %get-tuple-element.77.refs_0_), channel_id=1, source_target_pairs={{0,1},{1,0},{2,3},{3,2},{4,5},{5,4},{6,7},{7,6},{8,9},{9,8},{10,11... | collective-permute-start | bytes 196616 | tf_op jit(solution)/shard_map/ppermute | solution.py:628
  11.5 2.3 %collective-permute-start.2 = (bf16[16,2048]{1,0:T(8,128)(2,1)S(1)}, bf16[16,2048]{1,0:T(8,128)(2,1)S(1)}, u32[]{:S(2)}, u32[]{:S(2)}) collective-permute-start(bf16[16,2048]{1,0:T(8,128)(2,1)S(1)} %collective-permute-done.1.refs_2_), channel_id=1, source_target_pairs={{0,1},{1,0},{2,3},{3,2},{4,5},{5,4},{6,7},{7,6},{8,9},{9,8},{10,11... | collective-permute-start | bytes 196616 | tf_op jit(solution)/shard_map/ppermute | solution.py:628
  11.8 4.5 %collective-permute-start.4 = (bf16[16,2048]{1,0:T(8,128)(2,1)S(1)}, bf16[16,2048]{1,0:T(8,128)(2,1)S(1)}, u32[]{:S(2)}, u32[]{:S(2)}) collective-permute-start(bf16[16,2048]{1,0:T(8,128)(2,1)S(1)} %shard_map.119.refs_4_.refs_0_), channel_id=1, source_target_pairs={{0,2},{1,3},{2,0},{3,1},{4,6},{5,7},{6,4},{7,5},{8,10},{9,11},{10,... | collective-permute-start | bytes 196616 | tf_op jit(solution)/shard_map/ppermute | solution.py:629
  13.6 4.4 %collective-permute-start.3 = (bf16[16,2048]{1,0:T(8,128)(2,1)S(1)}, bf16[16,2048]{1,0:T(8,128)(2,1)S(1)}, u32[]{:S(2)}, u32[]{:S(2)}) collective-permute-start(bf16[16,2048]{1,0:T(8,128)(2,1)S(1)} %shard_map.119.refs_4_.refs_0_), channel_id=1, source_target_pairs={{0,1},{1,0},{2,3},{3,2},{4,5},{5,4},{6,7},{7,6},{8,9},{9,8},{10,11... | collective-permute-start | bytes 196616 | tf_op jit(solution)/shard_map/ppermute | solution.py:628
  16.3 1.6 %collective-permute-start.5 = (bf16[16,2048]{1,0:T(8,128)(2,1)S(1)}, bf16[16,2048]{1,0:T(8,128)(2,1)S(1)}, u32[]{:S(2)}, u32[]{:S(2)}) collective-permute-start(bf16[16,2048]{1,0:T(8,128)(2,1)S(1)} %collective-permute-done.4.refs_6_.refs_2_), channel_id=1, source_target_pairs={{0,1},{1,0},{2,3},{3,2},{4,5},{5,4},{6,7},{7,6},{8,9},{9,8},{10,11... | collective-permute-start | bytes 196616 | tf_op jit(solution)/shard_map/ppermute | solution.py:628
  16.3 5.9 %collective-permute-start.6 = (bf16[64,1024]{1,0:T(8,128)(2,1)S(1)}, bf16[64,1024]{1,0:T(8,128)(2,1)S(1)}, u32[]{:S(2)}, u32[]{:S(2)}) collective-permute-start(bf16[64,1024]{1,0:T(8,128)(2,1)S(1)} %shard_map.120), channel_id=1, source_target_pairs={{0,4},{4,0},{8,12},{12,8},{1,5},{5,1},{9,13},{13,9},{2,6},{6,2},{1... | collective-permute-start | bytes 393224 | tf_op jit(solution)/shard_map/ppermute | solution.py:630
  17.9 20.4 %slice-start.4 = ((s8[14680064]{0:T(1024)(128)(4,1)}), s8[4194304]{0:T(1024)(128)(4,1)S(1)}, s32[]{:S(2)}) async-start(s8[14680064]{0:T(1024)(128)(4,1)} %bitcast.4), calls=%async_computation.4 | async-start | bytes 8388608
  17.9 20.4 %slice-start.5 = ((s8[14680064]{0:T(1024)(128)(4,1)}), s8[4194304]{0:T(1024)(128)(4,1)S(1)}, s32[]{:S(2)}) async-start(s8[14680064]{0:T(1024)(128)(4,1)} %bitcast.4), calls=%async_computation.5 | async-start | bytes 8388608
  20.1 7.3 %collective-permute-start.8 = (bf16[64,1024]{1,0:T(8,128)(2,1)S(1)}, bf16[64,1024]{1,0:T(8,128)(2,1)S(1)}, u32[]{:S(2)}, u32[]{:S(2)}) collective-permute-start(bf16[64,1024]{1,0:T(8,128)(2,1)S(1)} %get-tuple-element.89), channel_id=1, source_target_pairs={{0,4},{4,0},{8,12},{12,8},{1,5},{5,1},{9,13},{13,9},{2,6},{6,2},{1... | collective-permute-start | bytes 393224 | tf_op jit(solution)/shard_map/ppermute | solution.py:630
  22.3 16.1 %slice-start.6 = ((s8[14680064]{0:T(1024)(128)(4,1)}), s8[4194304]{0:T(1024)(128)(4,1)S(1)}, s32[]{:S(2)}) async-start(s8[14680064]{0:T(1024)(128)(4,1)} %bitcast.4), calls=%async_computation.6 | async-start | bytes 8388608
  22.3 12.8 %collective-permute-start.7 = (bf16[64,1024]{1,0:T(8,128)(2,1)S(1)}, bf16[64,1024]{1,0:T(8,128)(2,1)S(1)}, u32[]{:S(2)}, u32[]{:S(2)}) collective-permute-start(bf16[64,1024]{1,0:T(8,128)(2,1)S(1)} %shard_map.122.refs_0_), channel_id=1, source_target_pairs={{0,8},{4,12},{8,0},{12,4},{1,9},{5,13},{9,1},{13,5},{2,10},{6,14},... | collective-permute-start | bytes 393224 | tf_op jit(solution)/shard_map/ppermute | solution.py:642
  26.4 11.2 %copy-start = (bf16[2,64,2048]{2,1,0:T(8,128)(2,1)S(1)}, bf16[2,64,2048]{2,1,0:T(8,128)(2,1)}, u32[]{:S(2)}) copy-start(bf16[2,64,2048]{2,1,0:T(8,128)(2,1)} %refs_2_.5) | copy-start | bytes 1572868
  27.4 10.9 %slice-start.7 = ((s8[14680064]{0:T(1024)(128)(4,1)}), s8[2097152]{0:T(1024)(128)(4,1)S(1)}, s32[]{:S(2)}) async-start(s8[14680064]{0:T(1024)(128)(4,1)} %bitcast.4), calls=%async_computation.7 | async-start | bytes 4194304
  27.5 9.5 %collective-permute-start.9 = (bf16[64,1024]{1,0:T(8,128)(2,1)S(1)}, bf16[64,1024]{1,0:T(8,128)(2,1)S(1)}, u32[]{:S(2)}, u32[]{:S(2)}) collective-permute-start(bf16[64,1024]{1,0:T(8,128)(2,1)S(1)} %shard_map.124.refs_0_), channel_id=1, source_target_pairs={{0,8},{4,12},{8,0},{12,4},{1,9},{5,13},{9,1},{13,5},{2,10},{6,14},... | collective-permute-start | bytes 393224 | tf_op jit(solution)/shard_map/ppermute | solution.py:642
  35.1 6.0 %collective-permute-start.10 = (bf16[64,1024]{1,0:T(8,128)(2,1)S(1)}, bf16[64,1024]{1,0:T(8,128)(2,1)S(1)}, u32[]{:S(2)}, u32[]{:S(2)}) collective-permute-start(bf16[64,1024]{1,0:T(8,128)(2,1)S(1)} %shard_map.126.refs_0_), channel_id=1, source_target_pairs={{0,4},{4,0},{8,12},{12,8},{1,5},{5,1},{9,13},{13,9},{2,6},{6,2},{1... | collective-permute-start | bytes 393224 | tf_op jit(solution)/shard_map/ppermute | solution.py:630
  37.0 6.0 %collective-permute-start.11 = (bf16[64,1024]{1,0:T(8,128)(2,1)S(1)}, bf16[64,1024]{1,0:T(8,128)(2,1)S(1)}, u32[]{:S(2)}, u32[]{:S(2)}) collective-permute-start(bf16[64,1024]{1,0:T(8,128)(2,1)S(1)} %shard_map.127.refs_1_), channel_id=1, source_target_pairs={{0,4},{4,0},{8,12},{12,8},{1,5},{5,1},{9,13},{13,9},{2,6},{6,2},{1... | collective-permute-start | bytes 393224 | tf_op jit(solution)/shard_map/ppermute | solution.py:630
  45.8 1.6 %collective-permute-start.12 = (bf16[64,1920]{1,0:T(8,128)(2,1)S(1)}, bf16[64,1920]{1,0:T(8,128)(2,1)S(1)}, u32[]{:S(2)}, u32[]{:S(2)}) collective-permute-start(bf16[64,1920]{1,0:T(8,128)(2,1)S(1)} %get-tuple-element.106), channel_id=1, source_target_pairs={{0,1},{1,0},{2,3},{3,2},{4,5},{5,4},{6,7},{7,6},{8,9},{9,8},{10,11... | collective-permute-start | bytes 737288 | tf_op jit(solution)/shard_map/ppermute | solution.py:628
  45.8 3.4 %collective-permute-start.14 = (bf16[64,1920]{1,0:T(8,128)(2,1)S(1)}, bf16[64,1920]{1,0:T(8,128)(2,1)S(1)}, u32[]{:S(2)}, u32[]{:S(2)}) collective-permute-start(bf16[64,1920]{1,0:T(8,128)(2,1)S(1)} %get-tuple-element.107), channel_id=1, source_target_pairs={{0,1},{1,0},{2,3},{3,2},{4,5},{5,4},{6,7},{7,6},{8,9},{9,8},{10,11... | collective-permute-start | bytes 737288 | tf_op jit(solution)/shard_map/ppermute | solution.py:628
  47.5 8.9 %collective-permute-start.13 = (bf16[64,1920]{1,0:T(8,128)(2,1)S(1)}, bf16[64,1920]{1,0:T(8,128)(2,1)S(1)}, u32[]{:S(2)}, u32[]{:S(2)}) collective-permute-start(bf16[64,1920]{1,0:T(8,128)(2,1)S(1)} %shard_map.133), channel_id=1, source_target_pairs={{0,2},{1,3},{2,0},{3,1},{4,6},{5,7},{6,4},{7,5},{8,10},{9,11},{10,... | collective-permute-start | bytes 737288 | tf_op jit(solution)/shard_map/ppermute | solution.py:629
  49.3 9.4 %slice-start = ((s8[14680064]{0:T(1024)(128)(4,1)}), s8[4194304]{0:T(1024)(128)(4,1)S(1)}, s32[]{:S(2)}) async-start(s8[14680064]{0:T(1024)(128)(4,1)} %bitcast.2), calls=%async_computation | async-start | bytes 8388608
  49.4 9.2 %slice-start.1 = ((s8[14680064]{0:T(1024)(128)(4,1)}), s8[4194304]{0:T(1024)(128)(4,1)S(1)}, s32[]{:S(2)}) async-start(s8[14680064]{0:T(1024)(128)(4,1)} %bitcast.2), calls=%async_computation.1 | async-start | bytes 8388608
  49.5 9.2 %slice-start.2 = ((s8[14680064]{0:T(1024)(128)(4,1)}), s8[4194304]{0:T(1024)(128)(4,1)S(1)}, s32[]{:S(2)}) async-start(s8[14680064]{0:T(1024)(128)(4,1)} %bitcast.2), calls=%async_computation.2 | async-start | bytes 8388608
  49.5 9.2 %slice-start.3 = ((s8[14680064]{0:T(1024)(128)(4,1)}), s8[2097152]{0:T(1024)(128)(4,1)S(1)}, s32[]{:S(2)}) async-start(s8[14680064]{0:T(1024)(128)(4,1)} %bitcast.2), calls=%async_computation.3 | async-start | bytes 4194304
  51.5 4.9 %collective-permute-start.15 = (bf16[64,1920]{1,0:T(8,128)(2,1)S(1)}, bf16[64,1920]{1,0:T(8,128)(2,1)S(1)}, u32[]{:S(2)}, u32[]{:S(2)}) collective-permute-start(bf16[64,1920]{1,0:T(8,128)(2,1)S(1)} %get-tuple-element.110), channel_id=1, source_target_pairs={{0,1},{1,0},{2,3},{3,2},{4,5},{5,4},{6,7},{7,6},{8,9},{9,8},{10,11... | collective-permute-start | bytes 737288 | tf_op jit(solution)/shard_map/ppermute | solution.py:628
  51.6 4.8 %collective-permute-start.16 = (bf16[64,1920]{1,0:T(8,128)(2,1)S(1)}, bf16[64,1920]{1,0:T(8,128)(2,1)S(1)}, u32[]{:S(2)}, u32[]{:S(2)}) collective-permute-start(bf16[64,1920]{1,0:T(8,128)(2,1)S(1)} %get-tuple-element.111), channel_id=1, source_target_pairs={{0,1},{1,0},{2,3},{3,2},{4,5},{5,4},{6,7},{7,6},{8,9},{9,8},{10,11... | collective-permute-start | bytes 737288 | tf_op jit(solution)/shard_map/ppermute | solution.py:628
  52.1 9.6 %collective-permute-start.18 = (bf16[64,1920]{1,0:T(8,128)(2,1)S(1)}, bf16[64,1920]{1,0:T(8,128)(2,1)S(1)}, u32[]{:S(2)}, u32[]{:S(2)}) collective-permute-start(bf16[64,1920]{1,0:T(8,128)(2,1)S(1)} %shard_map.134), channel_id=1, source_target_pairs={{0,2},{1,3},{2,0},{3,1},{4,6},{5,7},{6,4},{7,5},{8,10},{9,11},{10,... | collective-permute-start | bytes 737288 | tf_op jit(solution)/shard_map/ppermute | solution.py:629
  56.8 1.8 %collective-permute-start.19 = (bf16[64,896]{1,0:T(8,128)(2,1)S(1)}, bf16[64,896]{1,0:T(8,128)(2,1)S(1)}, u32[]{:S(2)}, u32[]{:S(2)}) collective-permute-start(bf16[64,896]{1,0:T(8,128)(2,1)S(1)} %shard_map.136.refs_0_), channel_id=1, source_target_pairs={{0,1},{1,0},{2,3},{3,2},{4,5},{5,4},{6,7},{7,6},{8,9},{9,8},{10,11... | collective-permute-start | bytes 344072 | tf_op jit(solution)/shard_map/ppermute | solution.py:628
  56.9 6.4 %collective-permute-start.17 = (bf16[64,896]{1,0:T(8,128)(2,1)S(1)}, bf16[64,896]{1,0:T(8,128)(2,1)S(1)}, u32[]{:S(2)}, u32[]{:S(2)}) collective-permute-start(bf16[64,896]{1,0:T(8,128)(2,1)S(1)} %shard_map.136.refs_0_), channel_id=1, source_target_pairs={{0,2},{1,3},{2,0},{3,1},{4,6},{5,7},{6,4},{7,5},{8,10},{9,11},{10,... | collective-permute-start | bytes 344072 | tf_op jit(solution)/shard_map/ppermute | solution.py:629
  61.9 3.1 %collective-permute-start.21 = (bf16[64,896]{1,0:T(8,128)(2,1)S(1)}, bf16[64,896]{1,0:T(8,128)(2,1)S(1)}, u32[]{:S(2)}, u32[]{:S(2)}) collective-permute-start(bf16[64,896]{1,0:T(8,128)(2,1)S(1)} %shard_map.138.refs_0_), channel_id=1, source_target_pairs={{0,1},{1,0},{2,3},{3,2},{4,5},{5,4},{6,7},{7,6},{8,9},{9,8},{10,11... | collective-permute-start | bytes 344072 | tf_op jit(solution)/shard_map/ppermute | solution.py:628
  63.3 3.6 %collective-permute-start.20 = (bf16[64,896]{1,0:T(8,128)(2,1)S(1)}, bf16[64,896]{1,0:T(8,128)(2,1)S(1)}, u32[]{:S(2)}, u32[]{:S(2)}) collective-permute-start(bf16[64,896]{1,0:T(8,128)(2,1)S(1)} %collective-permute-done.17.refs_0_), channel_id=1, source_target_pairs={{0,1},{1,0},{2,3},{3,2},{4,5},{5,4},{6,7},{7,6},{8,9},{9,8},{10,11... | collective-permute-start | bytes 344072 | tf_op jit(solution)/shard_map/ppermute | solution.py:628
  63.3 5.6 %collective-permute-start.22 = (bf16[64,896]{1,0:T(8,128)(2,1)S(1)}, bf16[64,896]{1,0:T(8,128)(2,1)S(1)}, u32[]{:S(2)}, u32[]{:S(2)}) collective-permute-start(bf16[64,896]{1,0:T(8,128)(2,1)S(1)} %shard_map.138.refs_0_), channel_id=1, source_target_pairs={{0,2},{1,3},{2,0},{3,1},{4,6},{5,7},{6,4},{7,5},{8,10},{9,11},{10,... | collective-permute-start | bytes 344072 | tf_op jit(solution)/shard_map/ppermute | solution.py:629
  68.9 1.3 %collective-permute-start.23 = (bf16[64,896]{1,0:T(8,128)(2,1)S(1)}, bf16[64,896]{1,0:T(8,128)(2,1)S(1)}, u32[]{:S(2)}, u32[]{:S(2)}) collective-permute-start(bf16[64,896]{1,0:T(8,128)(2,1)S(1)} %collective-permute-done.22.refs_3_.refs_0_), channel_id=1, source_target_pairs={{0,1},{1,0},{2,3},{3,2},{4,5},{5,4},{6,7},{7,6},{8,9},{9,8},{10,11... | collective-permute-start | bytes 344072 | tf_op jit(solution)/shard_map/ppermute | solution.py:628
  68.9 5.9 %collective-permute-start.24 = (bf16[64,1024]{1,0:T(8,128)(2,1)S(1)}, bf16[64,1024]{1,0:T(8,128)(2,1)S(1)}, u32[]{:S(2)}, u32[]{:S(2)}) collective-permute-start(bf16[64,1024]{1,0:T(8,128)(2,1)S(1)} %shard_map.140), channel_id=1, source_target_pairs={{0,4},{4,0},{8,12},{12,8},{1,5},{5,1},{9,13},{13,9},{2,6},{6,2},{1... | collective-permute-start | bytes 393224 | tf_op jit(solution)/shard_map/ppermute | solution.py:630
  72.2 5.9 %collective-permute-start.27 = (bf16[64,1024]{1,0:T(8,128)(2,1)S(1)}, bf16[64,1024]{1,0:T(8,128)(2,1)S(1)}, u32[]{:S(2)}, u32[]{:S(2)}) collective-permute-start(bf16[64,1024]{1,0:T(8,128)(2,1)S(1)} %get-tuple-element.122), channel_id=1, source_target_pairs={{0,4},{4,0},{8,12},{12,8},{1,5},{5,1},{9,13},{13,9},{2,6},{6,2},{1... | collective-permute-start | bytes 393224 | tf_op jit(solution)/shard_map/ppermute | solution.py:630
  74.8 12.7 %collective-permute-start.25 = (bf16[64,1024]{1,0:T(8,128)(2,1)S(1)}, bf16[64,1024]{1,0:T(8,128)(2,1)S(1)}, u32[]{:S(2)}, u32[]{:S(2)}) collective-permute-start(bf16[64,1024]{1,0:T(8,128)(2,1)S(1)} %shard_map.142.refs_0_), channel_id=1, source_target_pairs={{0,8},{4,12},{8,0},{12,4},{1,9},{5,13},{9,1},{13,5},{2,10},{6,14},... | collective-permute-start | bytes 393224 | tf_op jit(solution)/shard_map/ppermute | solution.py:642
  78.1 11.4 %collective-permute-start.28 = (bf16[64,1024]{1,0:T(8,128)(2,1)S(1)}, bf16[64,1024]{1,0:T(8,128)(2,1)S(1)}, u32[]{:S(2)}, u32[]{:S(2)}) collective-permute-start(bf16[64,1024]{1,0:T(8,128)(2,1)S(1)} %shard_map.145.refs_0_), channel_id=1, source_target_pairs={{0,8},{4,12},{8,0},{12,4},{1,9},{5,13},{9,1},{13,5},{2,10},{6,14},... | collective-permute-start | bytes 393224 | tf_op jit(solution)/shard_map/ppermute | solution.py:642
  87.6 6.4 %collective-permute-start.26 = (bf16[64,1024]{1,0:T(8,128)(2,1)S(1)}, bf16[64,1024]{1,0:T(8,128)(2,1)S(1)}, u32[]{:S(2)}, u32[]{:S(2)}) collective-permute-start(bf16[64,1024]{1,0:T(8,128)(2,1)S(1)} %shard_map.143.refs_2_), channel_id=1, source_target_pairs={{0,4},{4,0},{8,12},{12,8},{1,5},{5,1},{9,13},{13,9},{2,6},{6,2},{1... | collective-permute-start | bytes 393224 | tf_op jit(solution)/shard_map/ppermute | solution.py:630
  89.5 5.9 %collective-permute-start.29 = (bf16[64,1024]{1,0:T(8,128)(2,1)S(1)}, bf16[64,1024]{1,0:T(8,128)(2,1)S(1)}, u32[]{:S(2)}, u32[]{:S(2)}) collective-permute-start(bf16[64,1024]{1,0:T(8,128)(2,1)S(1)} %shard_map.146.refs_4_), channel_id=1, source_target_pairs={{0,4},{4,0},{8,12},{12,8},{1,5},{5,1},{9,13},{13,9},{2,6},{6,2},{1... | collective-permute-start | bytes 393224 | tf_op jit(solution)/shard_map/ppermute | solution.py:630

commit v5 on v4

--- a/solution.py
+++ b/solution.py
@@ -141,10 +141,11 @@
 
     for move in small:
         move.start()
-    start(0, 0)
+    for b in range(count):
+        start(b, 0)
     small[0].wait()
     for b in range(2 * count):
-        if b:
+        if b >= count:
             start(b, 0)
         for c in range(1, slots // PART):
             live = len_ref[b] > c * PART
@@ -363,7 +364,7 @@
 
 
 def second_kernel(chip, groups, where_ref, x_ref, f_ref, sq_ref, g_ref, u_ref, *refs):
-    give_refs, (keep_ref, buf) = refs[:groups], refs[groups:]
+    give_refs, keep_ref = refs[:groups], refs[groups]
     for n, give_ref in enumerate(give_refs):
         some = give_ref.shape[0]
         give_ref[:, keep_ref.shape[1] :] = packed(sq_ref[n * some : (n + 1) * some, :])
@@ -375,13 +376,13 @@
     start = pl.multiple_of(((me // 2) ^ chip) * (2 * own), 128)
     for k, w_ref in enumerate((g_ref, u_ref)):
         out = jnp.dot(x_ref[...], w_ref[deep if k else all_rows, pl.ds(start, 2 * own)], preferred_element_type=F32)
-        buf[...] = out + f_ref[:, pl.ds(pl.multiple_of(k * length + start, 128), 2 * own)]
-        mine = pl.ds(pl.multiple_of((me % 2) * own, 128), own)
-        other = pl.ds(pl.multiple_of((1 - me % 2) * own, 128), own)
+        out = out + f_ref[:, pl.ds(pl.multiple_of(k * length + start, 128), 2 * own)]
+        mine = jnp.where(me % 2 == 0, out[:, :own], out[:, own:])
+        other = jnp.where(me % 2 == 0, out[:, own:], out[:, :own]).astype(BF16)
         here = slice(k * own, (k + 1) * own)
-        keep_ref[:, here] = buf[:, mine]
+        keep_ref[:, here] = mine
         for n, give_ref in enumerate(give_refs):
-            give_ref[:, here] = buf[n * rows : (n + 1) * rows, other].astype(BF16)
+            give_ref[:, here] = other[n * rows : (n + 1) * rows]
 
 
 def gate_up_second(where, x, first, sq, weights, chip, groups):
@@ -395,7 +396,6 @@
         out_specs=[vmem] * (groups + 1),
         out_shape=[jax.ShapeDtypeStruct((rows // groups, 2 * own + LANES), BF16)] * groups
         + [jax.ShapeDtypeStruct((rows, 2 * own), F32)],
-        scratch_shapes=[pltpu.VMEM((rows, 2 * own), F32)],
         cost_estimate=cost(4 * rows * deep * 2 * own, 8 * deep * own),
         compiler_params=pltpu.CompilerParams(vmem_limit_bytes=6 * MIB),
     )(where, x, first, sq, *weights)

time: 97.2 us -> 96.2 us (0.990)
  waiting for transfers between devices: 31.1 us -> 32.2 us
    ppermute x6, starting transfers between devices: 10.6 us -> 9.13 us  [fast(): across = lambda value: lax.ppermute(value, 'dp', pairs(4, 2))]
    ppermute x6, waiting for transfers between devices: 8.27 us -> 9.43 us  [fast(): across = lambda value: lax.ppermute(value, 'dp', pairs(4, 2))]
where the time goes in v5:
time: 96.2 us
  Pallas kernels  37.2 us (39%)
  waiting for transfers between devices  32.2 us (33%)
  starting transfers between devices  26.3 us (27%)
    ppermute x8, waiting for transfers between devices, fast(): swap = lambda value: lax.ppermute(value, 'tensor', pairs(4, 1))  11 us
    ppermute x4, waiting for transfers between devices, sum_tensor(): crosses[n] = lax.ppermute(helds[n], 'tensor', pairs(4, 2))  9.8 us
    ppermute x6, waiting for transfers between devices, fast(): across = lambda value: lax.ppermute(value, 'dp', pairs(4, 2))  9.43 us
    ppermute x4, starting transfers between devices, sum_tensor(): crosses[n] = lax.ppermute(helds[n], 'tensor', pairs(4, 2))  9.35 us
    ppermute x6, starting transfers between devices, fast(): across = lambda value: lax.ppermute(value, 'dp', pairs(4, 2))  9.13 us
    pallas_call x5, Pallas kernels, down(): pl.pallas_call(functools.partial(down_kernel, keys), in_specs=[pl.BlockSp...  8.64 us
    ppermute x8, starting transfers between devices, fast(): swap = lambda value: lax.ppermute(value, 'tensor', pairs(4, 1))  6.07 us
    pallas_call x1, Pallas kernels, fetch(): pl.pallas_call(functools.partial(fetch_kernel, pieces), in_specs=[pl.Bloc...  5.85 us
  transfers between devices with their start and end apart: 30, of which 18 were waited for; matrix products, arithmetic and copies ran while one was open for 0% of the time, Pallas kernels for 29%

profile of v5, /device:TPU:0, one launch (start us, length us, event | category | flops | bytes accessed | tf_op | source)
XLA Modules:
  0.0 96.2 jit_solution(292501344003217527)
XLA Ops:
  0.0 0.1 pad_add_fusion.where_ref
  0.1 5.6 %shard_map.118 = (bf16[16,2048]{1,0:T(8,128)(2,1)S(1)}, s32[16,128]{1,0:T(8,128)S(1)}, bf16[2,16,2048]{2,1,0:T(8,128)(2,1)S(1)}, bf16[2,16,2,128]{3,2,1,0:T(2,12...) custom-call(s32[16]{0:T(128)} %len_hbm.1, ...), custom_call_target="tpu_custom_call" | custom-call | flops 67108 | bytes 16777 | tf_op jit(solution)/shard_map/pallas_call | solution.py:178
  5.7 2.7 %collective-permute-start.1 = (bf16[16,2048]{1,0:T(8,128)(2,1)S(1)}, bf16[16,2048]{1,0:T(8,128)(2,1)S(1)}, u32[]{:S(2)}, u32[]{:S(2)}) collective-permute-start(bf16[16,2048]{1,0:T(8,128)(2,1)S(1)} %get-tuple-element.77.refs_0_), channel_id=1, source_target_pairs={{0,2},{1,3},{2,0},{3,1},{4,6},{5,7},{6,4},{7,5},{8,10},{9,11},{10,... | collective-permute-start | bytes 196616 | tf_op jit(solution)/shard_map/ppermute | solution.py:629
  8.5 1.9 %shard_map.119.refs_4_.refs_0_ = bf16[16,2048]{1,0:T(8,128)(2,1)S(1)} custom-call(s32[16,128]{1,0:T(8,128)S(1)} %get-tuple-element.69.lens_ref, bf16[2,16,2048]{2,1,0:T(8,128)(2,1)S(1)} %get-tuple-element.70.q_ref, bf16[2,16,2,128]{3,2,1,0:T(2,128)(2,1)S(1)} %get-tuple-element.71.nk_ref, bf16[2,16,2,128]{3,2,1,0:T(2,128)(2,1)S(1)} %get-tuple-element.72.nv_ref, ...), custom_call_target="tpu_custom_call" | custom-call | flops 67108 | bytes 4194 | tf_op jit(solution)/shard_map/pallas_call | solution.py:210
  10.4 0.3 collective-permute-done.1.refs_2_
  10.7 0.2 collective-permute-start.2
  11.0 1.8 %collective-permute-start.4 = (bf16[16,2048]{1,0:T(8,128)(2,1)S(1)}, bf16[16,2048]{1,0:T(8,128)(2,1)S(1)}, u32[]{:S(2)}, u32[]{:S(2)}) collective-permute-start(bf16[16,2048]{1,0:T(8,128)(2,1)S(1)} %shard_map.119.refs_4_.refs_0_), channel_id=1, source_target_pairs={{0,2},{1,3},{2,0},{3,1},{4,6},{5,7},{6,4},{7,5},{8,10},{9,11},{10,... | collective-permute-start | bytes 196616 | tf_op jit(solution)/shard_map/ppermute | solution.py:629
  12.7 0.2 collective-permute-start.3
  13.0 1.4 %shard_map.120 = bf16[64,1024]{1,0:T(8,128)(2,1)S(1)} custom-call(s32[2]{0:T(128)S(1)} %pad_add_fusion.where_ref, bf16[16,2048]{1,0:T(8,128)(2,1)S(1)} %get-tuple-element.77.refs_0_, bf16[16,2048]{1,0:T(8,128)(2,1)S(1)} %collective-permute-done.refs_1_, bf16[16,2048]{1,0:T(8,128)(2,1)S(1)} %collective-permute-done.1.refs_2_, ...), custom_call_target="tpu_custom_call" | custom-call | flops 268435 | bytes 4194 | tf_op jit(solution)/shard_map/pallas_call | solution.py:279
  14.4 1.1 %collective-permute-done.4.refs_6_.refs_2_ = bf16[16,2048]{1,0:T(8,128)(2,1)S(1)} collective-permute-done((bf16[16,2048]{1,0:T(8,128)(2,1)S(1)}, bf16[16,2048]{1,0:T(8,128)(2,1)S(1)}, u32[]{:S(2)}, u32[]{:S(2)}) %collective-permute-start.4) | collective-permute-done | bytes 65568 | tf_op jit(solution)/shard_map/ppermute | solution.py:629
  15.5 2.1 %collective-permute-start.6 = (bf16[64,1024]{1,0:T(8,128)(2,1)S(1)}, bf16[64,1024]{1,0:T(8,128)(2,1)S(1)}, u32[]{:S(2)}, u32[]{:S(2)}) collective-permute-start(bf16[64,1024]{1,0:T(8,128)(2,1)S(1)} %shard_map.120), channel_id=1, source_target_pairs={{0,4},{4,0},{8,12},{12,8},{1,5},{5,1},{9,13},{13,9},{2,6},{6,2},{1... | collective-permute-start | bytes 393224 | tf_op jit(solution)/shard_map/ppermute | solution.py:630
  17.6 2.1 %shard_map.121 = (bf16[64,1024]{1,0:T(8,128)(2,1)S(1)}, bf16[64,1024]{1,0:T(8,128)(2,1)S(1)}) custom-call(s32[2]{0:T(128)S(1)} %pad_add_fusion.where_ref, bf16[16,2048]{1,0:T(8,128)(2,1)S(1)} %get-tuple-element.77.refs_0_, bf16[16,2048]{1,0:T(8,128)(2,1)S(1)} %collective-permute-done.refs_1_, bf16[16,2048]{1,0:T(8,128)(2,1)S(1)} %collective-permute-done.1.refs_2_, ...), custom_call_target="tpu_custom_call" | custom-call | flops 268435 | bytes 4194 | tf_op jit(solution)/shard_map/pallas_call | solution.py:279
  19.8 1.3 %collective-permute-start.8 = (bf16[64,1024]{1,0:T(8,128)(2,1)S(1)}, bf16[64,1024]{1,0:T(8,128)(2,1)S(1)}, u32[]{:S(2)}, u32[]{:S(2)}) collective-permute-start(bf16[64,1024]{1,0:T(8,128)(2,1)S(1)} %get-tuple-element.89), channel_id=1, source_target_pairs={{0,4},{4,0},{8,12},{12,8},{1,5},{5,1},{9,13},{13,9},{2,6},{6,2},{1... | collective-permute-start | bytes 393224 | tf_op jit(solution)/shard_map/ppermute | solution.py:630
  21.1 0.7 collective-permute-done.6.refs_1_
  21.8 2.8 %collective-permute-start.7 = (bf16[64,1024]{1,0:T(8,128)(2,1)S(1)}, bf16[64,1024]{1,0:T(8,128)(2,1)S(1)}, u32[]{:S(2)}, u32[]{:S(2)}) collective-permute-start(bf16[64,1024]{1,0:T(8,128)(2,1)S(1)} %shard_map.122.refs_0_), channel_id=1, source_target_pairs={{0,8},{4,12},{8,0},{12,4},{1,9},{5,13},{9,1},{13,5},{2,10},{6,14},... | collective-permute-start | bytes 393224 | tf_op jit(solution)/shard_map/ppermute | solution.py:642
  24.6 1.4 %shard_map.123.refs_0_ = bf16[64,1024]{1,0:T(8,128)(2,1)S(1)} custom-call(s32[2]{0:T(128)S(1)} %pad_add_fusion.where_ref, bf16[16,2048]{1,0:T(8,128)(2,1)S(1)} %shard_map.119.refs_4_.refs_0_, bf16[16,2048]{1,0:T(8,128)(2,1)S(1)} %collective-permute-done.3.refs_5_.refs_1_, bf16[16,2048]{1,0:T(8,128)(2,1)S(1)} %collective-permute-done.4.refs_6_.refs_2_, ...), custom_call_target="tpu_custom_call" | custom-call | flops 268435 | bytes 4194 | tf_op jit(solution)/shard_map/pallas_call | solution.py:279
  26.0 0.9 collective-permute-done.8.refs_1_
  27.0 1.8 %collective-permute-start.9 = (bf16[64,1024]{1,0:T(8,128)(2,1)S(1)}, bf16[64,1024]{1,0:T(8,128)(2,1)S(1)}, u32[]{:S(2)}, u32[]{:S(2)}) collective-permute-start(bf16[64,1024]{1,0:T(8,128)(2,1)S(1)} %shard_map.124.refs_0_), channel_id=1, source_target_pairs={{0,8},{4,12},{8,0},{12,4},{1,9},{5,13},{9,1},{13,5},{2,10},{6,14},... | collective-permute-start | bytes 393224 | tf_op jit(solution)/shard_map/ppermute | solution.py:642
  28.9 5.9 %shard_map.125 = (bf16[1024,3584]{1,0:T(8,128)(2,1)S(1)}, bf16[1024,3584]{1,0:T(8,128)(2,1)S(1)}) custom-call(s32[2]{0:T(128)S(1)} %pad_add_fusion.where_ref, bf16[2048,3584]{1,0:T(8,128)(2,1)} %src_ref.1, bf16[64,1024]{1,0:T(8,128)(2,1)S(1)} %shard_map.124.refs_0_), custom_call_target="tpu_custom_call" | custom-call | bytes 7340 | tf_op jit(solution)/shard_map/pallas_call | solution.py:245
  34.8 0.5 collective-permute-start.10
  35.3 1.4 %collective-permute-done.9.refs_1_ = bf16[64,1024]{1,0:T(8,128)(2,1)S(1)} collective-permute-done((bf16[64,1024]{1,0:T(8,128)(2,1)S(1)}, bf16[64,1024]{1,0:T(8,128)(2,1)S(1)}, u32[]{:S(2)}, u32[]{:S(2)}) %collective-permute-start.9) | collective-permute-done | bytes 131104 | tf_op jit(solution)/shard_map/ppermute | solution.py:642
  36.7 0.6 collective-permute-start.11
  37.3 0.7 shard_map.128
  38.1 2.6 %shard_map.129.f_ref = f32[128,7168]{1,0:T(8,128)S(1)} custom-call(s32[2]{0:T(128)S(1)} %pad_add_fusion.where_ref, bf16[128,1024]{1,0:T(8,128)(2,1)S(1)} %get-tuple-element.96.x_ref, bf16[1024,3584]{1,0:T(8,128)(2,1)S(1)} %get-tuple-element.97.g_ref, bf16[2048,3584]{1,0:T(8,128)(2,1)S(1)} %bitcast.5), custom_call_target="tpu_custom_call" | custom-call | flops 1879048 | bytes 14680 | tf_op jit(solution)/shard_map/pallas_call | solution.py:341
  40.7 0.1 collective-permute-done.10.refs_0_
  40.8 1.8 %collective-permute-done.11.refs_1_ = bf16[64,1024]{1,0:T(8,128)(2,1)S(1)} collective-permute-done((bf16[64,1024]{1,0:T(8,128)(2,1)S(1)}, bf16[64,1024]{1,0:T(8,128)(2,1)S(1)}, u32[]{:S(2)}, u32[]{:S(2)}) %collective-permute-start.11) | collective-permute-done | bytes 131104 | tf_op jit(solution)/shard_map/ppermute | solution.py:630
  42.6 0.8 shard_map.130
  43.4 1.8 %shard_map.132 = (bf16[64,1920]{1,0:T(8,128)(2,1)S(1)}, bf16[64,1920]{1,0:T(8,128)(2,1)S(1)}, f32[128,1792]{1,0:T(8,128)S(1)}) custom-call(s32[2]{0:T(128)S(1)} %pad_add_fusion.where_ref, bf16[128,1024]{1,0:T(8,128)(2,1)S(1)} %get-tuple-element.108.x_ref, f32[128,7168]{1,0:T(8,128)S(1)} %shard_map.129.f_ref, f32[128,128]{1,0:T(8,128)S(1)} %shard_map.131.sq_ref, ...), custom_call_target="tpu_custom_call" | custom-call | flops 939524 | bytes 7340 | tf_op jit(solution)/shard_map/pallas_call | solution.py:393
  45.2 0.1 collective-permute-start.12
  45.3 0.5 collective-permute-start.14
  45.8 1.0 %collective-permute-done.12.got_ref = bf16[64,1920]{1,0:T(8,128)(2,1)S(1)} collective-permute-done((bf16[64,1920]{1,0:T(8,128)(2,1)S(1)}, bf16[64,1920]{1,0:T(8,128)(2,1)S(1)}, u32[]{:S(2)}, u32[]{:S(2)}) %collective-permute-start.12) | collective-permute-done | bytes 245792 | tf_op jit(solution)/shard_map/ppermute | solution.py:628
  46.8 0.2 shard_map.133
  47.0 1.3 %collective-permute-start.13 = (bf16[64,1920]{1,0:T(8,128)(2,1)S(1)}, bf16[64,1920]{1,0:T(8,128)(2,1)S(1)}, u32[]{:S(2)}, u32[]{:S(2)}) collective-permute-start(bf16[64,1920]{1,0:T(8,128)(2,1)S(1)} %shard_map.133), channel_id=1, source_target_pairs={{0,2},{1,3},{2,0},{3,1},{4,6},{5,7},{6,4},{7,5},{8,10},{9,11},{10,... | collective-permute-start | bytes 737288 | tf_op jit(solution)/shard_map/ppermute | solution.py:629
  48.2 0.2 shard_map.134
  48.5 1.8 %shard_map.135 = (bf16[64,1920]{1,0:T(8,128)(2,1)S(1)}, bf16[64,1920]{1,0:T(8,128)(2,1)S(1)}, f32[128,1792]{1,0:T(8,128)S(1)}) custom-call(s32[2]{0:T(128)S(1)} %pad_add_fusion.where_ref, bf16[128,1024]{1,0:T(8,128)(2,1)S(1)} %get-tuple-element.108.x_ref, f32[128,7168]{1,0:T(8,128)S(1)} %shard_map.129.f_ref, f32[128,128]{1,0:T(8,128)S(1)} %shard_map.131.sq_ref, ...), custom_call_target="tpu_custom_call" | custom-call | flops 939524 | bytes 7340 | tf_op jit(solution)/shard_map/pallas_call | solution.py:393
  50.3 0.5 collective-permute-start.16
  50.8 0.8 collective-permute-start.18
  51.7 4.2 %collective-permute-done.13.far_ref = bf16[64,1920]{1,0:T(8,128)(2,1)S(1)} collective-permute-done((bf16[64,1920]{1,0:T(8,128)(2,1)S(1)}, bf16[64,1920]{1,0:T(8,128)(2,1)S(1)}, u32[]{:S(2)}, u32[]{:S(2)}) %collective-permute-start.13) | collective-permute-done | bytes 245792 | tf_op jit(solution)/shard_map/ppermute | solution.py:629
  55.8 0.2 shard_map.136.refs_0_
  56.1 0.1 collective-permute-start.19
  56.2 1.3 %collective-permute-start.17 = (bf16[64,896]{1,0:T(8,128)(2,1)S(1)}, bf16[64,896]{1,0:T(8,128)(2,1)S(1)}, u32[]{:S(2)}, u32[]{:S(2)}) collective-permute-start(bf16[64,896]{1,0:T(8,128)(2,1)S(1)} %shard_map.136.refs_0_), channel_id=1, source_target_pairs={{0,2},{1,3},{2,0},{3,1},{4,6},{5,7},{6,4},{7,5},{8,10},{9,11},{10,... | collective-permute-start | bytes 344072 | tf_op jit(solution)/shard_map/ppermute | solution.py:629
  57.5 2.1 %shard_map.137.refs_2_ = f32[64,2048]{1,0:T(8,128)S(1)} custom-call(s32[2]{0:T(128)S(1)} %pad_add_fusion.where_ref, bf16[64,896]{1,0:T(8,128)(2,1)S(1)} %shard_map.136.refs_0_, bf16[64,896]{1,0:T(8,128)(2,1)S(1)} %collective-permute-done.19.refs_1_, bf16[3584,2048]{1,0:T(8,128)(2,1)S(1)} %bitcast.3), custom_call_target="tpu_custom_call" | custom-call | flops 469762 | bytes 7340 | tf_op jit(solution)/shard_map/pallas_call | solution.py:512
  59.6 1.5 %collective-permute-done.18.far_ref = bf16[64,1920]{1,0:T(8,128)(2,1)S(1)} collective-permute-done((bf16[64,1920]{1,0:T(8,128)(2,1)S(1)}, bf16[64,1920]{1,0:T(8,128)(2,1)S(1)}, u32[]{:S(2)}, u32[]{:S(2)}) %collective-permute-start.18) | collective-permute-done | bytes 245792 | tf_op jit(solution)/shard_map/ppermute | solution.py:629
  61.1 0.2 shard_map.138.refs_0_
  61.3 0.1 collective-permute-start.21
  61.4 1.3 %collective-permute-done.17.refs_0_ = bf16[64,896]{1,0:T(8,128)(2,1)S(1)} collective-permute-done((bf16[64,896]{1,0:T(8,128)(2,1)S(1)}, bf16[64,896]{1,0:T(8,128)(2,1)S(1)}, u32[]{:S(2)}, u32[]{:S(2)}) %collective-permute-start.17) | collective-permute-done | bytes 114720 | tf_op jit(solution)/shard_map/ppermute | solution.py:629
  62.8 1.2 %collective-permute-start.22 = (bf16[64,896]{1,0:T(8,128)(2,1)S(1)}, bf16[64,896]{1,0:T(8,128)(2,1)S(1)}, u32[]{:S(2)}, u32[]{:S(2)}) collective-permute-start(bf16[64,896]{1,0:T(8,128)(2,1)S(1)} %shard_map.138.refs_0_), channel_id=1, source_target_pairs={{0,2},{1,3},{2,0},{3,1},{4,6},{5,7},{6,4},{7,5},{8,10},{9,11},{10,... | collective-permute-start | bytes 344072 | tf_op jit(solution)/shard_map/ppermute | solution.py:629
  64.0 1.9 %shard_map.139.refs_5_.refs_2_ = f32[64,2048]{1,0:T(8,128)S(1)} custom-call(s32[2]{0:T(128)S(1)} %pad_add_fusion.where_ref, bf16[64,896]{1,0:T(8,128)(2,1)S(1)} %shard_map.138.refs_0_, bf16[64,896]{1,0:T(8,128)(2,1)S(1)} %collective-permute-done.21.refs_1_, bf16[3584,2048]{1,0:T(8,128)(2,1)S(1)} %bitcast.3), custom_call_target="tpu_custom_call" | custom-call | flops 469762 | bytes 7340 | tf_op jit(solution)/shard_map/pallas_call | solution.py:512
  65.9 1.3 %shard_map.140 = bf16[64,1024]{1,0:T(8,128)(2,1)S(1)} custom-call(s32[2]{0:T(128)S(1)} %pad_add_fusion.where_ref, bf16[64,896]{1,0:T(8,128)(2,1)S(1)} %collective-permute-done.17.refs_0_, bf16[64,896]{1,0:T(8,128)(2,1)S(1)} %collective-permute-done.20.refs_1_, f32[64,2048]{1,0:T(8,128)S(1)} %shard_map.137.refs_2_, bf16[3584,2048]{1,0:T(8,128)(2,1)S(1)} %bitcast.3), custom_call_target="tpu_custom_call" | custom-call | flops 469762 | bytes 7340 | tf_op jit(solution)/shard_map/pallas_call | solution.py:512
  67.2 1.1 %collective-permute-done.22.refs_3_.refs_0_ = bf16[64,896]{1,0:T(8,128)(2,1)S(1)} collective-permute-done((bf16[64,896]{1,0:T(8,128)(2,1)S(1)}, bf16[64,896]{1,0:T(8,128)(2,1)S(1)}, u32[]{:S(2)}, u32[]{:S(2)}) %collective-permute-start.22) | collective-permute-done | bytes 114720 | tf_op jit(solution)/shard_map/ppermute | solution.py:629
  68.3 0.5 collective-permute-start.24
  68.8 0.9 collective-permute-done.23.refs_4_.refs_1_
  69.6 2.0 %shard_map.141 = (bf16[64,1024]{1,0:T(8,128)(2,1)S(1)}, bf16[64,1024]{1,0:T(8,128)(2,1)S(1)}) custom-call(s32[2]{0:T(128)S(1)} %pad_add_fusion.where_ref, bf16[64,896]{1,0:T(8,128)(2,1)S(1)} %collective-permute-done.17.refs_0_, bf16[64,896]{1,0:T(8,128)(2,1)S(1)} %collective-permute-done.20.refs_1_, f32[64,2048]{1,0:T(8,128)S(1)} %shard_map.137.refs_2_, ...), custom_call_target="tpu_custom_call" | custom-call | flops 469762 | bytes 7340 | tf_op jit(solution)/shard_map/pallas_call | solution.py:512
  71.6 0.8 collective-permute-start.27
  72.4 1.8 %collective-permute-done.24.refs_1_ = bf16[64,1024]{1,0:T(8,128)(2,1)S(1)} collective-permute-done((bf16[64,1024]{1,0:T(8,128)(2,1)S(1)}, bf16[64,1024]{1,0:T(8,128)(2,1)S(1)}, u32[]{:S(2)}, u32[]{:S(2)}) %collective-permute-start.24) | collective-permute-done | bytes 131104 | tf_op jit(solution)/shard_map/ppermute | solution.py:630
  74.3 1.9 %collective-permute-start.25 = (bf16[64,1024]{1,0:T(8,128)(2,1)S(1)}, bf16[64,1024]{1,0:T(8,128)(2,1)S(1)}, u32[]{:S(2)}, u32[]{:S(2)}) collective-permute-start(bf16[64,1024]{1,0:T(8,128)(2,1)S(1)} %shard_map.142.refs_0_), channel_id=1, source_target_pairs={{0,8},{4,12},{8,0},{12,4},{1,9},{5,13},{9,1},{13,5},{2,10},{6,14},... | collective-permute-start | bytes 393224 | tf_op jit(solution)/shard_map/ppermute | solution.py:642
  76.1 1.3 %shard_map.144.refs_0_ = bf16[64,1024]{1,0:T(8,128)(2,1)S(1)} custom-call(s32[2]{0:T(128)S(1)} %pad_add_fusion.where_ref, bf16[64,896]{1,0:T(8,128)(2,1)S(1)} %collective-permute-done.22.refs_3_.refs_0_, bf16[64,896]{1,0:T(8,128)(2,1)S(1)} %collective-permute-done.23.refs_4_.refs_1_, f32[64,2048]{1,0:T(8,128)S(1)} %shard_map.139.refs_5_.refs_2_, ...), custom_call_target="tpu_custom_call" | custom-call | flops 469762 | bytes 7340 | tf_op jit(solution)/shard_map/pallas_call | solution.py:512
  77.5 2.8 %collective-permute-start.28 = (bf16[64,1024]{1,0:T(8,128)(2,1)S(1)}, bf16[64,1024]{1,0:T(8,128)(2,1)S(1)}, u32[]{:S(2)}, u32[]{:S(2)}) collective-permute-start(bf16[64,1024]{1,0:T(8,128)(2,1)S(1)} %shard_map.145.refs_0_), channel_id=1, source_target_pairs={{0,8},{4,12},{8,0},{12,4},{1,9},{5,13},{9,1},{13,5},{2,10},{6,14},... | collective-permute-start | bytes 393224 | tf_op jit(solution)/shard_map/ppermute | solution.py:642
  80.3 6.7 %collective-permute-done.25.refs_1_ = bf16[64,1024]{1,0:T(8,128)(2,1)S(1)} collective-permute-done((bf16[64,1024]{1,0:T(8,128)(2,1)S(1)}, bf16[64,1024]{1,0:T(8,128)(2,1)S(1)}, u32[]{:S(2)}, u32[]{:S(2)}) %collective-permute-start.25) | collective-permute-done | bytes 131104 | tf_op jit(solution)/shard_map/ppermute | solution.py:642
  87.1 1.8 %collective-permute-done.28.refs_1_ = bf16[64,1024]{1,0:T(8,128)(2,1)S(1)} collective-permute-done((bf16[64,1024]{1,0:T(8,128)(2,1)S(1)}, bf16[64,1024]{1,0:T(8,128)(2,1)S(1)}, u32[]{:S(2)}, u32[]{:S(2)}) %collective-permute-start.28) | collective-permute-done | bytes 131104 | tf_op jit(solution)/shard_map/ppermute | solution.py:642
  88.9 0.3 collective-permute-start.29
  89.2 4.2 %collective-permute-done.26.refs_3_ = bf16[64,1024]{1,0:T(8,128)(2,1)S(1)} collective-permute-done((bf16[64,1024]{1,0:T(8,128)(2,1)S(1)}, bf16[64,1024]{1,0:T(8,128)(2,1)S(1)}, u32[]{:S(2)}, u32[]{:S(2)}) %collective-permute-start.26) | collective-permute-done | bytes 131104 | tf_op jit(solution)/shard_map/ppermute | solution.py:630
  93.4 1.4 %collective-permute-done.29.refs_5_ = bf16[64,1024]{1,0:T(8,128)(2,1)S(1)} collective-permute-done((bf16[64,1024]{1,0:T(8,128)(2,1)S(1)}, bf16[64,1024]{1,0:T(8,128)(2,1)S(1)}, u32[]{:S(2)}, u32[]{:S(2)}) %collective-permute-start.29) | collective-permute-done | bytes 131104 | tf_op jit(solution)/shard_map/ppermute | solution.py:630
  94.8 1.5 %shard_map.147 = bf16[2,64,2048]{2,1,0:T(8,128)(2,1)} custom-call(s32[2]{0:T(128)S(1)} %pad_add_fusion.where_ref, bf16[128,1024]{1,0:T(8,128)(2,1)S(1)} %get-tuple-element.95.refs_0_, bf16[128,1024]{1,0:T(8,128)(2,1)S(1)} %get-tuple-element.100.refs_1_, bf16[64,1024]{1,0:T(8,128)(2,1)S(1)} %shard_map.143.refs_2_, ...), custom_call_target="tpu_custom_call" | custom-call | flops 262 | bytes 1048 | tf_op jit(solution)/shard_map/pallas_call | solution.py:472
  (55 shorter events, 0.6 us)
Async XLA Ops:
  0.0 13.0 %slice-start.8 = ((s8[8388608]{0:T(1024)(128)(4,1)}), s8[4194304]{0:T(1024)(128)(4,1)S(1)}, s32[]{:S(2)}) async-start(s8[8388608]{0:T(1024)(128)(4,1)} %bitcast.6), calls=%async_computation.8 | async-start | bytes 8388608
  0.1 12.9 %slice-start.9 = ((s8[8388608]{0:T(1024)(128)(4,1)}), s8[4194304]{0:T(1024)(128)(4,1)S(1)}, s32[]{:S(2)}) async-start(s8[8388608]{0:T(1024)(128)(4,1)} %bitcast.6), calls=%async_computation.9 | async-start | bytes 8388608
  5.7 7.3 %copy-start.1 = (bf16[2048]{0:T(1024)(128)(2,1)S(1)}, bf16[2048]{0:T(1024)(128)(2,1)}, u32[]{:S(2)}) copy-start(bf16[2048]{0:T(1024)(128)(2,1)} %param.20) | copy-start | bytes 12292
  5.7 5.0 %collective-permute-start.1 = (bf16[16,2048]{1,0:T(8,128)(2,1)S(1)}, bf16[16,2048]{1,0:T(8,128)(2,1)S(1)}, u32[]{:S(2)}, u32[]{:S(2)}) collective-permute-start(bf16[16,2048]{1,0:T(8,128)(2,1)S(1)} %get-tuple-element.77.refs_0_), channel_id=1, source_target_pairs={{0,2},{1,3},{2,0},{3,1},{4,6},{5,7},{6,4},{7,5},{8,10},{9,11},{10,... | collective-permute-start | bytes 196616 | tf_op jit(solution)/shard_map/ppermute | solution.py:629
  8.5 4.5 %collective-permute-start = (bf16[16,2048]{1,0:T(8,128)(2,1)S(1)}, bf16[16,2048]{1,0:T(8,128)(2,1)S(1)}, u32[]{:S(2)}, u32[]{:S(2)}) collective-permute-start(bf16[16,2048]{1,0:T(8,128)(2,1)S(1)} %get-tuple-element.77.refs_0_), channel_id=1, source_target_pairs={{0,1},{1,0},{2,3},{3,2},{4,5},{5,4},{6,7},{7,6},{8,9},{9,8},{10,11... | collective-permute-start | bytes 196616 | tf_op jit(solution)/shard_map/ppermute | solution.py:628
  10.7 2.3 %collective-permute-start.2 = (bf16[16,2048]{1,0:T(8,128)(2,1)S(1)}, bf16[16,2048]{1,0:T(8,128)(2,1)S(1)}, u32[]{:S(2)}, u32[]{:S(2)}) collective-permute-start(bf16[16,2048]{1,0:T(8,128)(2,1)S(1)} %collective-permute-done.1.refs_2_), channel_id=1, source_target_pairs={{0,1},{1,0},{2,3},{3,2},{4,5},{5,4},{6,7},{7,6},{8,9},{9,8},{10,11... | collective-permute-start | bytes 196616 | tf_op jit(solution)/shard_map/ppermute | solution.py:628
  11.0 4.5 %collective-permute-start.4 = (bf16[16,2048]{1,0:T(8,128)(2,1)S(1)}, bf16[16,2048]{1,0:T(8,128)(2,1)S(1)}, u32[]{:S(2)}, u32[]{:S(2)}) collective-permute-start(bf16[16,2048]{1,0:T(8,128)(2,1)S(1)} %shard_map.119.refs_4_.refs_0_), channel_id=1, source_target_pairs={{0,2},{1,3},{2,0},{3,1},{4,6},{5,7},{6,4},{7,5},{8,10},{9,11},{10,... | collective-permute-start | bytes 196616 | tf_op jit(solution)/shard_map/ppermute | solution.py:629
  12.7 4.9 %collective-permute-start.3 = (bf16[16,2048]{1,0:T(8,128)(2,1)S(1)}, bf16[16,2048]{1,0:T(8,128)(2,1)S(1)}, u32[]{:S(2)}, u32[]{:S(2)}) collective-permute-start(bf16[16,2048]{1,0:T(8,128)(2,1)S(1)} %shard_map.119.refs_4_.refs_0_), channel_id=1, source_target_pairs={{0,1},{1,0},{2,3},{3,2},{4,5},{5,4},{6,7},{7,6},{8,9},{9,8},{10,11... | collective-permute-start | bytes 196616 | tf_op jit(solution)/shard_map/ppermute | solution.py:628
  15.5 2.1 %collective-permute-start.5 = (bf16[16,2048]{1,0:T(8,128)(2,1)S(1)}, bf16[16,2048]{1,0:T(8,128)(2,1)S(1)}, u32[]{:S(2)}, u32[]{:S(2)}) collective-permute-start(bf16[16,2048]{1,0:T(8,128)(2,1)S(1)} %collective-permute-done.4.refs_6_.refs_2_), channel_id=1, source_target_pairs={{0,1},{1,0},{2,3},{3,2},{4,5},{5,4},{6,7},{7,6},{8,9},{9,8},{10,11... | collective-permute-start | bytes 196616 | tf_op jit(solution)/shard_map/ppermute | solution.py:628
  15.5 6.2 %collective-permute-start.6 = (bf16[64,1024]{1,0:T(8,128)(2,1)S(1)}, bf16[64,1024]{1,0:T(8,128)(2,1)S(1)}, u32[]{:S(2)}, u32[]{:S(2)}) collective-permute-start(bf16[64,1024]{1,0:T(8,128)(2,1)S(1)} %shard_map.120), channel_id=1, source_target_pairs={{0,4},{4,0},{8,12},{12,8},{1,5},{5,1},{9,13},{13,9},{2,6},{6,2},{1... | collective-permute-start | bytes 393224 | tf_op jit(solution)/shard_map/ppermute | solution.py:630
  17.6 20.4 %slice-start.4 = ((s8[14680064]{0:T(1024)(128)(4,1)}), s8[4194304]{0:T(1024)(128)(4,1)S(1)}, s32[]{:S(2)}) async-start(s8[14680064]{0:T(1024)(128)(4,1)} %bitcast.4), calls=%async_computation.4 | async-start | bytes 8388608
  17.6 20.4 %slice-start.5 = ((s8[14680064]{0:T(1024)(128)(4,1)}), s8[4194304]{0:T(1024)(128)(4,1)S(1)}, s32[]{:S(2)}) async-start(s8[14680064]{0:T(1024)(128)(4,1)} %bitcast.4), calls=%async_computation.5 | async-start | bytes 8388608
  19.8 7.2 %collective-permute-start.8 = (bf16[64,1024]{1,0:T(8,128)(2,1)S(1)}, bf16[64,1024]{1,0:T(8,128)(2,1)S(1)}, u32[]{:S(2)}, u32[]{:S(2)}) collective-permute-start(bf16[64,1024]{1,0:T(8,128)(2,1)S(1)} %get-tuple-element.89), channel_id=1, source_target_pairs={{0,4},{4,0},{8,12},{12,8},{1,5},{5,1},{9,13},{13,9},{2,6},{6,2},{1... | collective-permute-start | bytes 393224 | tf_op jit(solution)/shard_map/ppermute | solution.py:630
  21.8 16.2 %slice-start.6 = ((s8[14680064]{0:T(1024)(128)(4,1)}), s8[4194304]{0:T(1024)(128)(4,1)S(1)}, s32[]{:S(2)}) async-start(s8[14680064]{0:T(1024)(128)(4,1)} %bitcast.4), calls=%async_computation.6 | async-start | bytes 8388608
  21.8 12.9 %collective-permute-start.7 = (bf16[64,1024]{1,0:T(8,128)(2,1)S(1)}, bf16[64,1024]{1,0:T(8,128)(2,1)S(1)}, u32[]{:S(2)}, u32[]{:S(2)}) collective-permute-start(bf16[64,1024]{1,0:T(8,128)(2,1)S(1)} %shard_map.122.refs_0_), channel_id=1, source_target_pairs={{0,8},{4,12},{8,0},{12,4},{1,9},{5,13},{9,1},{13,5},{2,10},{6,14},... | collective-permute-start | bytes 393224 | tf_op jit(solution)/shard_map/ppermute | solution.py:642
  26.0 11.2 %copy-start = (bf16[2,64,2048]{2,1,0:T(8,128)(2,1)S(1)}, bf16[2,64,2048]{2,1,0:T(8,128)(2,1)}, u32[]{:S(2)}) copy-start(bf16[2,64,2048]{2,1,0:T(8,128)(2,1)} %refs_2_.5) | copy-start | bytes 1572868
  27.0 11.0 %slice-start.7 = ((s8[14680064]{0:T(1024)(128)(4,1)}), s8[2097152]{0:T(1024)(128)(4,1)S(1)}, s32[]{:S(2)}) async-start(s8[14680064]{0:T(1024)(128)(4,1)} %bitcast.4), calls=%async_computation.7 | async-start | bytes 4194304
  27.0 9.6 %collective-permute-start.9 = (bf16[64,1024]{1,0:T(8,128)(2,1)S(1)}, bf16[64,1024]{1,0:T(8,128)(2,1)S(1)}, u32[]{:S(2)}, u32[]{:S(2)}) collective-permute-start(bf16[64,1024]{1,0:T(8,128)(2,1)S(1)} %shard_map.124.refs_0_), channel_id=1, source_target_pairs={{0,8},{4,12},{8,0},{12,4},{1,9},{5,13},{9,1},{13,5},{2,10},{6,14},... | collective-permute-start | bytes 393224 | tf_op jit(solution)/shard_map/ppermute | solution.py:642
  34.8 6.0 %collective-permute-start.10 = (bf16[64,1024]{1,0:T(8,128)(2,1)S(1)}, bf16[64,1024]{1,0:T(8,128)(2,1)S(1)}, u32[]{:S(2)}, u32[]{:S(2)}) collective-permute-start(bf16[64,1024]{1,0:T(8,128)(2,1)S(1)} %shard_map.126.refs_0_), channel_id=1, source_target_pairs={{0,4},{4,0},{8,12},{12,8},{1,5},{5,1},{9,13},{13,9},{2,6},{6,2},{1... | collective-permute-start | bytes 393224 | tf_op jit(solution)/shard_map/ppermute | solution.py:630
  36.7 5.9 %collective-permute-start.11 = (bf16[64,1024]{1,0:T(8,128)(2,1)S(1)}, bf16[64,1024]{1,0:T(8,128)(2,1)S(1)}, u32[]{:S(2)}, u32[]{:S(2)}) collective-permute-start(bf16[64,1024]{1,0:T(8,128)(2,1)S(1)} %shard_map.127.refs_1_), channel_id=1, source_target_pairs={{0,4},{4,0},{8,12},{12,8},{1,5},{5,1},{9,13},{13,9},{2,6},{6,2},{1... | collective-permute-start | bytes 393224 | tf_op jit(solution)/shard_map/ppermute | solution.py:630
  45.2 1.6 %collective-permute-start.12 = (bf16[64,1920]{1,0:T(8,128)(2,1)S(1)}, bf16[64,1920]{1,0:T(8,128)(2,1)S(1)}, u32[]{:S(2)}, u32[]{:S(2)}) collective-permute-start(bf16[64,1920]{1,0:T(8,128)(2,1)S(1)} %get-tuple-element.106), channel_id=1, source_target_pairs={{0,1},{1,0},{2,3},{3,2},{4,5},{5,4},{6,7},{7,6},{8,9},{9,8},{10,11... | collective-permute-start | bytes 737288 | tf_op jit(solution)/shard_map/ppermute | solution.py:628
  45.3 3.0 %collective-permute-start.14 = (bf16[64,1920]{1,0:T(8,128)(2,1)S(1)}, bf16[64,1920]{1,0:T(8,128)(2,1)S(1)}, u32[]{:S(2)}, u32[]{:S(2)}) collective-permute-start(bf16[64,1920]{1,0:T(8,128)(2,1)S(1)} %get-tuple-element.107), channel_id=1, source_target_pairs={{0,1},{1,0},{2,3},{3,2},{4,5},{5,4},{6,7},{7,6},{8,9},{9,8},{10,11... | collective-permute-start | bytes 737288 | tf_op jit(solution)/shard_map/ppermute | solution.py:628
  47.0 8.9 %collective-permute-start.13 = (bf16[64,1920]{1,0:T(8,128)(2,1)S(1)}, bf16[64,1920]{1,0:T(8,128)(2,1)S(1)}, u32[]{:S(2)}, u32[]{:S(2)}) collective-permute-start(bf16[64,1920]{1,0:T(8,128)(2,1)S(1)} %shard_map.133), channel_id=1, source_target_pairs={{0,2},{1,3},{2,0},{3,1},{4,6},{5,7},{6,4},{7,5},{8,10},{9,11},{10,... | collective-permute-start | bytes 737288 | tf_op jit(solution)/shard_map/ppermute | solution.py:629
  48.2 9.2 %slice-start = ((s8[14680064]{0:T(1024)(128)(4,1)}), s8[4194304]{0:T(1024)(128)(4,1)S(1)}, s32[]{:S(2)}) async-start(s8[14680064]{0:T(1024)(128)(4,1)} %bitcast.2), calls=%async_computation | async-start | bytes 8388608
  48.4 9.1 %slice-start.1 = ((s8[14680064]{0:T(1024)(128)(4,1)}), s8[4194304]{0:T(1024)(128)(4,1)S(1)}, s32[]{:S(2)}) async-start(s8[14680064]{0:T(1024)(128)(4,1)} %bitcast.2), calls=%async_computation.1 | async-start | bytes 8388608
  48.4 9.1 %slice-start.2 = ((s8[14680064]{0:T(1024)(128)(4,1)}), s8[4194304]{0:T(1024)(128)(4,1)S(1)}, s32[]{:S(2)}) async-start(s8[14680064]{0:T(1024)(128)(4,1)} %bitcast.2), calls=%async_computation.2 | async-start | bytes 8388608
  48.4 9.0 %slice-start.3 = ((s8[14680064]{0:T(1024)(128)(4,1)}), s8[2097152]{0:T(1024)(128)(4,1)S(1)}, s32[]{:S(2)}) async-start(s8[14680064]{0:T(1024)(128)(4,1)} %bitcast.2), calls=%async_computation.3 | async-start | bytes 4194304
  50.2 5.6 %collective-permute-start.15 = (bf16[64,1920]{1,0:T(8,128)(2,1)S(1)}, bf16[64,1920]{1,0:T(8,128)(2,1)S(1)}, u32[]{:S(2)}, u32[]{:S(2)}) collective-permute-start(bf16[64,1920]{1,0:T(8,128)(2,1)S(1)} %get-tuple-element.110), channel_id=1, source_target_pairs={{0,1},{1,0},{2,3},{3,2},{4,5},{5,4},{6,7},{7,6},{8,9},{9,8},{10,11... | collective-permute-start | bytes 737288 | tf_op jit(solution)/shard_map/ppermute | solution.py:628
  50.3 5.5 %collective-permute-start.16 = (bf16[64,1920]{1,0:T(8,128)(2,1)S(1)}, bf16[64,1920]{1,0:T(8,128)(2,1)S(1)}, u32[]{:S(2)}, u32[]{:S(2)}) collective-permute-start(bf16[64,1920]{1,0:T(8,128)(2,1)S(1)} %get-tuple-element.111), channel_id=1, source_target_pairs={{0,1},{1,0},{2,3},{3,2},{4,5},{5,4},{6,7},{7,6},{8,9},{9,8},{10,11... | collective-permute-start | bytes 737288 | tf_op jit(solution)/shard_map/ppermute | solution.py:628
  50.8 10.3 %collective-permute-start.18 = (bf16[64,1920]{1,0:T(8,128)(2,1)S(1)}, bf16[64,1920]{1,0:T(8,128)(2,1)S(1)}, u32[]{:S(2)}, u32[]{:S(2)}) collective-permute-start(bf16[64,1920]{1,0:T(8,128)(2,1)S(1)} %shard_map.134), channel_id=1, source_target_pairs={{0,2},{1,3},{2,0},{3,1},{4,6},{5,7},{6,4},{7,5},{8,10},{9,11},{10,... | collective-permute-start | bytes 737288 | tf_op jit(solution)/shard_map/ppermute | solution.py:629
  56.1 1.4 %collective-permute-start.19 = (bf16[64,896]{1,0:T(8,128)(2,1)S(1)}, bf16[64,896]{1,0:T(8,128)(2,1)S(1)}, u32[]{:S(2)}, u32[]{:S(2)}) collective-permute-start(bf16[64,896]{1,0:T(8,128)(2,1)S(1)} %shard_map.136.refs_0_), channel_id=1, source_target_pairs={{0,1},{1,0},{2,3},{3,2},{4,5},{5,4},{6,7},{7,6},{8,9},{9,8},{10,11... | collective-permute-start | bytes 344072 | tf_op jit(solution)/shard_map/ppermute | solution.py:628
  56.2 6.6 %collective-permute-start.17 = (bf16[64,896]{1,0:T(8,128)(2,1)S(1)}, bf16[64,896]{1,0:T(8,128)(2,1)S(1)}, u32[]{:S(2)}, u32[]{:S(2)}) collective-permute-start(bf16[64,896]{1,0:T(8,128)(2,1)S(1)} %shard_map.136.refs_0_), channel_id=1, source_target_pairs={{0,2},{1,3},{2,0},{3,1},{4,6},{5,7},{6,4},{7,5},{8,10},{9,11},{10,... | collective-permute-start | bytes 344072 | tf_op jit(solution)/shard_map/ppermute | solution.py:629
  61.3 2.6 %collective-permute-start.21 = (bf16[64,896]{1,0:T(8,128)(2,1)S(1)}, bf16[64,896]{1,0:T(8,128)(2,1)S(1)}, u32[]{:S(2)}, u32[]{:S(2)}) collective-permute-start(bf16[64,896]{1,0:T(8,128)(2,1)S(1)} %shard_map.138.refs_0_), channel_id=1, source_target_pairs={{0,1},{1,0},{2,3},{3,2},{4,5},{5,4},{6,7},{7,6},{8,9},{9,8},{10,11... | collective-permute-start | bytes 344072 | tf_op jit(solution)/shard_map/ppermute | solution.py:628
  62.7 3.2 %collective-permute-start.20 = (bf16[64,896]{1,0:T(8,128)(2,1)S(1)}, bf16[64,896]{1,0:T(8,128)(2,1)S(1)}, u32[]{:S(2)}, u32[]{:S(2)}) collective-permute-start(bf16[64,896]{1,0:T(8,128)(2,1)S(1)} %collective-permute-done.17.refs_0_), channel_id=1, source_target_pairs={{0,1},{1,0},{2,3},{3,2},{4,5},{5,4},{6,7},{7,6},{8,9},{9,8},{10,11... | collective-permute-start | bytes 344072 | tf_op jit(solution)/shard_map/ppermute | solution.py:628
  62.8 5.6 %collective-permute-start.22 = (bf16[64,896]{1,0:T(8,128)(2,1)S(1)}, bf16[64,896]{1,0:T(8,128)(2,1)S(1)}, u32[]{:S(2)}, u32[]{:S(2)}) collective-permute-start(bf16[64,896]{1,0:T(8,128)(2,1)S(1)} %shard_map.138.refs_0_), channel_id=1, source_target_pairs={{0,2},{1,3},{2,0},{3,1},{4,6},{5,7},{6,4},{7,5},{8,10},{9,11},{10,... | collective-permute-start | bytes 344072 | tf_op jit(solution)/shard_map/ppermute | solution.py:629
  68.3 1.3 %collective-permute-start.23 = (bf16[64,896]{1,0:T(8,128)(2,1)S(1)}, bf16[64,896]{1,0:T(8,128)(2,1)S(1)}, u32[]{:S(2)}, u32[]{:S(2)}) collective-permute-start(bf16[64,896]{1,0:T(8,128)(2,1)S(1)} %collective-permute-done.22.refs_3_.refs_0_), channel_id=1, source_target_pairs={{0,1},{1,0},{2,3},{3,2},{4,5},{5,4},{6,7},{7,6},{8,9},{9,8},{10,11... | collective-permute-start | bytes 344072 | tf_op jit(solution)/shard_map/ppermute | solution.py:628
  68.3 5.9 %collective-permute-start.24 = (bf16[64,1024]{1,0:T(8,128)(2,1)S(1)}, bf16[64,1024]{1,0:T(8,128)(2,1)S(1)}, u32[]{:S(2)}, u32[]{:S(2)}) collective-permute-start(bf16[64,1024]{1,0:T(8,128)(2,1)S(1)} %shard_map.140), channel_id=1, source_target_pairs={{0,4},{4,0},{8,12},{12,8},{1,5},{5,1},{9,13},{13,9},{2,6},{6,2},{1... | collective-permute-start | bytes 393224 | tf_op jit(solution)/shard_map/ppermute | solution.py:630
  71.6 5.8 %collective-permute-start.27 = (bf16[64,1024]{1,0:T(8,128)(2,1)S(1)}, bf16[64,1024]{1,0:T(8,128)(2,1)S(1)}, u32[]{:S(2)}, u32[]{:S(2)}) collective-permute-start(bf16[64,1024]{1,0:T(8,128)(2,1)S(1)} %get-tuple-element.122), channel_id=1, source_target_pairs={{0,4},{4,0},{8,12},{12,8},{1,5},{5,1},{9,13},{13,9},{2,6},{6,2},{1... | collective-permute-start | bytes 393224 | tf_op jit(solution)/shard_map/ppermute | solution.py:630
  74.3 12.7 %collective-permute-start.25 = (bf16[64,1024]{1,0:T(8,128)(2,1)S(1)}, bf16[64,1024]{1,0:T(8,128)(2,1)S(1)}, u32[]{:S(2)}, u32[]{:S(2)}) collective-permute-start(bf16[64,1024]{1,0:T(8,128)(2,1)S(1)} %shard_map.142.refs_0_), channel_id=1, source_target_pairs={{0,8},{4,12},{8,0},{12,4},{1,9},{5,13},{9,1},{13,5},{2,10},{6,14},... | collective-permute-start | bytes 393224 | tf_op jit(solution)/shard_map/ppermute | solution.py:642
  77.5 11.4 %collective-permute-start.28 = (bf16[64,1024]{1,0:T(8,128)(2,1)S(1)}, bf16[64,1024]{1,0:T(8,128)(2,1)S(1)}, u32[]{:S(2)}, u32[]{:S(2)}) collective-permute-start(bf16[64,1024]{1,0:T(8,128)(2,1)S(1)} %shard_map.145.refs_0_), channel_id=1, source_target_pairs={{0,8},{4,12},{8,0},{12,4},{1,9},{5,13},{9,1},{13,5},{2,10},{6,14},... | collective-permute-start | bytes 393224 | tf_op jit(solution)/shard_map/ppermute | solution.py:642
  87.0 6.4 %collective-permute-start.26 = (bf16[64,1024]{1,0:T(8,128)(2,1)S(1)}, bf16[64,1024]{1,0:T(8,128)(2,1)S(1)}, u32[]{:S(2)}, u32[]{:S(2)}) collective-permute-start(bf16[64,1024]{1,0:T(8,128)(2,1)S(1)} %shard_map.143.refs_2_), channel_id=1, source_target_pairs={{0,4},{4,0},{8,12},{12,8},{1,5},{5,1},{9,13},{13,9},{2,6},{6,2},{1... | collective-permute-start | bytes 393224 | tf_op jit(solution)/shard_map/ppermute | solution.py:630
  88.9 5.9 %collective-permute-start.29 = (bf16[64,1024]{1,0:T(8,128)(2,1)S(1)}, bf16[64,1024]{1,0:T(8,128)(2,1)S(1)}, u32[]{:S(2)}, u32[]{:S(2)}) collective-permute-start(bf16[64,1024]{1,0:T(8,128)(2,1)S(1)} %shard_map.146.refs_4_), channel_id=1, source_target_pairs={{0,4},{4,0},{8,12},{12,8},{1,5},{5,1},{9,13},{13,9},{2,6},{6,2},{1... | collective-permute-start | bytes 393224 | tf_op jit(solution)/shard_map/ppermute | solution.py:630
